TPU v7x, 32 devices: a whole 2x2x4 slice. The times are simulated.
32 devices in a mesh: req: 4 (over z), mlp: 8 (over y, x, core).
Axes of the slice: x: 2, y: 2, z: 4, core: 2. Of those that a mesh axis runs over, the one named last changes fastest.
Arguments:
- inputs: bfloat16 [2, 384, 4096], P(None, 'mlp', 'req'), may hold values from -6 to 6
- norm_gains: float32 [3, 4096], P(None, 'req'), may hold values from 0.25 to 1.75
- attn_weight: bfloat16 [4096, 12288], P('req', 'mlp'), may hold values from -0.09375 to 0.09375
- up_weight: bfloat16 [4096, 16384], P('req', 'mlp'), may hold values from -0.09375 to 0.09375
- dense_weight: bfloat16 [4096, 4096], P('mlp', 'req'), may hold values from -0.09375 to 0.09375
- down_weight: bfloat16 [16384, 4096], P('mlp', 'req'), may hold values from -0.046875 to 0.046875
- next_weight: bfloat16 [4096, 12288], P('req', 'mlp'), may hold values from -0.09375 to 0.09375
- cache_keys: bfloat16 [256, 128, 4096], P('req', None, 'mlp'), may hold values from -360 to 360
- cache_values: bfloat16 [256, 128, 4096], P('req', None, 'mlp'), may hold values from -6 to 6
- lengths: int32 [48], replicated, may hold values from 1 to 4096, as said below
- slot_table: int32 [2, 256], P(None, 'req'), may hold values from -1 to 47, as said below
- parents: int32 [1, 384], P(None, 'req'), may hold values from 0 to 7
Outputs:
- layer_out: bfloat16 [2, 384, 4096], P(None, 'mlp', 'req')
- next_qkv: bfloat16 [2, 384, 12288], P(None, 'req', 'mlp')
Inputs may be any that keep to these rules, and one draw needn't show every extreme that they name: `lengths`: each request has between 1 and 32 pages of 128 tokens; the longest request has exactly 32 full pages. `slot_table`: every page of every request is held by exactly one slot; an empty slot has request -1 and page 0. All requests together hold 220 pages, and in every draw the slots of some index of req are all in use.
All inputs are finite; a program needn't handle non-finite values.
Results may differ from a plain program's by a relative error of at most 0.04.
Values may be sent and summed in bfloat16 or wider, within the bound.
No kernel may reach another device: no remote copies, remote signals or barrier semaphores. Data moves between devices by JAX's collectives and lax.ppermute only.
A program may use at most 128 MiB of HBM per device.

v0:
```python
import math

import jax
import jax.numpy as jnp
from jax import lax
from jax.sharding import PartitionSpec as P

HD = 128
ROT = 32
PAGE = 128
BEAM = 8
STEPS = 2


NEG_FILL = -1e30
EPSILON = 1e-05


def combined_all(value, axis, combine):
    everything = jax.tree.map(
        lambda part, kind: lax.all_gather(part.astype(kind), axis),
        value,
        (jnp.bfloat16, jnp.bfloat16, jnp.bfloat16),
    )

    def take(k):
        return jax.tree.map(lambda part, own: part[k].astype(own.dtype), everything, value)

    return lax.fori_loop(
        1, lax.axis_size(axis), lambda k, so_far: combine(so_far, take(k)), take(0)
    )


def rotate(vectors, positions):
    half = ROT // 2
    freq = jnp.exp(jnp.arange(half, dtype=jnp.float32) * (-2.0 * math.log(10000.0) / ROT))
    angles = positions.astype(jnp.float32)[:, None] * freq[None, :]
    cosine = jnp.concatenate([jnp.cos(angles), jnp.cos(angles)], axis=1)[:, None, :]
    sine = jnp.concatenate([jnp.sin(angles), jnp.sin(angles)], axis=1)[:, None, :]
    turned = vectors[..., :ROT]
    swapped = jnp.concatenate([-turned[..., half:], turned[..., :half]], axis=-1)
    return jnp.concatenate([turned * cosine + swapped * sine, vectors[..., ROT:]], axis=-1)


def row_normalize(block):
    values = block.astype(jnp.float32)
    whole = lax.all_gather(block, "req", axis=1, tiled=True).astype(jnp.float32)
    row_mean = jnp.mean(whole, axis=1, keepdims=True)
    centred_whole = whole - row_mean
    row_var = jnp.mean(centred_whole * centred_whole, axis=1, keepdims=True)
    return (values - row_mean) * lax.rsqrt(row_var + EPSILON)


def merge_partials(first, second):
    top = jnp.maximum(first[0], second[0])
    left = jnp.exp(first[0] - top)
    right = jnp.exp(second[0] - top)
    return (
        top,
        first[1] * left + second[1] * right,
        first[2] * left[..., None] + second[2] * right[..., None],
    )


def shards(
    inputs,
    norm_gains,
    attn_weight,
    up_weight,
    dense_weight,
    down_weight,
    next_weight,
    cache_keys,
    cache_values,
    lengths,
    slot_table,
    parents,
):
    scale = 1.0 / math.sqrt(HD)
    highest = lax.Precision.HIGHEST
    own_count = parents.shape[1]
    request_count = lengths.shape[0]
    beam_total = request_count * BEAM
    head_count = dense_weight.shape[0] // HD
    triple_width = attn_weight.shape[1]
    slot_count = slot_table.shape[1]
    offset = lax.axis_index("req") * own_count
    beam_group = jnp.arange(beam_total, dtype=jnp.int32) // BEAM
    all_positions = lengths[beam_group]
    own_positions = lax.dynamic_slice_in_dim(all_positions, offset, own_count, 0)
    own_group = jnp.arange(own_count, dtype=jnp.int32) // BEAM
    slot_owner = slot_table[0]
    slot_pageno = slot_table[1]
    valid_owner = jnp.maximum(slot_owner, 0)
    token_pos = slot_pageno[:, None] * PAGE + jnp.arange(PAGE, dtype=jnp.int32)[None, :]
    live = (slot_owner[:, None] >= 0) & (token_pos < lengths[valid_owner][:, None])
    live_wide = live[:, None, None, :]
    owner_mask = slot_owner[:, None] == jnp.arange(request_count, dtype=jnp.int32)[None, :]
    owner_float = owner_mask.astype(jnp.float32)
    gather_rows = valid_owner[:, None] * BEAM + jnp.arange(BEAM, dtype=jnp.int32)[None, :]
    page_keys = cache_keys.reshape(slot_count, PAGE, head_count, HD)
    page_values = cache_values.reshape(slot_count, PAGE, head_count, HD)
    tail_keys = []
    tail_values = []
    layer_list = []
    next_list = []
    for step_index in range(STEPS):
        if step_index > 0:
            source = own_group * BEAM + parents[step_index - 1]
            tail_keys = [entry[source] for entry in tail_keys]
            tail_values = [entry[source] for entry in tail_values]
        block = inputs[step_index]
        normed = row_normalize(block)
        attn_in = (normed * norm_gains[0]).astype(jnp.bfloat16)
        mlp_in = (normed * norm_gains[1]).astype(jnp.bfloat16)
        joined = jnp.concatenate([attn_in, mlp_in], axis=1)
        split_at = attn_in.shape[1]
        piece = lax.all_gather(joined, "mlp", axis=0, tiled=True)
        first = jnp.dot(piece[:, :split_at], attn_weight, preferred_element_type=jnp.float32)
        second = jnp.dot(piece[:, split_at:], up_weight, preferred_element_type=jnp.float32)
        partial_sums = jnp.concatenate([first, second], axis=1)
        step_positions = own_positions + step_index
        shared = lax.psum_scatter(
            partial_sums.astype(jnp.bfloat16), "req", scatter_dimension=0, tiled=True
        ).astype(jnp.float32)
        mixed_own = shared[:, :triple_width].reshape(own_count, head_count, 3, HD)
        queries_own = rotate(mixed_own[:, :, 0], step_positions).astype(jnp.bfloat16)
        activated_own = jax.nn.gelu(shared[:, triple_width:], approximate=False).astype(
            jnp.bfloat16
        )
        queries_all = lax.all_gather(queries_own, "req", axis=0, tiled=True)
        keys_new = rotate(mixed_own[:, :, 1], step_positions).astype(jnp.bfloat16)
        values_new = mixed_own[:, :, 2].astype(jnp.bfloat16)
        chosen = queries_all[gather_rows]
        scores = (
            jnp.einsum("sbhd,sthd->sbht", chosen, page_keys, preferred_element_type=jnp.float32)
            * scale
        )
        masked = jnp.where(live_wide, scores, NEG_FILL)
        slot_top = jnp.max(masked, axis=3)
        weights = jnp.where(live_wide, jnp.exp(masked - slot_top[..., None]), 0.0)
        slot_total = jnp.sum(weights, axis=3)
        slot_out = jnp.einsum(
            "sbht,sthd->sbhd",
            weights.astype(jnp.bfloat16),
            page_values,
            preferred_element_type=jnp.float32,
        )
        request_top = jnp.max(
            jnp.where(owner_mask[:, :, None, None], slot_top[:, None], NEG_FILL), axis=0
        )
        factor = jnp.exp(slot_top - request_top[valid_owner])
        page_total = jnp.einsum(
            "sr,sbh->rbh", owner_float, slot_total * factor, precision=highest
        ).reshape(beam_total, head_count)
        page_out = jnp.einsum(
            "sr,sbhd->rbhd", owner_float, slot_out * factor[..., None], precision=highest
        ).reshape(beam_total, head_count, HD)
        page_top = request_top.reshape(beam_total, head_count)
        merged = combined_all((page_top, page_total, page_out), "req", merge_partials)
        own_top = lax.dynamic_slice_in_dim(merged[0], offset, own_count, 0)
        own_total = lax.dynamic_slice_in_dim(merged[1], offset, own_count, 0)
        own_out = lax.dynamic_slice_in_dim(merged[2], offset, own_count, 0)
        history_keys = jnp.stack(tail_keys + [keys_new], axis=0)
        history_values = jnp.stack(tail_values + [values_new], axis=0)
        own_scores = (
            jnp.einsum(
                "bhd,nbhd->bhn", queries_own, history_keys, preferred_element_type=jnp.float32
            )
            * scale
        )
        top = jnp.maximum(own_top, jnp.max(own_scores, axis=2))
        page_factor = jnp.exp(own_top - top)
        own_weights = jnp.exp(own_scores - top[..., None])
        total = own_total * page_factor + jnp.sum(own_weights, axis=2)
        summed = own_out * page_factor[..., None] + jnp.einsum(
            "bhn,nbhd->bhd",
            own_weights.astype(jnp.bfloat16),
            history_values,
            preferred_element_type=jnp.float32,
        )
        attended = (
            (summed / total[..., None]).astype(jnp.bfloat16).reshape(own_count, head_count * HD)
        )
        attended_all, activated_all = (
            lax.all_gather(attended, "req", axis=0, tiled=True),
            lax.all_gather(activated_own, "req", axis=0, tiled=True),
        )
        update = lax.psum_scatter(
            (
                jnp.dot(attended_all, dense_weight, preferred_element_type=jnp.float32)
                + jnp.dot(activated_all, down_weight, preferred_element_type=jnp.float32)
            ).astype(jnp.bfloat16),
            "mlp",
            scatter_dimension=0,
            tiled=True,
        ).astype(jnp.float32)
        layer = (block.astype(jnp.float32) + update).astype(jnp.bfloat16)
        next_in = (row_normalize(layer) * norm_gains[2]).astype(jnp.bfloat16)
        next_partial = jnp.dot(
            lax.all_gather(next_in, "mlp", axis=0, tiled=True),
            next_weight,
            preferred_element_type=jnp.float32,
        )
        next_out = lax.psum_scatter(
            next_partial.astype(jnp.bfloat16), "req", scatter_dimension=0, tiled=True
        )
        tail_keys = tail_keys + [keys_new]
        tail_values = tail_values + [values_new]
        layer_list.append(layer)
        next_list.append(next_out)
    return (jnp.stack(layer_list), jnp.stack(next_list))


def solution(mesh):
    in_specs = (
        P(None, "mlp", "req"),
        P(None, "req"),
        P("req", "mlp"),
        P("req", "mlp"),
        P("mlp", "req"),
        P("mlp", "req"),
        P("req", "mlp"),
        P("req", None, "mlp"),
        P("req", None, "mlp"),
        P(),
        P(None, "req"),
        P(None, "req"),
    )
    out_specs = (P(None, "mlp", "req"), P(None, "req", "mlp"))
    return jax.shard_map(shards, mesh=mesh, in_specs=in_specs, out_specs=out_specs, check_vma=False)
```

profile of v0, /device:TPU:0, one launch (start us, length us, event | category | flops | bytes accessed | tf_op | source)
XLA Modules:
  0.0 612.8 jit_solution(2128595723316784212)
XLA Ops:
  9.7 16.2 %all-gather = bf16[1,48,4096]{2,1,0:T(8,128)(2,1)S(1)} all-gather(bf16[1,48,1024]{2,1,0:T(8,128)(2,1)S(1)} %get-tuple-element.546), channel_id=2, replica_groups=mesh['req'=4,'mlp'=8] {'req'}, dimensions={2}, use_global_device_ids=true | all-gather | bytes 491520 | tf_op jit(solution)/shard_map/all_gather | solution.py:47
  26.4 15.4 %all-gather.1 = bf16[1,48,4096]{2,1,0:T(8,128)(2,1)S(1)} all-gather(bf16[1,48,1024]{2,1,0:T(8,128)(2,1)S(1)} %get-tuple-element.547), channel_id=3, replica_groups=mesh['req'=4,'mlp'=8] {'req'}, dimensions={2}, use_global_device_ids=true | all-gather | bytes 491520 | tf_op jit(solution)/shard_map/all_gather | solution.py:47
  44.1 25.7 %all-gather.15.cloned.1.call-done = bf16[384,2048]{1,0:T(8,128)(2,1)} async-done(((bf16[48,2048]{1,0:T(8,128)(2,1)}), bf16[384,2048]{1,0:T(8,128)(2,1)}) %all-gather.15.cloned.1.call-update) | async-done | bytes 1572880 | tf_op jit(solution)/shard_map/all_gather | solution.py:118
  76.4 21.6 %all-gather.9.cloned.1.call-done = bf16[384,2048]{1,0:T(8,128)(2,1)} async-done(((bf16[48,2048]{1,0:T(8,128)(2,1)}), bf16[384,2048]{1,0:T(8,128)(2,1)}) %all-gather.9.cloned.1.call-update) | async-done | bytes 1572880 | tf_op jit(solution)/shard_map/all_gather | solution.py:118
  113.2 25.7 %select_select_fusion = s32[384]{0:T(512)S(1)} fusion(pred[384]{0:T(512)(128)(4,1)S(1)} %get-tuple-element.625, pred[384]{0:T(512)(128)(4,1)S(1)} %get-tuple-element.626, pred[384]{0:T(512)(128)(4,1)S(1)} %get-tuple-element.627, pred[384]{0:T(512)(128)(4,1)S(1)} %get-tuple-element.628, pred[384]{0:T(512)(128)(4,1)S(1)} %get-tuple-element.629, ...), kind=kLoop, calls=%fused_computation.312 | loop fusion | flops 15744 | bytes 18980 | tf_op jit(solution)/shard_map/gather | solution.py:89
  140.5 14.0 %reduce-scatter.11.cloned.1.call-done = bf16[96,3584]{1,0:T(8,128)(2,1)} async-done(((bf16[384,3584]{1,0:T(8,128)(2,1)}), bf16[96,3584]{1,0:T(8,128)(2,1)}) %reduce-scatter.11.cloned.1.call-update) | async-done | bytes 688144 | tf_op jit(solution)/shard_map/reduce_scatter | solution.py:123
  158.2 17.8 %all_gather.76 = bf16[384,4,128]{2,1,0:T(4,128)(2,1)S(1)} all-gather(bf16[96,4,128]{2,1,0:T(4,128)(2,1)S(1)} %copy.395), channel_id=1, replica_groups=mesh['req'=4,'mlp'=8] {'req'}, dimensions={0}, use_global_device_ids=true | all-gather | bytes 491520 | tf_op jit(solution)/shard_map/all_gather | solution.py:131
  178.1 6.9 %fusion.168 = (f32[64,8,4]{1,2,0:T(4,128)S(1)}, f32[64,8,4,128]{3,1,2,0:T(8,128)S(1)}) fusion(bf16[64,8,4,128]{3,2,1,0:T(4,128)(2,1)S(1)} %bitcast.314, pred[64,128]{1,0:T(8,128)(4,1)S(1)} %fusion.130, bf16[64,128,512]{2,1,0:T(8,128)(2,1)} %param.23), kind=kOutput, calls=%fused_computation.355 | convolution fusion | flops 67893248 | bytes 9977856 | tf_op jit(solution)/shard_map/sbhd,sthd->sbht/dot_general | solution.py:136
  185.1 29.5 %reduce-scatter.7.cloned.1.call-done = bf16[96,3584]{1,0:T(8,128)(2,1)} async-done(((bf16[384,3584]{1,0:T(8,128)(2,1)}), bf16[96,3584]{1,0:T(8,128)(2,1)}) %reduce-scatter.7.cloned.1.call-update) | async-done | bytes 688144 | tf_op jit(solution)/shard_map/reduce_scatter | solution.py:123
  222.3 14.5 %all_gather.68 = bf16[384,4,128]{2,1,0:T(4,128)(2,1)S(1)} all-gather(bf16[96,4,128]{2,1,0:T(4,128)(2,1)S(1)} %copy.376), channel_id=1, replica_groups=mesh['req'=4,'mlp'=8] {'req'}, dimensions={0}, use_global_device_ids=true | all-gather | bytes 491520 | tf_op jit(solution)/shard_map/all_gather | solution.py:131
  239.3 8.1 %fusion.167 = (f32[64,8,4]{1,2,0:T(4,128)S(1)}, f32[64,8,4,128]{3,1,2,0:T(8,128)S(1)}) fusion(bf16[64,8,4,128]{3,2,1,0:T(4,128)(2,1)} %bitcast.313, pred[64,128]{1,0:T(8,128)(4,1)S(1)} %fusion.130, bf16[64,128,512]{2,1,0:T(8,128)(2,1)} %param.23), kind=kOutput, calls=%fused_computation.354 | convolution fusion | flops 67893248 | bytes 9977856 | tf_op jit(solution)/shard_map/sbhd,sthd->sbht/dot_general | solution.py:136
  251.7 4.7 fusion.24
  260.4 4.7 fusion.27
  276.5 13.3 %all_gather.77 = bf16[4,384,4]{1,2,0:T(4,128)(2,1)S(1)} all-gather(bf16[1,384,4]{1,2,0:T(4,128)(2,1)S(1)} %convert_element_type.365), channel_id=1, replica_groups=mesh['req'=4,'mlp'=8] {'req'}, dimensions={0}, use_global_device_ids=true | all-gather | bytes 15360 | tf_op jit(solution)/shard_map/all_gather | solution.py:21
  289.8 13.0 %all_gather.69 = bf16[4,384,4]{1,2,0:T(4,128)(2,1)S(1)} all-gather(bf16[1,384,4]{1,2,0:T(4,128)(2,1)S(1)} %convert_element_type.339), channel_id=1, replica_groups=mesh['req'=4,'mlp'=8] {'req'}, dimensions={0}, use_global_device_ids=true | all-gather | bytes 15360 | tf_op jit(solution)/shard_map/all_gather | solution.py:21
  302.8 13.3 %all_gather.70 = bf16[4,384,4]{1,2,0:T(4,128)(2,1)S(1)} all-gather(bf16[1,384,4]{1,2,0:T(4,128)(2,1)S(1)} %convert_element_type.343), channel_id=1, replica_groups=mesh['req'=4,'mlp'=8] {'req'}, dimensions={0}, use_global_device_ids=true | all-gather | bytes 15360 | tf_op jit(solution)/shard_map/all_gather | solution.py:21
  316.1 13.4 %all_gather.78 = bf16[4,384,4]{1,2,0:T(4,128)(2,1)S(1)} all-gather(bf16[1,384,4]{1,2,0:T(4,128)(2,1)S(1)} %convert_element_type.369), channel_id=1, replica_groups=mesh['req'=4,'mlp'=8] {'req'}, dimensions={0}, use_global_device_ids=true | all-gather | bytes 15360 | tf_op jit(solution)/shard_map/all_gather | solution.py:21
  335.0 10.4 %while.39 = (s32[]{:T(128)}, f32[384,4]{0,1:T(4,128)S(1)}, f32[384,4]{0,1:T(4,128)S(1)}, f32[384,4,128]{2,1,0:T(4,128)S(1)}, bf16[4,384,4]{1,2,0:T(4,128)(2,1)S(...) while((s32[]{:T(128)}, f32[384,4]{0,1:T(4,128)S(1)}, ...), condition=%wide.region_16.17_spmd, body=%wide.region_15.16_spmd.sunk | while | flops 798725 | bytes 2832527 | solution.py:29
  347.0 10.4 %while.38 = (s32[]{:T(128)}, f32[384,4]{0,1:T(4,128)S(1)}, f32[384,4]{0,1:T(4,128)S(1)}, f32[384,4,128]{2,1,0:T(4,128)S(1)}, bf16[4,384,4]{1,2,0:T(4,128)(2,1)S(...) while((s32[]{:T(128)}, f32[384,4]{0,1:T(4,128)S(1)}, ...), condition=%wide.region_7.8_spmd, body=%wide.region_6.7_spmd.sunk | while | flops 798725 | bytes 2832527 | solution.py:29
  360.1 17.4 %all_gather.80 = bf16[384,512]{1,0:T(8,128)(2,1)S(1)} all-gather(bf16[96,512]{1,0:T(8,128)(2,1)S(1)} %bitcast.341), channel_id=1, replica_groups=mesh['req'=4,'mlp'=8] {'req'}, dimensions={0}, use_global_device_ids=true | all-gather | bytes 491520 | tf_op jit(solution)/shard_map/all_gather | solution.py:186
  379.3 4.4 fusion.170
  385.3 17.6 %all_gather.72 = bf16[384,512]{1,0:T(8,128)(2,1)S(1)} all-gather(bf16[96,512]{1,0:T(8,128)(2,1)S(1)} %bitcast.342), channel_id=1, replica_groups=mesh['req'=4,'mlp'=8] {'req'}, dimensions={0}, use_global_device_ids=true | all-gather | bytes 491520 | tf_op jit(solution)/shard_map/all_gather | solution.py:186
  402.9 19.1 %all-gather.13.cloned.1.call-done = bf16[384,2048]{1,0:T(8,128)(2,1)} async-done(((bf16[96,2048]{1,0:T(8,128)(2,1)}), bf16[384,2048]{1,0:T(8,128)(2,1)}) %all-gather.13.cloned.1.call-update) | async-done | bytes 1572880 | tf_op jit(solution)/shard_map/all_gather | solution.py:187
  428.1 30.9 %reduce-scatter.13.cloned.1.call-done = bf16[48,1024]{1,0:T(8,128)(2,1)} async-done(((bf16[384,1024]{1,0:T(8,128)(2,1)}), bf16[48,1024]{1,0:T(8,128)(2,1)}) %reduce-scatter.13.cloned.1.call-update) | async-done | bytes 98320 | tf_op jit(solution)/shard_map/reduce_scatter | solution.py:189
  459.0 38.0 %reduce-scatter.9.cloned.1.call-done = bf16[48,1024]{1,0:T(8,128)(2,1)} async-done(((bf16[384,1024]{1,0:T(8,128)(2,1)}), bf16[48,1024]{1,0:T(8,128)(2,1)}) %reduce-scatter.9.cloned.1.call-update) | async-done | bytes 98320 | tf_op jit(solution)/shard_map/reduce_scatter | solution.py:189
  498.0 14.6 %all_gather.82 = bf16[48,4096]{1,0:T(8,128)(2,1)S(1)} all-gather(bf16[48,1024]{1,0:T(8,128)(2,1)S(1)} %get-tuple-element.544), channel_id=1, replica_groups=mesh['req'=4,'mlp'=8] {'req'}, dimensions={1}, use_global_device_ids=true | all-gather | bytes 491520 | tf_op jit(solution)/shard_map/all_gather | solution.py:47
  513.0 15.2 %all_gather.84 = bf16[48,4096]{1,0:T(8,128)(2,1)S(1)} all-gather(bf16[48,1024]{1,0:T(8,128)(2,1)S(1)} %get-tuple-element.545), channel_id=1, replica_groups=mesh['req'=4,'mlp'=8] {'req'}, dimensions={1}, use_global_device_ids=true | all-gather | bytes 491520 | tf_op jit(solution)/shard_map/all_gather | solution.py:47
  528.9 10.5 %all_gather.83 = bf16[384,1024]{1,0:T(8,128)(2,1)S(1)} all-gather(bf16[48,1024]{1,0:T(8,128)(2,1)S(1)} %get-tuple-element.560), channel_id=1, replica_groups=mesh['req'=4,'mlp'=8] {'mlp'}, dimensions={0}, use_global_device_ids=true | all-gather | bytes 884736 | tf_op jit(solution)/shard_map/all_gather | solution.py:201
  543.8 9.3 %all_gather.85 = bf16[384,1024]{1,0:T(8,128)(2,1)S(1)} all-gather(bf16[48,1024]{1,0:T(8,128)(2,1)S(1)} %get-tuple-element.561), channel_id=1, replica_groups=mesh['req'=4,'mlp'=8] {'mlp'}, dimensions={0}, use_global_device_ids=true | all-gather | bytes 884736 | tf_op jit(solution)/shard_map/all_gather | solution.py:201
  553.1 4.5 convolution_convert_fusion.2
  558.3 15.2 %reduce-scatter.15.cloned.1.call-done = bf16[96,1536]{1,0:T(8,128)(2,1)} async-done(((bf16[384,1536]{1,0:T(8,128)(2,1)}), bf16[96,1536]{1,0:T(8,128)(2,1)}) %reduce-scatter.15.cloned.1.call-update) | async-done | bytes 294928 | tf_op jit(solution)/shard_map/reduce_scatter | solution.py:205
  573.5 30.1 %reduce-scatter.17.cloned.1.call-done = bf16[96,1536]{1,0:T(8,128)(2,1)} async-done(((bf16[384,1536]{1,0:T(8,128)(2,1)}), bf16[96,1536]{1,0:T(8,128)(2,1)}) %reduce-scatter.17.cloned.1.call-update) | async-done | bytes 294928 | tf_op jit(solution)/shard_map/reduce_scatter | solution.py:205
  (286 shorter events, 112.2 us)
Async XLA Ops:
  7.2 62.6 %copy-start = (bf16[1024,1536]{1,0:T(8,128)(2,1)S(1)}, bf16[1024,1536]{1,0:T(8,128)(2,1)}, u32[]{:S(2)}) copy-start(bf16[1024,1536]{1,0:T(8,128)(2,1)} %param.18) | copy-start | bytes 9437188
  7.2 35.2 %copy-start.7 = (bf16[2,48,1024]{2,1,0:T(8,128)(2,1)S(1)}, bf16[2,48,1024]{2,1,0:T(8,128)(2,1)}, u32[]{:S(2)}) copy-start(bf16[2,48,1024]{2,1,0:T(8,128)(2,1)} %param.16) | copy-start | bytes 589828
  7.2 62.6 %all-gather.15.cloned.1.call-start = ((), (), s32[]{:S(2)}) async-start(), calls=%async_computation.11 | async-start | bytes 1769472 | tf_op jit(solution)/shard_map/all_gather | solution.py:118
  43.3 54.7 %all-gather.9.cloned.1.call-start = ((), (), s32[]{:S(2)}) async-start(), calls=%async_computation.6 | async-start | bytes 1769472 | tf_op jit(solution)/shard_map/all_gather | solution.py:118
  44.0 110.4 %reduce-scatter.11.cloned.1.call-start = ((), (), s32[]{:S(2)}) async-start(), calls=%async_computation.12 | async-start | bytes 3440640 | tf_op jit(solution)/shard_map/reduce_scatter | solution.py:123
  76.3 138.2 %reduce-scatter.7.cloned.1.call-start = ((), (), s32[]{:S(2)}) async-start(), calls=%async_computation.7 | async-start | bytes 3440640 | tf_op jit(solution)/shard_map/reduce_scatter | solution.py:123
  104.5 229.0 %all-gather.17.cloned.1.call-start = ((), (), s32[]{:S(2)}) async-start(), calls=%async_computation.13 | async-start | bytes 1966080 | tf_op jit(solution)/shard_map/all_gather | solution.py:21
  105.4 151.0 %copy-start.22 = (s32[64]{0:T(128)}, s32[64]{0:T(128)S(1)}, u32[]{:S(2)}) copy-start(s32[64]{0:T(128)S(1)} %get-tuple-element.564) | copy-start | bytes 772
  217.9 21.4 %copy-start.4 = (f32[96,4,3,128]{3,2,1,0:T(4,128)}, f32[96,4,3,128]{3,2,1,0:T(4,128)S(1)}, u32[]{:S(2)}) copy-start(f32[96,4,3,128]{3,2,1,0:T(4,128)S(1)} %reshape.502) | copy-start | bytes 1769476
  219.0 28.4 %copy-start.12 = (bf16[96,4,96]{0,2,1:T(8,128)(2,1)}, bf16[96,4,96]{0,2,1:T(8,128)(2,1)S(1)}, u32[]{:S(2)}) copy-start(bf16[96,4,96]{0,2,1:T(8,128)(2,1)S(1)} %slice.365) | copy-start | bytes 221188
  239.3 8.2 %copy-start.21 = (pred[64,48]{0,1:T(8,128)(4,1)S(1)}, pred[64,48]{0,1:T(8,128)(4,1)}, u32[]{:S(2)}) copy-start(pred[64,48]{0,1:T(8,128)(4,1)} %iota_compare_fusion) | copy-start | bytes 9220
  258.7 86.8 %all-gather.11.cloned.1.call-start = ((), (), s32[]{:S(2)}) async-start(), calls=%async_computation.8 | async-start | bytes 1966080 | tf_op jit(solution)/shard_map/all_gather | solution.py:21
  260.4 7.1 %copy-start.31 = (s32[1,96]{1,0:T(1,128)S(1)}, s32[1,96]{1,0:T(1,128)}, u32[]{:S(2)}) copy-start(s32[1,96]{1,0:T(1,128)} %param.27) | copy-start | bytes 1156
  265.1 5.1 copy-start.18
  265.2 6.6 %copy-start.6 = (bf16[96,3584]{1,0:T(8,128)(2,1)S(1)}, bf16[96,3584]{1,0:T(8,128)(2,1)}, u32[]{:S(2)}) copy-start(bf16[96,3584]{1,0:T(8,128)(2,1)} %reduce-scatter.11.cloned.1.call-done) | copy-start | bytes 2064388
  267.4 111.9 %all-gather.19.cloned.1.call-start = ((), (), s32[]{:S(2)}) async-start(), calls=%async_computation.14 | async-start | bytes 1966080 | tf_op jit(solution)/shard_map/all_gather | solution.py:187
  270.1 5.8 copy-start.15
  270.2 6.2 %copy-start.5 = (bf16[96,3584]{1,0:T(8,128)(2,1)S(1)}, bf16[96,3584]{1,0:T(8,128)(2,1)}, u32[]{:S(2)}) copy-start(bf16[96,3584]{1,0:T(8,128)(2,1)} %reduce-scatter.7.cloned.1.call-done) | copy-start | bytes 2064388
  271.8 57.7 %copy-start.13 = (bf16[96,4,96]{0,2,1:T(8,128)(2,1)S(1)}, bf16[96,4,96]{0,2,1:T(8,128)(2,1)}, u32[]{:S(2)}) copy-start(bf16[96,4,96]{0,2,1:T(8,128)(2,1)} %copy-done.12) | copy-start | bytes 221188
  271.8 57.7 %copy-start.17 = (bf16[96,4,32]{0,2,1:T(8,128)(2,1)S(1)}, bf16[96,4,32]{0,2,1:T(8,128)(2,1)}, u32[]{:S(2)}) copy-start(bf16[96,4,32]{0,2,1:T(8,128)(2,1)} %copy-done.16) | copy-start | bytes 73732
  271.9 57.6 %copy-start.19 = (bf16[96,4,32]{0,2,1:T(8,128)(2,1)S(1)}, bf16[96,4,32]{0,2,1:T(8,128)(2,1)}, u32[]{:S(2)}) copy-start(bf16[96,4,32]{0,2,1:T(8,128)(2,1)} %get-tuple-element.551) | copy-start | bytes 73732
  271.9 58.6 %copy-start.9 = (f32[96,4,128]{0,2,1:T(8,128)S(1)}, f32[96,4,128]{0,2,1:T(8,128)}, u32[]{:S(2)}) copy-start(f32[96,4,128]{0,2,1:T(8,128)} %get-tuple-element.549) | copy-start | bytes 589828
  271.9 58.6 %copy-start.20 = (bf16[1,96,4,32]{1,3,2,0:T(8,128)(2,1)S(1)}, bf16[1,96,4,32]{1,3,2,0:T(8,128)(2,1)}, u32[]{:S(2)}) copy-start(bf16[1,96,4,32]{1,3,2,0:T(8,128)(2,1)} %get-tuple-element.553) | copy-start | bytes 73732
  274.4 147.7 %all-gather.13.cloned.1.call-start = ((), (), s32[]{:S(2)}) async-start(), calls=%async_computation.9 | async-start | bytes 1966080 | tf_op jit(solution)/shard_map/all_gather | solution.py:187
  333.2 125.8 %reduce-scatter.13.cloned.1.call-start = ((), (), s32[]{:S(2)}) async-start(), calls=%async_computation.15 | async-start | bytes 884736 | tf_op jit(solution)/shard_map/reduce_scatter | solution.py:189
  377.6 6.2 %copy-start.3 = (bf16[512,1024]{1,0:T(8,128)(2,1)S(1)}, bf16[512,1024]{1,0:T(8,128)(2,1)}, u32[]{:S(2)}) copy-start(bf16[512,1024]{1,0:T(8,128)(2,1)} %param.20) | copy-start | bytes 3145732
  385.3 111.7 %reduce-scatter.9.cloned.1.call-start = ((), (), s32[]{:S(2)}) async-start(), calls=%async_computation.10 | async-start | bytes 884736 | tf_op jit(solution)/shard_map/reduce_scatter | solution.py:189
  426.5 70.5 %copy-start.8 = (bf16[2,48,1024]{2,1,0:T(8,128)(2,1)S(1)}, bf16[2,48,1024]{2,1,0:T(8,128)(2,1)}, u32[]{:S(2)}) copy-start(bf16[2,48,1024]{2,1,0:T(8,128)(2,1)} %param.16) | copy-start | bytes 589828
  428.0 100.7 %copy-start.24 = (f32[1,1024]{1,0:T(1,128)S(1)}, f32[1,1024]{1,0:T(1,128)}, u32[]{:S(2)}) copy-start(f32[1,1024]{1,0:T(1,128)} %get-tuple-element.554) | copy-start | bytes 12292
  428.1 145.5 %reduce-scatter.15.cloned.1.call-start = ((), (), s32[]{:S(2)}) async-start(), calls=%async_computation.16 | async-start | bytes 1474560 | tf_op jit(solution)/shard_map/reduce_scatter | solution.py:205
  543.7 59.9 %reduce-scatter.17.cloned.1.call-start = ((), (), s32[]{:S(2)}) async-start(), calls=%async_computation.17 | async-start | bytes 1474560 | tf_op jit(solution)/shard_map/reduce_scatter | solution.py:205
  553.1 52.4 %copy-start.1 = (bf16[1024,1536]{1,0:T(8,128)(2,1)S(1)}, bf16[1024,1536]{1,0:T(8,128)(2,1)}, u32[]{:S(2)}) copy-start(bf16[1024,1536]{1,0:T(8,128)(2,1)} %param.18) | copy-start | bytes 9437188
  (12 other events, 27.0 us)
Sparse Core Ops, SparseCore 0:
  43.4 26.3 all-gather.14
  72.3 25.6 all-gather.8
  100.3 54.1 reduce-scatter.10
  156.7 57.8 reduce-scatter.6
  258.8 38.9 all-gather.16
  299.2 36.2 all-gather.10
  337.0 42.2 all-gather.18
  381.4 40.5 all-gather.12
  425.2 33.7 reduce-scatter.12
  462.0 34.9 reduce-scatter.8
  543.8 29.6 reduce-scatter.14
  575.7 27.8 reduce-scatter.16
where the time goes:
time: 621 us; the launch traced here: 613 us
  waiting for transfers between devices  226 us (36%)
  blocking collectives  202 us (33%)
  other arithmetic  70.8 us (11%)
  matrix products  58.5 us (9%)
  local copies, waits for them, and re-layouts  39.1 us (6%)
  between operations  15.6 us (3%)
    reduce_scatter x2, waiting for transfers between devices, shards(): lax.psum_scatter((jnp.dot(attended_all, dense_weight, preferred_element_t...  68.9 us
    all_gather x4, blocking collectives, row_normalize(): whole = lax.all_gather(block, 'req', axis=1, tiled=True).astype(jnp.float32)  61.4 us
    all_gather x4, blocking collectives, combined_all(): lax.all_gather(part.astype(kind), axis)  53 us
    all_gather x2, waiting for transfers between devices, shards(): piece = lax.all_gather(joined, 'mlp', axis=0, tiled=True)  47.3 us
    reduce_scatter x2, waiting for transfers between devices, shards(): lax.psum_scatter(next_partial.astype(jnp.bfloat16), 'req', scatter_dimens...  45.3 us
    reduce_scatter x2, waiting for transfers between devices, shards(): lax.psum_scatter(partial_sums.astype(jnp.bfloat16), 'req', scatter_dimens...  43.5 us
    all_gather x2, blocking collectives, shards(): lax.all_gather(attended, 'req', axis=0, tiled=True)  35 us
    all_gather x2, blocking collectives, shards(): queries_all = lax.all_gather(queries_own, 'req', axis=0, tiled=True)  32.2 us
  transfers between devices with their start and end apart: 12, of which 10 were waited for; matrix products, arithmetic and copies ran while one was open for 20% of the time, Pallas kernels for 0%

commit v1 on v0

v1 whole, which is shorter than its diff:
```python
import functools
import math

import jax
import jax.numpy as jnp
from jax import lax
from jax.experimental import pallas as pl
from jax.experimental.pallas import tpu as pltpu
from jax.sharding import PartitionSpec as P

HD = 128
ROT = 32
PAGE = 128
BEAM = 8
STEPS = 2
LANES = 128
STAT_ROWS = 16
GROUP = 8

NEG_FILL = -1e30
EPSILON = 1e-05
F32 = jnp.float32
BF16 = jnp.bfloat16


def rotated(array, axis, distance):
    size = lax.axis_size(axis)
    return lax.ppermute(array, axis, [(k, (k + distance) % size) for k in range(size)])


def flipped(array, axis, bits):
    return lax.ppermute(array, axis, [(k, k ^ bits) for k in range(lax.axis_size(axis))])


def gather_rows(block):
    size = lax.axis_size("mlp")
    me = lax.axis_index("mlp")
    pair, core = me // 2, me % 2
    pairs = size // 2
    near = [block] + [flipped(block, "mlp", 2 * d) for d in range(1, pairs)]
    near = jnp.stack(near)
    far = flipped(near, "mlp", 1)
    order = pair ^ jnp.arange(pairs)
    near, far = near[order], far[order]
    first = jnp.where(core == 0, near, far)
    second = jnp.where(core == 0, far, near)
    return jnp.stack([first, second], axis=1).reshape((size,) + block.shape)


def scatter_rows(partial):
    size = lax.axis_size("mlp")
    me = lax.axis_index("mlp")
    pair, core = me // 2, me % 2
    pairs = size // 2
    split = partial.reshape((pairs, 2) + partial.shape[1:])
    mine = lax.dynamic_index_in_dim(split, core, 1, keepdims=False)
    other = lax.dynamic_index_in_dim(split, 1 - core, 1, keepdims=False)
    summed = (mine.astype(F32) + flipped(other, "mlp", 1).astype(F32)).astype(BF16)
    total = lax.dynamic_index_in_dim(summed, pair, 0, keepdims=False).astype(F32)
    for d in range(1, pairs):
        piece = lax.dynamic_index_in_dim(summed, pair ^ d, 0, keepdims=False)
        total = total + flipped(piece, "mlp", 2 * d).astype(F32)
    return total


def row_statistics(values):
    size = lax.axis_size("req")
    width = values.shape[1]
    part_mean = jnp.mean(values, axis=1)
    part_square = jnp.sum(jnp.square(values - part_mean[:, None]), axis=1)
    packed = jnp.stack([part_mean, part_square]).reshape(2, -1, LANES)
    parts = jnp.stack([packed] + [rotated(packed, "req", d) for d in range(1, size)])
    mean = jnp.mean(parts[:, 0], axis=0)
    square = jnp.sum(parts[:, 1] + width * jnp.square(parts[:, 0] - mean), axis=0)
    scale = lax.rsqrt(square / (width * size) + EPSILON)
    return mean.reshape(-1, 1), scale.reshape(-1, 1)


def rotary_tables(positions):
    lane = jnp.arange(HD, dtype=jnp.int32)[None, :]
    half = ROT // 2
    freq = jnp.exp((lane % half).astype(F32) * (-2.0 * math.log(10000.0) / ROT))
    angles = positions.astype(F32)[:, None] * freq
    cosine = jnp.where(lane < ROT, jnp.cos(angles), 1.0)
    sine = jnp.sin(angles)
    upper = jnp.where(lane < half, -sine, 0.0)
    lower = jnp.where((lane >= half) & (lane < ROT), sine, 0.0)
    return cosine, upper, lower


def full_block(shape):
    return pl.BlockSpec(shape, lambda *_: (0,) * len(shape))


def head_split_kernel(heads, parts, requests, x_ref, c_ref, u_ref, l_ref, q_ref, k_ref, v_ref):
    rows = requests * BEAM
    for head in range(heads):
        for kind, out in enumerate((q_ref, k_ref, v_ref)):
            column = (head * 3 + kind) * HD
            value = x_ref[:, column : column + HD].astype(F32)
            if kind < 2:
                value = (
                    value * c_ref[...]
                    + pltpu.roll(value, HD - ROT // 2, 1) * u_ref[...]
                    + pltpu.roll(value, ROT // 2, 1) * l_ref[...]
                )
            for part in range(parts):
                for request in range(requests):
                    first = part * STEPS * rows + request * BEAM
                    pair = [value[first + s * rows : first + s * rows + BEAM] for s in range(STEPS)]
                    at = ((part * requests + request) * heads + head) * STEPS * BEAM
                    out[at : at + STEPS * BEAM, :] = jnp.concatenate(pair, axis=0).astype(BF16)


def head_split(shared, tables, heads, parts, requests):
    rows = parts * requests * heads * STEPS * BEAM
    shape = jax.ShapeDtypeStruct((rows, HD), BF16)
    return pl.pallas_call(
        functools.partial(head_split_kernel, heads, parts, requests),
        out_shape=(shape, shape, shape),
        compiler_params=pltpu.CompilerParams(vmem_limit_bytes=32 << 20),
    )(shared, *tables)


def page_kernel(heads, ranks, own_rows, slot_ref, length_ref, me_ref, q_ref, k_ref, v_ref, *rest):
    outs, (top_ref, sum_ref, out_ref) = rest[:ranks], rest[ranks:]
    step = pl.program_id(0)
    height = heads * STEPS * BEAM
    chunk = STEPS * BEAM
    scale = 1.0 / math.sqrt(HD)

    @pl.when(step == 0)
    def _():
        top_ref[...] = jnp.full(top_ref.shape, NEG_FILL, F32)
        sum_ref[...] = jnp.zeros(sum_ref.shape, F32)
        out_ref[...] = jnp.zeros(out_ref.shape, F32)

    lane = lax.broadcasted_iota(jnp.int32, (height, PAGE), 1)
    found = []
    for g in range(GROUP):
        slot = step * GROUP + g
        owner = slot_ref[0, slot]
        valid = jnp.maximum(owner, 0)
        limit = jnp.where(owner >= 0, length_ref[valid] - slot_ref[1, slot] * PAGE, 0)
        base = pl.multiple_of(valid * height, height)
        scores = []
        for h in range(heads):
            query = q_ref[pl.ds(pl.multiple_of(base + h * chunk, chunk), chunk), :]
            key = k_ref[g, :, h * HD : (h + 1) * HD]
            scores.append(
                lax.dot_general(query, key, (((1,), (1,)), ((), ())), preferred_element_type=F32)
            )
        live = lane < limit
        score = jnp.where(live, jnp.concatenate(scores, axis=0) * scale, NEG_FILL)
        top = jnp.max(score, axis=1, keepdims=True)
        weight = jnp.where(live, jnp.exp(score - top), 0.0)
        total = jnp.sum(weight, axis=1, keepdims=True)
        weight = weight.astype(BF16)
        value = [
            jnp.dot(
                weight[h * chunk : (h + 1) * chunk],
                v_ref[g, :, h * HD : (h + 1) * HD],
                preferred_element_type=F32,
            )
            for h in range(heads)
        ]
        found.append((base, top, total, jnp.concatenate(value, axis=0)))
    for base, top, total, value in found:
        at = pl.ds(base, height)
        old = top_ref[at, :]
        new = jnp.maximum(old, top)
        left = jnp.exp(old - new)
        right = jnp.exp(top - new)
        top_ref[at, :] = new
        sum_ref[at, :] = sum_ref[at, :] * left + total * right
        out_ref[at, :] = out_ref[at, :] * left + value * right

    @pl.when(step == pl.num_programs(0) - 1)
    def _():
        eye = lax.broadcasted_iota(jnp.int32, (LANES, LANES), 0) == lax.broadcasted_iota(
            jnp.int32, (LANES, LANES), 1
        )
        blocks = own_rows // LANES
        for d in range(ranks):
            rank = lax.rem(me_ref[0] + d, ranks)
            levels = []
            for block in range(blocks):
                first = pl.multiple_of(rank * own_rows + block * LANES, LANES)
                total = sum_ref[pl.ds(first, LANES), :]
                some = total > 0.0
                total = jnp.where(some, total, 1.0)
                outs[d][block * LANES : (block + 1) * LANES, :] = (
                    out_ref[pl.ds(first, LANES), :] / total
                ).astype(BF16)
                level = jnp.where(some, top_ref[pl.ds(first, LANES), :] + jnp.log(total), NEG_FILL)
                levels.append(jnp.sum(jnp.where(eye, level, 0.0), axis=0, keepdims=True))
            levels.append(jnp.zeros((STAT_ROWS - blocks, LANES), F32))
            level = jnp.concatenate(levels, axis=0)
            for k in range(3):
                rounded = level.astype(BF16)
                level = level - rounded.astype(F32)
                outs[d][own_rows + k * STAT_ROWS : own_rows + (k + 1) * STAT_ROWS, :] = rounded


def page_attention(queries, keys, values, slot_table, lengths, heads, ranks):
    slots = keys.shape[0]
    rows = queries.shape[0]
    own_rows = rows // ranks
    me = lax.axis_index("req").astype(jnp.int32).reshape(1)
    out_rows = own_rows + 3 * STAT_ROWS
    shape = jax.ShapeDtypeStruct((out_rows, LANES), BF16)
    page_block = pl.BlockSpec((GROUP, PAGE, heads * HD), lambda g, *_: (g, 0, 0))
    return pl.pallas_call(
        functools.partial(page_kernel, heads, ranks, own_rows),
        out_shape=(shape,) * ranks,
        grid_spec=pltpu.PrefetchScalarGridSpec(
            num_scalar_prefetch=3,
            grid=(slots // GROUP,),
            in_specs=[full_block((rows, HD)), page_block, page_block],
            out_specs=[full_block((out_rows, LANES))] * ranks,
            scratch_shapes=[pltpu.VMEM((rows, LANES), F32)] * 3,
        ),
        compiler_params=pltpu.CompilerParams(vmem_limit_bytes=40 << 20),
        cost_estimate=pl.CostEstimate(
            flops=4 * slots * PAGE * heads * HD * STEPS * BEAM,
            bytes_accessed=2 * slots * PAGE * heads * HD * 2,
            transcendentals=slots * PAGE * heads * STEPS * BEAM,
        ),
    )(slot_table, lengths, me, queries, keys, values)


def merge_kernel(heads, ranks, parts, requests, q_ref, k_ref, v_ref, parent_ref, *rest):
    pieces, out, work = rest[:ranks], rest[ranks], rest[ranks + 1]
    chunk = STEPS * BEAM
    height = heads * chunk
    own_rows = q_ref.shape[0]
    scale = 1.0 / math.sqrt(HD)
    eye = lax.broadcasted_iota(jnp.int32, (LANES, LANES), 0) == lax.broadcasted_iota(
        jnp.int32, (LANES, LANES), 1
    )
    late = lax.broadcasted_iota(jnp.int32, (LANES, 1), 0) % chunk >= BEAM
    levels = []
    for piece in pieces:
        level = jnp.zeros((STAT_ROWS, LANES), F32)
        for k in range(3):
            first = own_rows + k * STAT_ROWS
            level = level + piece[first : first + STAT_ROWS, :].astype(F32)
        levels.append(level)
    for block in range(own_rows // LANES):
        at = slice(block * LANES, (block + 1) * LANES)
        query = q_ref[at, :].astype(F32)
        key = k_ref[at, :].astype(F32)
        value = v_ref[at, :].astype(F32)
        held_keys, held_values = [], []
        for tile in range(LANES // chunk):
            first = tile * chunk
            request = (block * LANES + first) // height
            parent = parent_ref[request * BEAM : (request + 1) * BEAM, :]
            for held, source in ((held_keys, key), (held_values, value)):
                chosen = jnp.zeros((BEAM, HD), F32)
                for beam in range(BEAM):
                    row = source[first + beam : first + beam + 1, :]
                    chosen = jnp.where(parent == beam, row, chosen)
                held += [jnp.zeros((BEAM, HD), F32), chosen]
        held_key = jnp.concatenate(held_keys, axis=0)
        held_value = jnp.concatenate(held_values, axis=0)
        own = jnp.sum(query * key, axis=1, keepdims=True) * scale
        past = jnp.sum(query * held_key, axis=1, keepdims=True) * scale
        past = jnp.where(late, past, NEG_FILL)
        columns = [
            jnp.sum(jnp.where(eye, level[block : block + 1, :], 0.0), axis=1, keepdims=True)
            for level in levels
        ]
        top = functools.reduce(jnp.maximum, columns, jnp.maximum(own, past))
        own = jnp.exp(own - top)
        past = jnp.where(late, jnp.exp(past - top), 0.0)
        total = own + past
        result = own * value + past * held_value
        for column, piece in zip(columns, pieces):
            factor = jnp.exp(column - top)
            total = total + factor
            result = result + factor * piece[at, :].astype(F32)
        work[at, :] = result / total
    rows = requests * BEAM
    for part in range(parts):
        for request in range(0, requests, 2):
            for head in range(heads):
                for s in range(STEPS):
                    tiles = []
                    for r in (request, request + 1):
                        first = (part * requests + r) * height + head * chunk + s * BEAM
                        tiles.append(work[first : first + BEAM, :])
                    first = (part * STEPS + s) * rows + request * BEAM
                    out[first : first + 2 * BEAM, head * HD : (head + 1) * HD] = jnp.concatenate(
                        tiles, axis=0
                    ).astype(BF16)


def merge(queries, keys, values, parents, pieces, heads, parts, requests):
    ranks = len(pieces)
    rows = parts * requests * STEPS * BEAM
    return pl.pallas_call(
        functools.partial(merge_kernel, heads, ranks, parts, requests),
        out_shape=jax.ShapeDtypeStruct((rows, heads * HD), BF16),
        scratch_shapes=[pltpu.VMEM(queries.shape, F32)],
        compiler_params=pltpu.CompilerParams(vmem_limit_bytes=32 << 20),
    )(queries, keys, values, parents, *pieces)


def shards(
    inputs,
    norm_gains,
    attn_weight,
    up_weight,
    dense_weight,
    down_weight,
    next_weight,
    cache_keys,
    cache_values,
    lengths,
    slot_table,
    parents,
):
    ranks = lax.axis_size("req")
    parts = lax.axis_size("mlp") // ranks
    own_count = parents.shape[1]
    beams = inputs.shape[1]
    width = inputs.shape[2]
    requests = beams // BEAM
    own_requests = own_count // BEAM
    heads = dense_weight.shape[0] // HD
    rank = lax.axis_index("req")

    own_lengths = lax.dynamic_slice_in_dim(lengths, rank * own_requests, own_requests, 0)
    positions = jnp.broadcast_to(
        own_lengths.reshape(parts, 1, requests, 1)
        + jnp.arange(STEPS, dtype=jnp.int32).reshape(1, STEPS, 1, 1),
        (parts, STEPS, requests, BEAM),
    ).reshape(-1)
    tables = rotary_tables(positions)
    parent_wide = jnp.broadcast_to(parents[0][:, None], (own_count, LANES))

    block = inputs.reshape(STEPS * beams, width)
    with jax.named_scope("gather_inputs"):
        everything = gather_rows(block).reshape(-1, width).astype(F32)
    with jax.named_scope("norm"):
        mean, scale = row_statistics(everything)
        normed = (everything - mean) * scale
        attn_in = (normed * norm_gains[0]).astype(BF16)
        mlp_in = (normed * norm_gains[1]).astype(BF16)
    with jax.named_scope("qkv"):
        mixed = jnp.dot(attn_in, attn_weight, preferred_element_type=F32).astype(BF16)
        mixed = lax.psum_scatter(mixed, "req", scatter_dimension=0, tiled=True)
    with jax.named_scope("up"):
        hidden = jnp.dot(mlp_in, up_weight, preferred_element_type=F32).astype(BF16)
        hidden = lax.psum_scatter(hidden, "req", scatter_dimension=0, tiled=True).astype(F32)
        activated = jax.nn.gelu(hidden, approximate=False).astype(BF16)
        activated = lax.all_gather(activated, "req", axis=0, tiled=True)
    with jax.named_scope("attention"):
        queries, keys, values = head_split(mixed, tables, heads, parts, requests)
        queries_all = lax.all_gather(queries, "req", axis=0, tiled=True)
        pieces = page_attention(
            queries_all, cache_keys, cache_values, slot_table, lengths, heads, ranks
        )
        pieces = [pieces[0]] + [rotated(pieces[d], "req", d) for d in range(1, ranks)]
        attended = merge(queries, keys, values, parent_wide, pieces, heads, parts, requests)
        attended = lax.all_gather(attended, "req", axis=0, tiled=True)
    with jax.named_scope("down"):
        update = jnp.dot(attended, dense_weight, preferred_element_type=F32) + jnp.dot(
            activated, down_weight, preferred_element_type=F32
        )
        update = scatter_rows(update.astype(BF16).reshape(-1, STEPS * beams, width))
        layer = (block.astype(F32) + update).astype(BF16)
    with jax.named_scope("next"):
        everything = gather_rows(layer).reshape(-1, width).astype(F32)
        mean, scale = row_statistics(everything)
        next_in = ((everything - mean) * scale * norm_gains[2]).astype(BF16)
        following = jnp.dot(next_in, next_weight, preferred_element_type=F32).astype(BF16)
        following = lax.psum_scatter(following, "req", scatter_dimension=0, tiled=True)
        following = following.reshape(parts, STEPS, beams, -1).transpose(1, 0, 2, 3)
    return layer.reshape(STEPS, beams, width), following.reshape(STEPS, own_count, -1)


def solution(mesh):
    in_specs = (
        P(None, "mlp", "req"),
        P(None, "req"),
        P("req", "mlp"),
        P("req", "mlp"),
        P("mlp", "req"),
        P("mlp", "req"),
        P("req", "mlp"),
        P("req", None, "mlp"),
        P("req", None, "mlp"),
        P(),
        P(None, "req"),
        P(None, "req"),
    )
    out_specs = (P(None, "mlp", "req"), P(None, "req", "mlp"))
    return jax.shard_map(shards, mesh=mesh, in_specs=in_specs, out_specs=out_specs, check_vma=False)
```

time: 621 us -> 372 us (0.60); the launches traced: 613 us -> 371 us
  blocking collectives: 202 us -> 50.1 us
  other arithmetic: 70.8 us -> 17 us
  matrix products: 58.5 us -> 21.1 us
  starting transfers between devices: 0.96 us -> 26.3 us
  waiting for transfers between devices: 226 us -> 203 us
  Pallas kernels: 0 us -> 22.3 us
  local copies, waits for them, and re-layouts: 39.1 us -> 17.3 us
    all_gather x14 -> x2, blocking collectives: 202 us -> 50.1 us  [the longest x1 27.2 us: shards(): attended = lax.all_gather(attended, 'req', axis=0, tiled=True)]
    all_gather x6 -> x1, waiting for transfers between devices: 68.2 us -> 0.01 us  [shards(): activated = lax.all_gather(activated, 'req', axis=0, tiled=True)]
    ppermute x0 -> x21, waiting for transfers between devices: none -> 55.3 us  [the longest x12 29.7 us: flipped(): lax.ppermute(array, axis, [(k, k ^ bits) for k in range(lax.axis_size(axi...]
    dot_general x19 -> x5, matrix products: 58.5 us -> 21.1 us  [the longest x1 6.22 us: shards(): jnp.dot(activated, down_weight, preferred_element_type=F32)]
    gather x26 -> x1, other arithmetic: 30.6 us -> 0.01 us  [gather_rows(): near, far = (near[order], far[order])]
    ppermute x0 -> x21, starting transfers between devices: none -> 26.1 us  [the longest x9 14.3 us: rotated(): lax.ppermute(array, axis, [(k, (k + distance) % size) for k in range(size)])]
    pallas_call x0 -> x3, Pallas kernels: none -> 22.3 us  [the longest x1 20.8 us: page_attention(): pl.pallas_call(functools.partial(page_kernel, heads, ranks, own_rows), ou...]
    add x14 -> x0, other arithmetic: 12.7 us -> none  [the longest x6 12.4 us: merge_partials(): first[2] * left[..., None] + second[2] * right[..., None]]
  transfers between devices with their start and end apart: 12 -> 25, of which waited for: 10 -> 15; matrix products, arithmetic and copies ran while one was open for 20% -> 5% of each run, Pallas kernels for 0% -> 6%
where the time goes in v1:
time: 372 us; the launch traced here: 371 us
  waiting for transfers between devices  203 us (55%)
  blocking collectives  50.1 us (13%)
  starting transfers between devices  26.3 us (7%)
  Pallas kernels  22.3 us (6%)
  matrix products  21.1 us (6%)
  local copies, waits for them, and re-layouts  17.3 us (5%)
  other arithmetic  17 us (5%)
  between operations  14.2 us (4%)
    reduce_scatter x1, waiting for transfers between devices, shards(): lax.psum_scatter(hidden, 'req', scatter_dimension=0, tiled=True).astype(F32)  54.8 us
    reduce_scatter x1, waiting for transfers between devices, shards(): lax.psum_scatter(following, 'req', scatter_dimension=0, tiled=True)  48.2 us
    reduce_scatter x1, waiting for transfers between devices, shards(): mixed = lax.psum_scatter(mixed, 'req', scatter_dimension=0, tiled=True)  44.3 us
    ppermute x12, waiting for transfers between devices, flipped(): lax.ppermute(array, axis, [(k, k ^ bits) for k in range(lax.axis_size(axi...  29.7 us
    all_gather x1, blocking collectives, shards(): attended = lax.all_gather(attended, 'req', axis=0, tiled=True)  27.2 us
    ppermute x9, waiting for transfers between devices, rotated(): lax.ppermute(array, axis, [(k, (k + distance) % size) for k in range(size)])  25.5 us
    all_gather x1, blocking collectives, shards(): queries_all = lax.all_gather(queries, 'req', axis=0, tiled=True)  22.9 us
    pallas_call x1, Pallas kernels, page_attention(): pl.pallas_call(functools.partial(page_kernel, heads, ranks, own_rows), ou...  20.8 us
  transfers between devices with their start and end apart: 25, of which 15 were waited for; matrix products, arithmetic and copies ran while one was open for 5% of the time, Pallas kernels for 6%

profile of v1, /device:TPU:0, one launch (start us, length us, event | category | flops | bytes accessed | tf_op | source)
XLA Modules:
  0.0 371.0 jit_solution(8879913674614466613)
XLA Ops:
  7.2 3.0 collective-permute-start
  11.8 4.4 %collective-permute-done = bf16[96,1024]{1,0:T(8,128)(2,1)S(1)} collective-permute-done((bf16[96,1024]{1,0:T(8,128)(2,1)}, bf16[96,1024]{1,0:T(8,128)(2,1)S(1)}, u32[]{:S(2)}, u32[]{:S(2)}) %collective-permute-start) | collective-permute-done | bytes 196640 | tf_op jit(solution)/shard_map/gather_inputs/ppermute | solution.py:32
  16.2 4.8 %collective-permute-done.1 = bf16[96,1024]{1,0:T(8,128)(2,1)S(1)} collective-permute-done((bf16[96,1024]{1,0:T(8,128)(2,1)}, bf16[96,1024]{1,0:T(8,128)(2,1)S(1)}, u32[]{:S(2)}, u32[]{:S(2)}) %collective-permute-start.1) | collective-permute-done | bytes 196640 | tf_op jit(solution)/shard_map/gather_inputs/ppermute | solution.py:32
  21.0 1.9 pad_maximum_fusion.1
  23.0 2.6 gather_fusion
  25.6 2.6 gather_fusion.1
  33.2 2.6 collective-permute-start.5
  37.8 1.7 collective-permute-done.6
  39.5 3.4 multiply_convert_fusion.1
  42.9 4.8 %convolution_convert_fusion.2 = bf16[768,2048]{1,0:T(8,128)(2,1)} fusion(bf16[768,1024]{1,0:T(8,128)(2,1)S(1)} %get-tuple-element.17, bf16[1024,2048]{1,0:T(8,128)(2,1)S(1)} %copy-done.15), kind=kOutput, calls=%fused_computation.6 | convolution fusion | flops 3222798336 | bytes 8912896 | tf_op jit(solution)/shard_map/up/dot_general | solution.py:355
  47.8 5.3 %convolution_convert_fusion.1 = bf16[768,1536]{1,0:T(8,128)(2,1)} fusion(bf16[768,1024]{1,0:T(8,128)(2,1)} %get-tuple-element.16, bf16[1024,1536]{1,0:T(8,128)(2,1)S(1)} %copy-done), kind=kOutput, calls=%fused_computation.5 | convolution fusion | flops 2417098752 | bytes 7077888 | tf_op jit(solution)/shard_map/qkv/dot_general | solution.py:352
  53.2 54.8 %reduce-scatter.6.cloned.1.call-done = bf16[192,2048]{1,0:T(8,128)(2,1)} async-done(((bf16[768,2048]{1,0:T(8,128)(2,1)}), bf16[192,2048]{1,0:T(8,128)(2,1)}) %reduce-scatter.6.cloned.1.call-update) | async-done | bytes 786448 | tf_op jit(solution)/shard_map/up/reduce_scatter | solution.py:356
  108.0 5.2 %fusion.5 = bf16[192,2048]{1,0:T(8,128)(2,1)} fusion(bf16[192,2048]{1,0:T(8,128)(2,1)} %reduce-scatter.6.cloned.1.call-done), kind=kLoop, calls=%fused_computation.23 | loop fusion | flops 25952256 | bytes 1572864 | tf_op jit(solution)/shard_map/up/convert_element_type | solution.py:357
  114.1 44.3 %reduce-scatter.4.cloned.1.call-done.x_ref = bf16[192,1536]{1,0:T(8,128)(2,1)} async-done(((bf16[768,1536]{1,0:T(8,128)(2,1)}), bf16[192,1536]{1,0:T(8,128)(2,1)}) %reduce-scatter.4.cloned.1.call-update) | async-done | bytes 589840 | tf_op jit(solution)/shard_map/qkv/reduce_scatter | solution.py:353
  159.8 22.9 %all_gather.9.q_ref = bf16[3072,128]{1,0:T(8,128)(2,1)S(1)} all-gather(bf16[768,128]{1,0:T(8,128)(2,1)S(1)} %get-tuple-element.9.q_ref), channel_id=1, replica_groups=mesh['req'=4,'mlp'=8] {'req'}, dimensions={0}, use_global_device_ids=true | all-gather | bytes 983040 | tf_op jit(solution)/shard_map/attention/all_gather | solution.py:361
  182.7 3.4 copy-done.2
  186.1 20.8 %attention.4 = (bf16[816,128]{1,0:T(8,128)(2,1)S(1)}, bf16[816,128]{1,0:T(8,128)(2,1)S(1)}, bf16[816,128]{1,0:T(8,128)(2,1)S(1)}, bf16[816,128]{1,0:T(8,128)(2,1)S(1)}) custom-call(s32[2,64]{1,0:T(2,128)S(1)} %copy-done.4, s32[48]{0:T(128)S(1)} %copy-done.5, s32[1]{0:T(128)} %bitcast.19.me_ref, bf16[3072,128]{1,0:T(8,128)(2,1)S(1)} %all_gather.9.q_ref, ...), custom_call_target="tpu_custom_call" | custom-call | flops 268435456 | bytes 16777216 | tf_op jit(solution)/shard_map/attention/pallas_call | solution.py:213
  207.0 1.8 collective-permute-start.7
  208.7 3.2 collective-permute-start.8
  211.9 9.9 %collective-permute-done.7.rest_1_ = bf16[816,128]{1,0:T(8,128)(2,1)S(1)} collective-permute-done((bf16[816,128]{1,0:T(8,128)(2,1)S(1)}, bf16[816,128]{1,0:T(8,128)(2,1)S(1)}, u32[]{:S(2)}, u32[]{:S(2)}) %collective-permute-start.7) | collective-permute-done | bytes 208928 | tf_op jit(solution)/shard_map/attention/ppermute | solution.py:28
  221.8 13.5 %collective-permute-done.8.rest_2_ = bf16[816,128]{1,0:T(8,128)(2,1)S(1)} collective-permute-done((bf16[816,128]{1,0:T(8,128)(2,1)S(1)}, bf16[816,128]{1,0:T(8,128)(2,1)S(1)}, u32[]{:S(2)}, u32[]{:S(2)}) %collective-permute-start.8) | collective-permute-done | bytes 208928 | tf_op jit(solution)/shard_map/attention/ppermute | solution.py:28
  236.5 27.2 %all_gather.10 = bf16[768,512]{1,0:T(8,128)(2,1)S(1)} all-gather(bf16[192,512]{1,0:T(8,128)(2,1)S(1)} %attention.5), channel_id=1, replica_groups=mesh['req'=4,'mlp'=8] {'req'}, dimensions={0}, use_global_device_ids=true | all-gather | bytes 983040 | tf_op jit(solution)/shard_map/attention/all_gather | solution.py:367
  263.7 6.2 %fusion.60 = f32[768,1024]{1,0:T(8,128)S(1)} fusion(bf16[768,2048]{1,0:T(8,128)(2,1)} %all-gather.2.cloned.1.call-done, bf16[2048,1024]{1,0:T(8,128)(2,1)} %param.17), kind=kOutput, calls=%fused_computation.119 | convolution fusion | flops 3221225472 | bytes 10485760 | tf_op jit(solution)/shard_map/down/dot_general | solution.py:369
  271.1 2.2 collective-permute-done.10
  277.3 4.3 %collective-permute-done.11 = bf16[96,1024]{1,0:T(8,128)(2,1)S(1)} collective-permute-done((bf16[96,1024]{1,0:T(8,128)(2,1)S(1)}, bf16[96,1024]{1,0:T(8,128)(2,1)S(1)}, u32[]{:S(2)}, u32[]{:S(2)}) %collective-permute-start.11) | collective-permute-done | bytes 196640 | tf_op jit(solution)/shard_map/down/ppermute | solution.py:32
  281.5 4.6 %collective-permute-done.12 = bf16[96,1024]{1,0:T(8,128)(2,1)S(1)} collective-permute-done((bf16[96,1024]{1,0:T(8,128)(2,1)S(1)}, bf16[96,1024]{1,0:T(8,128)(2,1)S(1)}, u32[]{:S(2)}, u32[]{:S(2)}) %collective-permute-start.12) | collective-permute-done | bytes 196640 | tf_op jit(solution)/shard_map/down/ppermute | solution.py:32
  289.9 4.2 %collective-permute-done.14 = bf16[96,1024]{1,0:T(8,128)(2,1)S(1)} collective-permute-done((bf16[96,1024]{1,0:T(8,128)(2,1)S(1)}, bf16[96,1024]{1,0:T(8,128)(2,1)S(1)}, u32[]{:S(2)}, u32[]{:S(2)}) %collective-permute-start.14) | collective-permute-done | bytes 196640 | tf_op jit(solution)/shard_map/next/ppermute | solution.py:32
  294.1 3.5 collective-permute-done.15
  302.5 2.3 collective-permute-start.19
  310.5 3.8 %convolution_convert_fusion = bf16[768,1536]{1,0:T(8,128)(2,1)} fusion(bf16[768,1024]{1,0:T(8,128)(2,1)S(1)} %fusion.2, bf16[1024,1536]{1,0:T(8,128)(2,1)S(1)} %copy-done.16), kind=kOutput, calls=%fused_computation.4 | convolution fusion | flops 2417098752 | bytes 7077888 | tf_op jit(solution)/shard_map/next/dot_general | solution.py:378
  314.3 48.2 %reduce-scatter.8.cloned.1.call-done = bf16[192,1536]{1,0:T(8,128)(2,1)} async-done(((bf16[768,1536]{1,0:T(8,128)(2,1)}), bf16[192,1536]{1,0:T(8,128)(2,1)}) %reduce-scatter.8.cloned.1.call-update) | async-done | bytes 589840 | tf_op jit(solution)/shard_map/next/reduce_scatter | solution.py:379
  362.6 1.9 copy.53
  (127 shorter events, 31.2 us)
Async XLA Ops:
  7.2 40.6 %copy-start = (bf16[1024,1536]{1,0:T(8,128)(2,1)S(1)}, bf16[1024,1536]{1,0:T(8,128)(2,1)}, u32[]{:S(2)}) copy-start(bf16[1024,1536]{1,0:T(8,128)(2,1)} %param.14) | copy-start | bytes 9437188
  7.2 100.8 %reduce-scatter.6.cloned.1.call-start = ((), (), s32[]{:S(2)}) async-start(), calls=%async_computation.4 | async-start | bytes 3932160 | tf_op jit(solution)/shard_map/up/reduce_scatter | solution.py:356
  7.2 8.9 %collective-permute-start = (bf16[96,1024]{1,0:T(8,128)(2,1)}, bf16[96,1024]{1,0:T(8,128)(2,1)S(1)}, u32[]{:S(2)}, u32[]{:S(2)}) collective-permute-start(bf16[96,1024]{1,0:T(8,128)(2,1)} %bitcast.126), channel_id=1, source_target_pairs={{0,2},{1,3},{2,0},{3,1},{4,6},{5,7},{6,4},{7,5},{8,10},{9,11},{10,... | collective-permute-start | bytes 589832 | tf_op jit(solution)/shard_map/gather_inputs/ppermute | solution.py:32
  10.2 10.8 %collective-permute-start.1 = (bf16[96,1024]{1,0:T(8,128)(2,1)}, bf16[96,1024]{1,0:T(8,128)(2,1)S(1)}, u32[]{:S(2)}, u32[]{:S(2)}) collective-permute-start(bf16[96,1024]{1,0:T(8,128)(2,1)} %bitcast.127), channel_id=1, source_target_pairs={{0,4},{1,5},{2,6},{3,7},{4,0},{5,1},{6,2},{7,3},{8,12},{9,13},{10,... | collective-permute-start | bytes 589832 | tf_op jit(solution)/shard_map/gather_inputs/ppermute | solution.py:32
  11.7 9.3 %collective-permute-start.2 = (bf16[96,1024]{1,0:T(8,128)(2,1)}, bf16[96,1024]{1,0:T(8,128)(2,1)S(1)}, u32[]{:S(2)}, u32[]{:S(2)}) collective-permute-start(bf16[96,1024]{1,0:T(8,128)(2,1)} %bitcast.128), channel_id=1, source_target_pairs={{0,6},{1,7},{2,4},{3,5},{4,2},{5,3},{6,0},{7,1},{8,14},{9,15},{10,... | collective-permute-start | bytes 589832 | tf_op jit(solution)/shard_map/gather_inputs/ppermute | solution.py:32
  23.0 2.7 collective-permute-start.3
  31.6 5.7 %collective-permute-start.4 = (f32[2,6,128]{2,1,0:T(8,128)S(1)}, f32[2,6,128]{2,1,0:T(8,128)S(1)}, u32[]{:S(2)}, u32[]{:S(2)}) collective-permute-start(f32[2,6,128]{2,1,0:T(8,128)S(1)} %constant_dynamic-update-slice_fusion), channel_id=1, source_target_pairs={{0,8},{8,16},{16,24},{24,0},{1,9},{9,17},{17,25},{25,1},{2,10},{10... | collective-permute-start | bytes 18440 | tf_op jit(solution)/shard_map/norm/ppermute | solution.py:28
  33.2 4.5 %collective-permute-start.5 = (f32[2,6,128]{2,1,0:T(8,128)S(1)}, f32[2,6,128]{2,1,0:T(8,128)S(1)}, u32[]{:S(2)}, u32[]{:S(2)}) collective-permute-start(f32[2,6,128]{2,1,0:T(8,128)S(1)} %constant_dynamic-update-slice_fusion), channel_id=1, source_target_pairs={{0,16},{8,24},{16,0},{24,8},{1,17},{9,25},{17,1},{25,9},{2,18},{10... | collective-permute-start | bytes 18440 | tf_op jit(solution)/shard_map/norm/ppermute | solution.py:28
  35.8 3.7 collective-permute-start.6
  47.7 110.7 %reduce-scatter.4.cloned.1.call-start = ((), (), s32[]{:S(2)}) async-start(), calls=%async_computation.3 | async-start | bytes 2949120 | tf_op jit(solution)/shard_map/qkv/reduce_scatter | solution.py:353
  53.1 60.2 %copy-start.5 = (s32[48]{0:T(128)S(1)}, s32[48]{0:T(128)}, u32[]{:S(2)}) copy-start(s32[48]{0:T(128)} %length_ref.1) | copy-start | bytes 580
  53.1 210.6 %all-gather.2.cloned.1.call-start = ((), (), s32[]{:S(2)}) async-start(), calls=%async_computation.5 | async-start | bytes 3932160 | tf_op jit(solution)/shard_map/up/all_gather | solution.py:358
  113.2 69.6 %copy-start.4 = (s32[2,64]{1,0:T(2,128)S(1)}, s32[2,64]{1,0:T(2,128)}, u32[]{:S(2)}) copy-start(s32[2,64]{1,0:T(2,128)} %slot_ref.1) | copy-start | bytes 1540
  113.2 249.4 %reduce-scatter.8.cloned.1.call-start = ((), (), s32[]{:S(2)}) async-start(), calls=%async_computation.6 | async-start | bytes 2949120 | tf_op jit(solution)/shard_map/next/reduce_scatter | solution.py:379
  186.1 49.2 %copy-start.14 = (s32[1,96]{1,0:T(1,128)S(1)}, s32[1,96]{1,0:T(1,128)}, u32[]{:S(2)}) copy-start(s32[1,96]{1,0:T(1,128)} %param.23) | copy-start | bytes 1156
  207.0 14.8 %collective-permute-start.7 = (bf16[816,128]{1,0:T(8,128)(2,1)S(1)}, bf16[816,128]{1,0:T(8,128)(2,1)S(1)}, u32[]{:S(2)}, u32[]{:S(2)}) collective-permute-start(bf16[816,128]{1,0:T(8,128)(2,1)S(1)} %get-tuple-element.13), channel_id=1, source_target_pairs={{0,8},{8,16},{16,24},{24,0},{1,9},{9,17},{17,25},{25,1},{2,10},{10... | collective-permute-start | bytes 626696 | tf_op jit(solution)/shard_map/attention/ppermute | solution.py:28
  208.7 26.6 %collective-permute-start.8 = (bf16[816,128]{1,0:T(8,128)(2,1)S(1)}, bf16[816,128]{1,0:T(8,128)(2,1)S(1)}, u32[]{:S(2)}, u32[]{:S(2)}) collective-permute-start(bf16[816,128]{1,0:T(8,128)(2,1)S(1)} %get-tuple-element.14), channel_id=1, source_target_pairs={{0,16},{8,24},{16,0},{24,8},{1,17},{9,25},{17,1},{25,9},{2,18},{10... | collective-permute-start | bytes 626696 | tf_op jit(solution)/shard_map/attention/ppermute | solution.py:28
  211.9 23.4 %collective-permute-start.9 = (bf16[816,128]{1,0:T(8,128)(2,1)S(1)}, bf16[816,128]{1,0:T(8,128)(2,1)S(1)}, u32[]{:S(2)}, u32[]{:S(2)}) collective-permute-start(bf16[816,128]{1,0:T(8,128)(2,1)S(1)} %get-tuple-element.15), channel_id=1, source_target_pairs={{0,24},{8,0},{16,8},{24,16},{1,25},{9,1},{17,9},{25,17},{2,26},{10... | collective-permute-start | bytes 626696 | tf_op jit(solution)/shard_map/attention/ppermute | solution.py:28
  271.0 2.4 collective-permute-start.10
  271.1 15.0 %copy-start.11 = (bf16[2,48,1024]{2,1,0:T(8,128)(2,1)S(1)}, bf16[2,48,1024]{2,1,0:T(8,128)(2,1)}, u32[]{:S(2)}) copy-start(bf16[2,48,1024]{2,1,0:T(8,128)(2,1)} %param.12) | copy-start | bytes 589828
  273.7 7.8 %collective-permute-start.11 = (bf16[96,1024]{1,0:T(8,128)(2,1)S(1)}, bf16[96,1024]{1,0:T(8,128)(2,1)S(1)}, u32[]{:S(2)}, u32[]{:S(2)}) collective-permute-start(bf16[96,1024]{1,0:T(8,128)(2,1)S(1)} %get-tuple-element.22), channel_id=1, source_target_pairs={{0,2},{1,3},{2,0},{3,1},{4,6},{5,7},{6,4},{7,5},{8,10},{9,11},{10,... | collective-permute-start | bytes 589832 | tf_op jit(solution)/shard_map/down/ppermute | solution.py:32
  275.2 10.9 %collective-permute-start.12 = (bf16[96,1024]{1,0:T(8,128)(2,1)S(1)}, bf16[96,1024]{1,0:T(8,128)(2,1)S(1)}, u32[]{:S(2)}, u32[]{:S(2)}) collective-permute-start(bf16[96,1024]{1,0:T(8,128)(2,1)S(1)} %get-tuple-element.24), channel_id=1, source_target_pairs={{0,4},{1,5},{2,6},{3,7},{4,0},{5,1},{6,2},{7,3},{8,12},{9,13},{10,... | collective-permute-start | bytes 589832 | tf_op jit(solution)/shard_map/down/ppermute | solution.py:32
  276.7 9.4 %collective-permute-start.13 = (bf16[96,1024]{1,0:T(8,128)(2,1)S(1)}, bf16[96,1024]{1,0:T(8,128)(2,1)S(1)}, u32[]{:S(2)}, u32[]{:S(2)}) collective-permute-start(bf16[96,1024]{1,0:T(8,128)(2,1)S(1)} %get-tuple-element.23), channel_id=1, source_target_pairs={{0,6},{1,7},{2,4},{3,5},{4,2},{5,3},{6,0},{7,1},{8,14},{9,15},{10,... | collective-permute-start | bytes 589832 | tf_op jit(solution)/shard_map/down/ppermute | solution.py:32
  286.3 12.1 %copy-start.12 = (bf16[96,1024]{1,0:T(8,128)(2,1)}, bf16[96,1024]{1,0:T(8,128)(2,1)S(1)}, u32[]{:S(2)}) copy-start(bf16[96,1024]{1,0:T(8,128)(2,1)S(1)} %fusion.40) | copy-start | bytes 589828
  286.3 7.8 %collective-permute-start.14 = (bf16[96,1024]{1,0:T(8,128)(2,1)S(1)}, bf16[96,1024]{1,0:T(8,128)(2,1)S(1)}, u32[]{:S(2)}, u32[]{:S(2)}) collective-permute-start(bf16[96,1024]{1,0:T(8,128)(2,1)S(1)} %fusion.40), channel_id=1, source_target_pairs={{0,2},{1,3},{2,0},{3,1},{4,6},{5,7},{6,4},{7,5},{8,10},{9,11},{10,... | collective-permute-start | bytes 589832 | tf_op jit(solution)/shard_map/next/ppermute | solution.py:32
  287.6 10.0 %collective-permute-start.15 = (bf16[96,1024]{1,0:T(8,128)(2,1)S(1)}, bf16[96,1024]{1,0:T(8,128)(2,1)S(1)}, u32[]{:S(2)}, u32[]{:S(2)}) collective-permute-start(bf16[96,1024]{1,0:T(8,128)(2,1)S(1)} %fusion.40), channel_id=1, source_target_pairs={{0,4},{1,5},{2,6},{3,7},{4,0},{5,1},{6,2},{7,3},{8,12},{9,13},{10,... | collective-permute-start | bytes 589832 | tf_op jit(solution)/shard_map/next/ppermute | solution.py:32
  288.4 9.2 %collective-permute-start.16 = (bf16[96,1024]{1,0:T(8,128)(2,1)S(1)}, bf16[96,1024]{1,0:T(8,128)(2,1)S(1)}, u32[]{:S(2)}, u32[]{:S(2)}) collective-permute-start(bf16[96,1024]{1,0:T(8,128)(2,1)S(1)} %fusion.40), channel_id=1, source_target_pairs={{0,6},{1,7},{2,4},{3,5},{4,2},{5,3},{6,0},{7,1},{8,14},{9,15},{10,... | collective-permute-start | bytes 589832 | tf_op jit(solution)/shard_map/next/ppermute | solution.py:32
  297.7 2.4 collective-permute-start.17
  302.5 6.0 %collective-permute-start.18 = (f32[2,6,128]{2,1,0:T(8,128)S(1)}, f32[2,6,128]{2,1,0:T(8,128)S(1)}, u32[]{:S(2)}, u32[]{:S(2)}) collective-permute-start(f32[2,6,128]{2,1,0:T(8,128)S(1)} %constant_dynamic-update-slice_fusion.2), channel_id=1, source_target_pairs={{0,8},{8,16},{16,24},{24,0},{1,9},{9,17},{17,25},{25,1},{2,10},{10... | collective-permute-start | bytes 18440 | tf_op jit(solution)/shard_map/next/ppermute | solution.py:28
  302.5 6.0 %collective-permute-start.19 = (f32[2,6,128]{2,1,0:T(8,128)S(1)}, f32[2,6,128]{2,1,0:T(8,128)S(1)}, u32[]{:S(2)}, u32[]{:S(2)}) collective-permute-start(f32[2,6,128]{2,1,0:T(8,128)S(1)} %constant_dynamic-update-slice_fusion.2), channel_id=1, source_target_pairs={{0,16},{8,24},{16,0},{24,8},{1,17},{9,25},{17,1},{25,9},{2,18},{10... | collective-permute-start | bytes 18440 | tf_op jit(solution)/shard_map/next/ppermute | solution.py:28
  304.9 3.7 collective-permute-start.20
  314.3 50.2 %copy-start.1 = (bf16[1024,1536]{1,0:T(8,128)(2,1)S(1)}, bf16[1024,1536]{1,0:T(8,128)(2,1)}, u32[]{:S(2)}) copy-start(bf16[1024,1536]{1,0:T(8,128)(2,1)} %param.14) | copy-start | bytes 9437188
  (10 other events, 27.9 us)
Sparse Core Ops, SparseCore 0:
  47.8 60.1 reduce-scatter.5
  110.3 48.0 reduce-scatter.3
  159.9 85.0 all-gather.1
  314.4 48.0 reduce-scatter.7

commit v2 on v1

--- a/solution.py
+++ b/solution.py
@@ -32,48 +32,224 @@
     return lax.ppermute(array, axis, [(k, k ^ bits) for k in range(lax.axis_size(axis))])
 
 
-def gather_rows(block):
-    size = lax.axis_size("mlp")
-    me = lax.axis_index("mlp")
-    pair, core = me // 2, me % 2
-    pairs = size // 2
+def gather_pieces(block):
+    pairs = lax.axis_size("mlp") // 2
     near = [block] + [flipped(block, "mlp", 2 * d) for d in range(1, pairs)]
-    near = jnp.stack(near)
-    far = flipped(near, "mlp", 1)
-    order = pair ^ jnp.arange(pairs)
-    near, far = near[order], far[order]
-    first = jnp.where(core == 0, near, far)
-    second = jnp.where(core == 0, far, near)
-    return jnp.stack([first, second], axis=1).reshape((size,) + block.shape)
-
-
-def scatter_rows(partial):
-    size = lax.axis_size("mlp")
-    me = lax.axis_index("mlp")
-    pair, core = me // 2, me % 2
-    pairs = size // 2
-    split = partial.reshape((pairs, 2) + partial.shape[1:])
-    mine = lax.dynamic_index_in_dim(split, core, 1, keepdims=False)
-    other = lax.dynamic_index_in_dim(split, 1 - core, 1, keepdims=False)
+    far = [flipped(piece, "mlp", 1) for piece in near]
+    return near + far
+
+
+def scatter_sum(mine, other):
+    size = lax.axis_size("req")
+    pair = lax.axis_index("mlp") // 2
+    rank = lax.axis_index("req")
     summed = (mine.astype(F32) + flipped(other, "mlp", 1).astype(F32)).astype(BF16)
-    total = lax.dynamic_index_in_dim(summed, pair, 0, keepdims=False).astype(F32)
-    for d in range(1, pairs):
-        piece = lax.dynamic_index_in_dim(summed, pair ^ d, 0, keepdims=False)
-        total = total + flipped(piece, "mlp", 2 * d).astype(F32)
+
+    def block(owner):
+        return lax.dynamic_index_in_dim(summed, (rank - owner) % size, 0, keepdims=False)
+
+    total = block(pair).astype(F32)
+    for d in range(1, size):
+        total = total + flipped(block(pair ^ d), "mlp", 2 * d).astype(F32)
     return total
 
 
-def row_statistics(values):
+def line_scatter(partial):
     size = lax.axis_size("req")
-    width = values.shape[1]
-    part_mean = jnp.mean(values, axis=1)
-    part_square = jnp.sum(jnp.square(values - part_mean[:, None]), axis=1)
-    packed = jnp.stack([part_mean, part_square]).reshape(2, -1, LANES)
-    parts = jnp.stack([packed] + [rotated(packed, "req", d) for d in range(1, size)])
+    rank = lax.axis_index("req")
+
+    def block(owner):
+        return lax.dynamic_index_in_dim(
+            partial, jnp.clip(owner, 0, size - 1), 0, keepdims=False
+        ).astype(F32)
+
+    right = left = None
+    for t in range(1, size):
+        to_right, to_left = block(rank + size - t), block(rank - size + t)
+        if right is not None:
+            to_right, to_left = to_right + right, to_left + left
+        right = lax.ppermute(to_right.astype(BF16), "req", [(k, k + 1) for k in range(t)])
+        left = lax.ppermute(
+            to_left.astype(BF16), "req", [(size - 1 - k, size - 2 - k) for k in range(t)]
+        )
+        right, left = right.astype(F32), left.astype(F32)
+    return block(rank) + right + left
+
+
+def line_gather(block):
+    size = lax.axis_size("req")
+    rights, lefts = [], []
+    right = left = block
+    for t in range(1, size):
+        right = lax.ppermute(right, "req", [(k, k + 1) for k in range(t - 1, size - 1)])
+        left = lax.ppermute(left, "req", [(k + 1, k) for k in range(size - t)])
+        rights.append(right)
+        lefts.append(left)
+    return rights, lefts
+
+
+def eye_mask(rows):
+    shape = (rows, LANES)
+    return lax.broadcasted_iota(jnp.int32, shape, 0) == lax.broadcasted_iota(jnp.int32, shape, 1)
+
+
+def project_kernel(count, steps, place_ref, gain_ref, weight_ref, *refs):
+    pieces, (out, stats, *extra, held) = refs[:count], refs[count:]
+    rows = pieces[0].shape[0]
+    beams = rows // steps
+
+    @pl.when(pl.program_id(0) == 0)
+    def _():
+        eye = eye_mask(rows)
+        pair, core = place_ref[0] // 2, place_ref[0] % 2
+        for k in range(count):
+            d, away = k % (count // 2), k // (count // 2)
+            owner = (pair ^ d) * 2 + (core ^ away)
+            value = pieces[k][...].astype(F32)
+            mean = jnp.mean(value, axis=1, keepdims=True)
+            centred = value - mean
+            square = jnp.sum(centred * centred, axis=1, keepdims=True)
+            for row, column in ((owner, mean), (count + owner, square)):
+                stats[pl.ds(row, 1), :] = jnp.sum(
+                    jnp.where(eye, column, 0.0), axis=0, keepdims=True
+                )
+            at = pl.ds(pl.multiple_of(owner * rows, rows), rows)
+            held[at, :] = (centred * gain_ref[0:1, :]).astype(BF16)
+            if extra:
+                scaled = (centred * gain_ref[1:2, :]).astype(BF16)
+                at = pl.ds(pl.multiple_of(owner * beams, beams), beams)
+                for s in range(steps):
+                    extra[s][at, :] = scaled[s * beams : (s + 1) * beams]
+
+    out[...] = jnp.dot(held[...], weight_ref[...], preferred_element_type=F32).astype(BF16)
+
+
+def project(pieces, gains, weight, steps):
+    count = len(pieces)
+    rows, width = pieces[0].shape
+    columns = weight.shape[1]
+    tile = math.gcd(columns, 256)
+    place = lax.axis_index("mlp").astype(jnp.int32).reshape(1)
+    extra = jax.ShapeDtypeStruct((count * rows // steps, width), BF16)
+    extras = (extra,) * (steps if gains.shape[0] > 1 else 0)
+    stats = jax.ShapeDtypeStruct((2 * count, LANES), F32)
+    return pl.pallas_call(
+        functools.partial(project_kernel, count, steps),
+        out_shape=(jax.ShapeDtypeStruct((count * rows, columns), BF16), stats) + extras,
+        grid=(columns // tile,),
+        in_specs=[
+            pl.BlockSpec(memory_space=pltpu.SMEM),
+            full_block(gains.shape),
+            pl.BlockSpec((width, tile), lambda n: (0, n)),
+        ]
+        + [full_block((rows, width))] * count,
+        out_specs=[pl.BlockSpec((count * rows, tile), lambda n: (0, n)), full_block(stats.shape)]
+        + [full_block(extra.shape)] * len(extras),
+        scratch_shapes=[pltpu.VMEM((count * rows, width), BF16)],
+        compiler_params=pltpu.CompilerParams(vmem_limit_bytes=32 << 20),
+        cost_estimate=pl.CostEstimate(
+            flops=2 * count * rows * width * columns,
+            bytes_accessed=2 * (width * columns + count * rows * (2 * width + columns)),
+            transcendentals=0,
+        ),
+    )(place, gains, weight, *pieces)
+
+
+def exchange(part):
+    return [part] + [rotated(part, "req", d) for d in range(1, lax.axis_size("req"))]
+
+
+def own_statistics(stats, width, rows):
+    size = lax.axis_size("req")
+    count = stats.shape[0] // 2
+    parts = jnp.stack(exchange(stats)).reshape(size, 2, count, LANES)
+    parts = lax.dynamic_slice_in_dim(parts, 2 * lax.axis_index("req"), 2, 2)[..., :rows]
     mean = jnp.mean(parts[:, 0], axis=0)
-    square = jnp.sum(parts[:, 1] + width * jnp.square(parts[:, 0] - mean), axis=0)
-    scale = lax.rsqrt(square / (width * size) + EPSILON)
-    return mean.reshape(-1, 1), scale.reshape(-1, 1)
+    away = parts[:, 0] - mean
+    square = jnp.sum(parts[:, 1] + width * jnp.square(away), axis=0)
+    return away, lax.rsqrt(square / (width * size) + EPSILON)
+
+
+def weight_sums(gain, weight):
+    high = gain.astype(BF16)
+    low = (gain - high.astype(F32)).astype(BF16)
+    rows = jnp.zeros((16, gain.shape[0]), BF16).at[0].set(high).at[1].set(low)
+    both = jnp.dot(rows, weight, preferred_element_type=F32)
+    return both[0] + both[1]
+
+
+def corrected(total, away, scale, sums):
+    for part, columns in zip(away, sums):
+        total = total + part.reshape(-1, 1) * columns[None, :]
+    return total * scale.reshape(-1, 1)
+
+
+def update_kernel(ranks, steps, step, place_ref, down_ref, dense_ref, *refs):
+    attended, refs = refs[:ranks], refs[ranks:]
+    own, rights, lefts = refs[0], refs[1:ranks], refs[ranks : 2 * ranks - 1]
+    mine, other, hidden, heads = refs[2 * ranks - 1 :]
+    rows = own.shape[0]
+    rank, core = place_ref[0], place_ref[1]
+
+    @pl.when(pl.program_id(0) == 0)
+    def _():
+        hidden[0:rows, :] = own[...]
+        for d in range(1, ranks):
+            at = slice(d * rows, (d + 1) * rows)
+
+            @pl.when(rank >= d)
+            def _():
+                hidden[at, :] = rights[d - 1][...]
+
+            @pl.when(rank < d)
+            def _():
+                hidden[at, :] = lefts[ranks - d - 1][...]
+
+        for d in range(ranks):
+            heads[d * rows : (d + 1) * rows, :] = attended[d][step * rows : (step + 1) * rows, :]
+
+    result = jnp.dot(hidden[...], down_ref[...], preferred_element_type=F32) + jnp.dot(
+        heads[...], dense_ref[...], preferred_element_type=F32
+    )
+    half = rows // 2
+    for d in range(ranks):
+        first = result[d * rows : d * rows + half]
+        second = result[d * rows + half : (d + 1) * rows]
+        mine[d] = jnp.where(core == 0, first, second).astype(BF16)
+        other[d] = jnp.where(core == 0, second, first).astype(BF16)
+
+
+def layer_update(step, attended, own, rights, lefts, dense_weight, down_weight):
+    ranks = lax.axis_size("req")
+    rows, hidden = own.shape
+    head_width, width = dense_weight.shape
+    tile = min(256, width)
+    place = jnp.stack([lax.axis_index("req"), lax.axis_index("mlp") % 2]).astype(jnp.int32)
+    shape = jax.ShapeDtypeStruct((ranks, rows // 2, width), BF16)
+    out_block = pl.BlockSpec((ranks, rows // 2, tile), lambda n: (0, 0, n))
+    return pl.pallas_call(
+        functools.partial(update_kernel, ranks, STEPS, step),
+        out_shape=(shape, shape),
+        grid=(width // tile,),
+        in_specs=[
+            pl.BlockSpec(memory_space=pltpu.SMEM),
+            pl.BlockSpec((hidden, tile), lambda n: (0, n)),
+            pl.BlockSpec((head_width, tile), lambda n: (0, n)),
+        ]
+        + [full_block(attended[0].shape)] * ranks
+        + [full_block((rows, hidden))] * (2 * ranks - 1),
+        out_specs=(out_block, out_block),
+        scratch_shapes=[
+            pltpu.VMEM((ranks * rows, hidden), BF16),
+            pltpu.VMEM((ranks * rows, head_width), BF16),
+        ],
+        compiler_params=pltpu.CompilerParams(vmem_limit_bytes=40 << 20),
+        cost_estimate=pl.CostEstimate(
+            flops=2 * ranks * rows * (hidden + head_width) * width,
+            bytes_accessed=2 * (hidden + head_width) * width + 4 * ranks * rows * hidden,
+            transcendentals=0,
+        ),
+    )(place, down_weight, dense_weight, *attended, own, *rights, *lefts)
 
 
 def rotary_tables(positions):
@@ -92,17 +268,22 @@
     return pl.BlockSpec(shape, lambda *_: (0,) * len(shape))
 
 
-def head_split_kernel(heads, parts, requests, x_ref, c_ref, u_ref, l_ref, q_ref, k_ref, v_ref):
+def head_split_kernel(heads, parts, requests, ranks, x_ref, stat_ref, sum_ref, *refs):
+    tables, outs = refs[:3], refs[3:]
     rows = requests * BEAM
+    scale = stat_ref[:, ranks : ranks + 1]
     for head in range(heads):
-        for kind, out in enumerate((q_ref, k_ref, v_ref)):
+        for kind, out in enumerate(outs):
             column = (head * 3 + kind) * HD
             value = x_ref[:, column : column + HD].astype(F32)
+            for d in range(ranks):
+                value = value + stat_ref[:, d : d + 1] * sum_ref[d : d + 1, column : column + HD]
+            value = value * scale
             if kind < 2:
                 value = (
-                    value * c_ref[...]
-                    + pltpu.roll(value, HD - ROT // 2, 1) * u_ref[...]
-                    + pltpu.roll(value, ROT // 2, 1) * l_ref[...]
+                    value * tables[0][...]
+                    + pltpu.roll(value, HD - ROT // 2, 1) * tables[1][...]
+                    + pltpu.roll(value, ROT // 2, 1) * tables[2][...]
                 )
             for part in range(parts):
                 for request in range(requests):
@@ -112,18 +293,21 @@
                     out[at : at + STEPS * BEAM, :] = jnp.concatenate(pair, axis=0).astype(BF16)
 
 
-def head_split(shared, tables, heads, parts, requests):
-    rows = parts * requests * heads * STEPS * BEAM
-    shape = jax.ShapeDtypeStruct((rows, HD), BF16)
+def head_split(shared, away, scale, sums, tables, heads, parts, requests):
+    ranks = len(sums)
+    stats = jnp.concatenate([away.reshape(ranks, -1), scale.reshape(1, -1)]).T
+    stats = jnp.pad(stats, ((0, 0), (0, LANES - ranks - 1)))
+    shape = jax.ShapeDtypeStruct((parts * requests * heads * STEPS * BEAM, HD), BF16)
     return pl.pallas_call(
-        functools.partial(head_split_kernel, heads, parts, requests),
+        functools.partial(head_split_kernel, heads, parts, requests, ranks),
         out_shape=(shape, shape, shape),
         compiler_params=pltpu.CompilerParams(vmem_limit_bytes=32 << 20),
-    )(shared, *tables)
-
-
-def page_kernel(heads, ranks, own_rows, slot_ref, length_ref, me_ref, q_ref, k_ref, v_ref, *rest):
-    outs, (top_ref, sum_ref, out_ref) = rest[:ranks], rest[ranks:]
+    )(shared, stats, jnp.stack(sums), *tables)
+
+
+def page_kernel(heads, ranks, own_rows, slot_ref, length_ref, me_ref, k_ref, v_ref, *rest):
+    queries, outs = rest[:ranks], rest[ranks : 2 * ranks]
+    q_ref, top_ref, sum_ref, out_ref = rest[2 * ranks :]
     step = pl.program_id(0)
     height = heads * STEPS * BEAM
     chunk = STEPS * BEAM
@@ -131,6 +315,9 @@
 
     @pl.when(step == 0)
     def _():
+        for d in range(ranks):
+            rank = lax.rem(me_ref[0] + ranks - d, ranks)
+            q_ref[pl.ds(pl.multiple_of(rank * own_rows, own_rows), own_rows), :] = queries[d][...]
         top_ref[...] = jnp.full(top_ref.shape, NEG_FILL, F32)
         sum_ref[...] = jnp.zeros(sum_ref.shape, F32)
         out_ref[...] = jnp.zeros(out_ref.shape, F32)
@@ -204,8 +391,8 @@
 
 def page_attention(queries, keys, values, slot_table, lengths, heads, ranks):
     slots = keys.shape[0]
-    rows = queries.shape[0]
-    own_rows = rows // ranks
+    own_rows = queries[0].shape[0]
+    rows = own_rows * ranks
     me = lax.axis_index("req").astype(jnp.int32).reshape(1)
     out_rows = own_rows + 3 * STAT_ROWS
     shape = jax.ShapeDtypeStruct((out_rows, LANES), BF16)
@@ -216,9 +403,9 @@
         grid_spec=pltpu.PrefetchScalarGridSpec(
             num_scalar_prefetch=3,
             grid=(slots // GROUP,),
-            in_specs=[full_block((rows, HD)), page_block, page_block],
+            in_specs=[page_block, page_block] + [full_block((own_rows, HD))] * ranks,
             out_specs=[full_block((out_rows, LANES))] * ranks,
-            scratch_shapes=[pltpu.VMEM((rows, LANES), F32)] * 3,
+            scratch_shapes=[pltpu.VMEM((rows, HD), BF16)] + [pltpu.VMEM((rows, LANES), F32)] * 3,
         ),
         compiler_params=pltpu.CompilerParams(vmem_limit_bytes=40 << 20),
         cost_estimate=pl.CostEstimate(
@@ -226,10 +413,10 @@
             bytes_accessed=2 * slots * PAGE * heads * HD * 2,
             transcendentals=slots * PAGE * heads * STEPS * BEAM,
         ),
-    )(slot_table, lengths, me, queries, keys, values)
-
-
-def merge_kernel(heads, ranks, parts, requests, q_ref, k_ref, v_ref, parent_ref, *rest):
+    )(slot_table, lengths, me, keys, values, *queries)
+
+
+def merge_kernel(heads, ranks, requests, q_ref, k_ref, v_ref, parent_ref, *rest):
     pieces, out, work = rest[:ranks], rest[ranks], rest[ranks + 1]
     chunk = STEPS * BEAM
     height = heads * chunk
@@ -282,25 +469,24 @@
             result = result + factor * piece[at, :].astype(F32)
         work[at, :] = result / total
     rows = requests * BEAM
-    for part in range(parts):
-        for request in range(0, requests, 2):
-            for head in range(heads):
-                for s in range(STEPS):
-                    tiles = []
-                    for r in (request, request + 1):
-                        first = (part * requests + r) * height + head * chunk + s * BEAM
-                        tiles.append(work[first : first + BEAM, :])
-                    first = (part * STEPS + s) * rows + request * BEAM
-                    out[first : first + 2 * BEAM, head * HD : (head + 1) * HD] = jnp.concatenate(
-                        tiles, axis=0
-                    ).astype(BF16)
-
-
-def merge(queries, keys, values, parents, pieces, heads, parts, requests):
+    for request in range(0, requests, 2):
+        for head in range(heads):
+            for s in range(STEPS):
+                tiles = []
+                for r in (request, request + 1):
+                    first = r * height + head * chunk + s * BEAM
+                    tiles.append(work[first : first + BEAM, :])
+                first = s * rows + request * BEAM
+                out[first : first + 2 * BEAM, head * HD : (head + 1) * HD] = jnp.concatenate(
+                    tiles, axis=0
+                ).astype(BF16)
+
+
+def merge(queries, keys, values, parents, pieces, heads, requests):
     ranks = len(pieces)
-    rows = parts * requests * STEPS * BEAM
+    rows = requests * STEPS * BEAM
     return pl.pallas_call(
-        functools.partial(merge_kernel, heads, ranks, parts, requests),
+        functools.partial(merge_kernel, heads, ranks, requests),
         out_shape=jax.ShapeDtypeStruct((rows, heads * HD), BF16),
         scratch_shapes=[pltpu.VMEM(queries.shape, F32)],
         compiler_params=pltpu.CompilerParams(vmem_limit_bytes=32 << 20),
@@ -322,14 +508,15 @@
     parents,
 ):
     ranks = lax.axis_size("req")
-    parts = lax.axis_size("mlp") // ranks
     own_count = parents.shape[1]
     beams = inputs.shape[1]
     width = inputs.shape[2]
+    parts = own_count // beams
     requests = beams // BEAM
     own_requests = own_count // BEAM
     heads = dense_weight.shape[0] // HD
     rank = lax.axis_index("req")
+    assert parts == 2 and lax.axis_size("mlp") == 2 * ranks
 
     own_lengths = lax.dynamic_slice_in_dim(lengths, rank * own_requests, own_requests, 0)
     positions = jnp.broadcast_to(
@@ -340,45 +527,65 @@
     tables = rotary_tables(positions)
     parent_wide = jnp.broadcast_to(parents[0][:, None], (own_count, LANES))
 
-    block = inputs.reshape(STEPS * beams, width)
-    with jax.named_scope("gather_inputs"):
-        everything = gather_rows(block).reshape(-1, width).astype(F32)
-    with jax.named_scope("norm"):
-        mean, scale = row_statistics(everything)
-        normed = (everything - mean) * scale
-        attn_in = (normed * norm_gains[0]).astype(BF16)
-        mlp_in = (normed * norm_gains[1]).astype(BF16)
+    with jax.named_scope("inputs_gather"):
+        pieces = gather_pieces(inputs.reshape(STEPS * beams, width))
+    with jax.named_scope("weight_sums"):
+        weights = (attn_weight, up_weight, next_weight)
+        sums = jnp.concatenate([weight_sums(norm_gains[k], w) for k, w in enumerate(weights)])
+        sums = [part.reshape(-1) for part in exchange(sums.reshape(-1, LANES))]
+        cuts = (0, weights[0].shape[1], weights[0].shape[1] + weights[1].shape[1], sums[0].shape[0])
+        sums = [[part[a:b] for part in sums] for a, b in zip(cuts, cuts[1:])]
     with jax.named_scope("qkv"):
-        mixed = jnp.dot(attn_in, attn_weight, preferred_element_type=F32).astype(BF16)
-        mixed = lax.psum_scatter(mixed, "req", scatter_dimension=0, tiled=True)
+        partial, stats, *mlp_in = project(pieces, norm_gains[:2], attn_weight, STEPS)
+        mixed = lax.psum_scatter(partial, "req", scatter_dimension=0, tiled=True)
+    with jax.named_scope("statistics"):
+        away, scale = own_statistics(stats, width, STEPS * beams)
     with jax.named_scope("up"):
-        hidden = jnp.dot(mlp_in, up_weight, preferred_element_type=F32).astype(BF16)
-        hidden = lax.psum_scatter(hidden, "req", scatter_dimension=0, tiled=True).astype(F32)
-        activated = jax.nn.gelu(hidden, approximate=False).astype(BF16)
-        activated = lax.all_gather(activated, "req", axis=0, tiled=True)
+        hiddens = []
+        for s in range(STEPS):
+            partial = jnp.dot(mlp_in[s], up_weight, preferred_element_type=F32).astype(BF16)
+            partial, away, scale, sums = lax.optimization_barrier((partial, away, scale, sums))
+            hiddens.append(lax.psum_scatter(partial, "req", scatter_dimension=0, tiled=True))
+
+    def activate(s, hidden):
+        at = slice(s * beams, (s + 1) * beams)
+        with jax.named_scope("gelu"):
+            hidden = corrected(hidden.astype(F32), away[..., at], scale[:, at], sums[1])
+            own = jax.nn.gelu(hidden, approximate=False).astype(BF16)
+        with jax.named_scope("activated_gather"):
+            return (own,) + line_gather(own)
+
     with jax.named_scope("attention"):
-        queries, keys, values = head_split(mixed, tables, heads, parts, requests)
-        queries_all = lax.all_gather(queries, "req", axis=0, tiled=True)
+        queries, keys, values = head_split(
+            mixed, away, scale, sums[0], tables, heads, parts, requests
+        )
+        queries_all = exchange(queries)
         pieces = page_attention(
             queries_all, cache_keys, cache_values, slot_table, lengths, heads, ranks
         )
+    hiddens[0], pieces = lax.optimization_barrier((hiddens[0], pieces))
+    activated = [activate(0, hiddens[0])]
+    with jax.named_scope("attention"):
         pieces = [pieces[0]] + [rotated(pieces[d], "req", d) for d in range(1, ranks)]
-        attended = merge(queries, keys, values, parent_wide, pieces, heads, parts, requests)
-        attended = lax.all_gather(attended, "req", axis=0, tiled=True)
-    with jax.named_scope("down"):
-        update = jnp.dot(attended, dense_weight, preferred_element_type=F32) + jnp.dot(
-            activated, down_weight, preferred_element_type=F32
-        )
-        update = scatter_rows(update.astype(BF16).reshape(-1, STEPS * beams, width))
-        layer = (block.astype(F32) + update).astype(BF16)
-    with jax.named_scope("next"):
-        everything = gather_rows(layer).reshape(-1, width).astype(F32)
-        mean, scale = row_statistics(everything)
-        next_in = ((everything - mean) * scale * norm_gains[2]).astype(BF16)
-        following = jnp.dot(next_in, next_weight, preferred_element_type=F32).astype(BF16)
-        following = lax.psum_scatter(following, "req", scatter_dimension=0, tiled=True)
-        following = following.reshape(parts, STEPS, beams, -1).transpose(1, 0, 2, 3)
-    return layer.reshape(STEPS, beams, width), following.reshape(STEPS, own_count, -1)
+        attended = merge(queries, keys, values, parent_wide, pieces, heads, own_requests)
+        attended = exchange(attended)
+    hiddens[1], first = lax.optimization_barrier((hiddens[1], activated[0][1][0]))
+    activated[0][1][0] = first
+    activated.append(activate(1, hiddens[1]))
+    layers, followings = [], []
+    for s in range(STEPS):
+        with jax.named_scope(f"down_{s}"):
+            mine, other = layer_update(s, attended, *activated[s], dense_weight, down_weight)
+            layer = (inputs[s].astype(F32) + scatter_sum(mine, other)).astype(BF16)
+            if s + 1 < STEPS:
+                activated[s + 1], layer = lax.optimization_barrier((activated[s + 1], layer))
+            layers.append(layer)
+        with jax.named_scope(f"next_{s}"):
+            partial, stats = project(gather_pieces(layer), norm_gains[2:], next_weight, 1)
+            total = lax.psum_scatter(partial, "req", scatter_dimension=0, tiled=True).astype(F32)
+            away, scale = own_statistics(stats, width, beams)
+            followings.append(corrected(total, away, scale, sums[2]).astype(BF16))
+    return jnp.stack(layers), jnp.stack(followings)
 
 
 def solution(mesh):

time: 372 us -> 348 us (0.935)
  starting transfers between devices: 26.3 us -> 91.7 us
  waiting for transfers between devices: 203 us -> 140 us
  blocking collectives: 50.1 us -> 0 us
  Pallas kernels: 22.3 us -> 49.5 us
  matrix products: 21.1 us -> 14.2 us
  local copies, waits for them, and re-layouts: 17.3 us -> 23.9 us
  other arithmetic: 17 us -> 12.9 us
    reduce_scatter x3 -> x5, waiting for transfers between devices: 147 us -> 35.2 us  [the longest x1 18.6 us: shards(): mixed = lax.psum_scatter(partial, 'req', scatter_dimension=0, tiled=True)]
    all_gather x2 -> x0, blocking collectives: 50.1 us -> none  [the longest x1 27.2 us: shards(): attended = lax.all_gather(attended, 'req', axis=0, tiled=True)]
    ppermute x0 -> x12, starting transfers between devices: none -> 37.7 us  [the longest x6 29.8 us: line_gather(): lax.ppermute(right, 'req', [(k, k + 1) for k in range(t - 1, size - 1)])]
    ppermute x9 -> x21, waiting for transfers between devices: 25.5 us -> 61.8 us  [rotated(): lax.ppermute(array, axis, [(k, (k + distance) % size) for k in range(size)])]
    pallas_call x1 -> x6, Pallas kernels: 1.11 us -> 25.8 us  [the longest x3 13.9 us: project(): pl.pallas_call(functools.partial(project_kernel, count, steps), out_shape...]
    ppermute x9 -> x21, starting transfers between devices: 14.3 us -> 34.3 us  [rotated(): lax.ppermute(array, axis, [(k, (k + distance) % size) for k in range(size)])]
    ppermute x0 -> x12, waiting for transfers between devices: none -> 12 us  [the longest x6 11.9 us: line_gather(): left = lax.ppermute(left, 'req', [(k + 1, k) for k in range(size - t)])]
    unnamed x37 -> x48, local copies, waits for them, and re-layouts: 7.41 us -> 18.9 us
  transfers between devices with their start and end apart: 25 -> 67, of which waited for: 15 -> 33; matrix products, arithmetic and copies ran while one was open for 5% -> 9% of each run, Pallas kernels for 6% -> 12%
where the time goes in v2:
time: 348 us; the launch traced here: 347 us
  waiting for transfers between devices  140 us (40%)
  starting transfers between devices  91.7 us (26%)
  Pallas kernels  49.5 us (14%)
  local copies, waits for them, and re-layouts  23.9 us (7%)
  between operations  14.4 us (4%)
  matrix products  14.2 us (4%)
  other arithmetic  12.9 us (4%)
    ppermute x21, waiting for transfers between devices, rotated(): lax.ppermute(array, axis, [(k, (k + distance) % size) for k in range(size)])  61.8 us
    ppermute x21, starting transfers between devices, rotated(): lax.ppermute(array, axis, [(k, (k + distance) % size) for k in range(size)])  34.3 us
    ppermute x29, waiting for transfers between devices, flipped(): lax.ppermute(array, axis, [(k, k ^ bits) for k in range(lax.axis_size(axi...  31.3 us
    ppermute x6, starting transfers between devices, line_gather(): lax.ppermute(right, 'req', [(k, k + 1) for k in range(t - 1, size - 1)])  29.8 us
    pallas_call x1, Pallas kernels, page_attention(): pl.pallas_call(functools.partial(page_kernel, heads, ranks, own_rows), ou...  21.6 us
    ppermute x29, starting transfers between devices, flipped(): lax.ppermute(array, axis, [(k, k ^ bits) for k in range(lax.axis_size(axi...  19.5 us
    unnamed x48, local copies, waits for them, and re-layouts  18.9 us
    reduce_scatter x1, waiting for transfers between devices, shards(): mixed = lax.psum_scatter(partial, 'req', scatter_dimension=0, tiled=True)  18.6 us
  transfers between devices with their start and end apart: 67, of which 33 were waited for; matrix products, arithmetic and copies ran while one was open for 9% of the time, Pallas kernels for 12%

profile of v2, /device:TPU:0, one launch (start us, length us, event | category | flops | bytes accessed | tf_op | source)
XLA Modules:
  0.0 347.0 jit_solution(14899149462884467514)
XLA Ops:
  7.2 3.0 collective-permute-start
  12.5 3.7 %collective-permute-done.refs_1_ = bf16[96,1024]{1,0:T(8,128)(2,1)S(1)} collective-permute-done((bf16[96,1024]{1,0:T(8,128)(2,1)}, bf16[96,1024]{1,0:T(8,128)(2,1)S(1)}, u32[]{:S(2)}, u32[]{:S(2)}) %collective-permute-start) | collective-permute-done | bytes 196640 | tf_op jit(solution)/shard_map/inputs_gather/ppermute | solution.py:32
  16.2 4.8 %collective-permute-done.1.refs_2_ = bf16[96,1024]{1,0:T(8,128)(2,1)S(1)} collective-permute-done((bf16[96,1024]{1,0:T(8,128)(2,1)}, bf16[96,1024]{1,0:T(8,128)(2,1)S(1)}, u32[]{:S(2)}, u32[]{:S(2)}) %collective-permute-start.1) | collective-permute-done | bytes 196640 | tf_op jit(solution)/shard_map/inputs_gather/ppermute | solution.py:32
  25.5 5.1 %qkv.1 = (bf16[768,1536]{1,0:T(8,128)(2,1)S(1)}, f32[16,128]{1,0:T(8,128)S(1)}, bf16[384,1024]{1,0:T(8,128)(2,1)S(1)}, bf16[384,1024]{1,0:T(8,128)(2,1)S(1)}) custom-call(s32[1]{0:T(128)} %bitcast.place_ref, f32[2,1024]{1,0:T(2,128)S(1)} %slice.225.gain_ref, bf16[1024,1536]{1,0:T(8,128)(2,1)S(1)} %copy-done.4, bf16[96,1024]{1,0:T(8,128)(2,1)S(1)} %bitcast.136, ...), custom_call_target="tpu_custom_call" | custom-call | flops 2415919104 | bytes 8650752 | tf_op jit(solution)/shard_map/qkv/pallas_call | solution.py:136
  34.2 2.6 fusion.62
  38.7 3.7 %collective-permute-start.12 = (f32[40,128]{1,0:T(8,128)S(1)}, f32[40,128]{1,0:T(8,128)S(1)}, u32[]{:S(2)}, u32[]{:S(2)}) collective-permute-start(f32[40,128]{1,0:T(8,128)S(1)} %maximum_bitcast_fusion), channel_id=1, source_target_pairs={{0,24},{8,0},{16,8},{24,16},{1,25},{9,1},{17,9},{25,17},{2,26},{10... | collective-permute-start | bytes 61448 | tf_op jit(solution)/shard_map/weight_sums/ppermute | solution.py:28
  44.3 3.4 collective-permute-done.11
  52.6 5.3 %convolution_convert_fusion = bf16[384,2048]{1,0:T(8,128)(2,1)} fusion(bf16[384,1024]{1,0:T(8,128)(2,1)S(1)} %copy-done.18, bf16[1024,2048]{1,0:T(8,128)(2,1)} %param.27), kind=kOutput, calls=%fused_computation | convolution fusion | flops 1611399168 | bytes 6553600 | tf_op jit(solution)/shard_map/up/dot_general | solution.py:546
  58.0 5.2 %convolution_convert_fusion.1 = bf16[384,2048]{1,0:T(8,128)(2,1)} fusion(bf16[384,1024]{1,0:T(8,128)(2,1)S(1)} %copy-done.16, bf16[1024,2048]{1,0:T(8,128)(2,1)} %param.27), kind=kOutput, calls=%fused_computation.1 | convolution fusion | flops 1611399168 | bytes 6553600 | tf_op jit(solution)/shard_map/up/dot_general | solution.py:546
  65.0 18.6 %reduce-scatter.10.cloned.1.call-done.x_ref = bf16[192,1536]{1,0:T(8,128)(2,1)} async-done(((bf16[768,1536]{1,0:T(8,128)(2,1)}), bf16[192,1536]{1,0:T(8,128)(2,1)}) %reduce-scatter.10.cloned.1.call-update) | async-done | bytes 589840 | tf_op jit(solution)/shard_map/qkv/reduce_scatter | solution.py:540
  92.0 5.2 %collective-permute-done.13.rest_1_ = bf16[768,128]{1,0:T(8,128)(2,1)S(1)} collective-permute-done((bf16[768,128]{1,0:T(8,128)(2,1)S(1)}, bf16[768,128]{1,0:T(8,128)(2,1)S(1)}, u32[]{:S(2)}, u32[]{:S(2)}) %collective-permute-start.13) | collective-permute-done | bytes 196640 | tf_op jit(solution)/shard_map/attention/ppermute | solution.py:28
  97.1 16.4 %collective-permute-done.14.rest_2_ = bf16[768,128]{1,0:T(8,128)(2,1)S(1)} collective-permute-done((bf16[768,128]{1,0:T(8,128)(2,1)S(1)}, bf16[768,128]{1,0:T(8,128)(2,1)S(1)}, u32[]{:S(2)}, u32[]{:S(2)}) %collective-permute-start.14) | collective-permute-done | bytes 196640 | tf_op jit(solution)/shard_map/attention/ppermute | solution.py:28
  113.5 3.4 copy-done.2
  117.0 21.6 %attention.4 = (bf16[816,128]{1,0:T(8,128)(2,1)S(1)}, bf16[816,128]{1,0:T(8,128)(2,1)}, bf16[816,128]{1,0:T(8,128)(2,1)}, bf16[816,128]{1,0:T(8,128)(2,1)S(1)}) custom-call(s32[2,64]{1,0:T(2,128)S(1)} %copy-done.13, s32[48]{0:T(128)S(1)} %copy-done.14, s32[1]{0:T(128)} %bitcast.23.me_ref, bf16[64,128,512]{2,1,0:T(8,128)(2,1)S(1)} %copy-done.2, ...), custom_call_target="tpu_custom_call" | custom-call | flops 268435456 | bytes 16777216 | tf_op jit(solution)/shard_map/attention/pallas_call | solution.py:400
  138.6 3.2 fusion.2.refs_4_
  141.8 18.9 %collective-permute-start.16 = (bf16[96,2048]{1,0:T(8,128)(2,1)S(1)}, bf16[96,2048]{1,0:T(8,128)(2,1)}, u32[]{:S(2)}, u32[]{:S(2)}) collective-permute-start(bf16[96,2048]{1,0:T(8,128)(2,1)S(1)} %fusion.2.refs_4_), channel_id=1, source_target_pairs={{0,8},{8,16},{16,24},{1,9},{9,17},{17,25},{2,10},{10,18},{18,26},{... | collective-permute-start | bytes 1179656 | tf_op jit(solution)/shard_map/activated_gather/ppermute | solution.py:84
  162.0 2.7 collective-permute-start.23
  167.5 15.5 %collective-permute-done.23.rest_1_ = bf16[816,128]{1,0:T(8,128)(2,1)S(1)} collective-permute-done((bf16[816,128]{1,0:T(8,128)(2,1)}, bf16[816,128]{1,0:T(8,128)(2,1)S(1)}, u32[]{:S(2)}, u32[]{:S(2)}) %collective-permute-start.23) | collective-permute-done | bytes 208928 | tf_op jit(solution)/shard_map/attention/ppermute | solution.py:28
  183.0 7.5 %collective-permute-done.24.rest_2_ = bf16[816,128]{1,0:T(8,128)(2,1)S(1)} collective-permute-done((bf16[816,128]{1,0:T(8,128)(2,1)}, bf16[816,128]{1,0:T(8,128)(2,1)S(1)}, u32[]{:S(2)}, u32[]{:S(2)}) %collective-permute-start.24) | collective-permute-done | bytes 208928 | tf_op jit(solution)/shard_map/attention/ppermute | solution.py:28
  191.8 4.9 %collective-permute-start.26 = (bf16[192,512]{1,0:T(8,128)(2,1)S(1)}, bf16[192,512]{1,0:T(8,128)(2,1)S(1)}, u32[]{:S(2)}, u32[]{:S(2)}) collective-permute-start(bf16[192,512]{1,0:T(8,128)(2,1)S(1)} %attention.5.refs_0_), channel_id=1, source_target_pairs={{0,8},{8,16},{16,24},{24,0},{1,9},{9,17},{17,25},{25,1},{2,10},{10... | collective-permute-start | bytes 589832 | tf_op jit(solution)/shard_map/attention/ppermute | solution.py:28
  200.8 3.1 fusion.5.refs_4_
  203.9 5.9 %collective-permute-start.17 = (bf16[96,2048]{1,0:T(8,128)(2,1)S(1)}, bf16[96,2048]{1,0:T(8,128)(2,1)S(1)}, u32[]{:S(2)}, u32[]{:S(2)}) collective-permute-start(bf16[96,2048]{1,0:T(8,128)(2,1)S(1)} %fusion.5.refs_4_), channel_id=1, source_target_pairs={{0,8},{8,16},{16,24},{1,9},{9,17},{17,25},{2,10},{10,18},{18,26},{... | collective-permute-start | bytes 1179656 | tf_op jit(solution)/shard_map/activated_gather/ppermute | solution.py:84
  212.6 6.6 %collective-permute-done.32.refs_9_ = bf16[96,2048]{1,0:T(8,128)(2,1)} collective-permute-done((bf16[96,2048]{1,0:T(8,128)(2,1)}, bf16[96,2048]{1,0:T(8,128)(2,1)}, u32[]{:S(2)}, u32[]{:S(2)}) %collective-permute-start.32) | collective-permute-done | bytes 393248 | tf_op jit(solution)/shard_map/activated_gather/ppermute | solution.py:85
  222.2 5.3 %collective-permute-done.20.refs_8_ = bf16[96,2048]{1,0:T(8,128)(2,1)S(1)} collective-permute-done((bf16[96,2048]{1,0:T(8,128)(2,1)S(1)}, bf16[96,2048]{1,0:T(8,128)(2,1)S(1)}, u32[]{:S(2)}, u32[]{:S(2)}) %collective-permute-start.20) | collective-permute-done | bytes 393248 | tf_op jit(solution)/shard_map/activated_gather/ppermute | solution.py:85
  228.8 10.4 %collective-permute-done.28.refs_3_ = bf16[192,512]{1,0:T(8,128)(2,1)S(1)} collective-permute-done((bf16[192,512]{1,0:T(8,128)(2,1)S(1)}, bf16[192,512]{1,0:T(8,128)(2,1)S(1)}, u32[]{:S(2)}, u32[]{:S(2)}) %collective-permute-start.28) | collective-permute-done | bytes 196640 | tf_op jit(solution)/shard_map/attention/ppermute | solution.py:28
  241.4 5.8 %down_0.1 = (bf16[4,48,1024]{2,1,0:T(8,128)(2,1)S(1)}, bf16[4,48,1024]{2,1,0:T(8,128)(2,1)}) custom-call(s32[2]{0:T(128)S(1)} %pad_add_fusion.place_ref, bf16[2048,1024]{1,0:T(8,128)(2,1)S(1)} %copy-done, bf16[512,1024]{1,0:T(8,128)(2,1)S(1)} %copy-done.3, bf16[192,512]{1,0:T(8,128)(2,1)S(1)} %attention.5.refs_0_, ...), custom_call_target="tpu_custom_call" | custom-call | flops 2013265920 | bytes 8388608 | tf_op jit(solution)/shard_map/down_0/pallas_call | solution.py:230
  274.0 4.4 %next_0.1 = (bf16[384,1536]{1,0:T(8,128)(2,1)}, f32[16,128]{1,0:T(8,128)S(1)}) custom-call(s32[1]{0:T(128)} %bitcast.place_ref, f32[1,1024]{1,0:T(1,128)S(1)} %get-tuple-element.222.gain_ref, bf16[1024,1536]{1,0:T(8,128)(2,1)S(1)} %copy-done.6, bf16[48,1024]{1,0:T(8,128)(2,1)S(1)} %fusion.29.refs_0_, bf16[48,1024]{1,0:T(8,128)(2,1)S(1)} %collective-permute-done.42.refs_1_, ...), custom_call_target="tpu_custom_call" | custom-call | flops 1207959552 | bytes 5898240 | tf_op jit(solution)/shard_map/next_0/pallas_call | solution.py:136
  280.6 5.0 %down_1.1 = (bf16[4,48,1024]{2,1,0:T(8,128)(2,1)S(1)}, bf16[4,48,1024]{2,1,0:T(8,128)(2,1)S(1)}) custom-call(s32[2]{0:T(128)S(1)} %pad_add_fusion.place_ref, bf16[2048,1024]{1,0:T(8,128)(2,1)S(1)} %copy-done.1, bf16[512,1024]{1,0:T(8,128)(2,1)S(1)} %copy-done.3, bf16[192,512]{1,0:T(8,128)(2,1)S(1)} %attention.5.refs_0_, ...), custom_call_target="tpu_custom_call" | custom-call | flops 2013265920 | bytes 8388608 | tf_op jit(solution)/shard_map/down_1/pallas_call | solution.py:230
  304.7 4.3 %next_1.1 = (bf16[384,1536]{1,0:T(8,128)(2,1)}, f32[16,128]{1,0:T(8,128)S(1)}) custom-call(s32[1]{0:T(128)} %bitcast.place_ref, f32[1,1024]{1,0:T(1,128)S(1)} %get-tuple-element.222.gain_ref, bf16[1024,1536]{1,0:T(8,128)(2,1)S(1)} %copy-done.7, bf16[48,1024]{1,0:T(8,128)(2,1)S(1)} %fusion.25.refs_0_, bf16[48,1024]{1,0:T(8,128)(2,1)S(1)} %collective-permute-done.52.refs_1_, ...), custom_call_target="tpu_custom_call" | custom-call | flops 1207959552 | bytes 5898240 | tf_op jit(solution)/shard_map/next_1/pallas_call | solution.py:136
  311.5 2.4 collective-permute-start.51
  313.9 2.5 collective-permute-start.60
  321.4 16.6 %reduce-scatter.14.cloned.1.call-done = bf16[96,1536]{1,0:T(8,128)(2,1)} async-done(((bf16[384,1536]{1,0:T(8,128)(2,1)}), bf16[96,1536]{1,0:T(8,128)(2,1)}) %reduce-scatter.14.cloned.1.call-update) | async-done | bytes 294928 | tf_op jit(solution)/shard_map/next_1/reduce_scatter | solution.py:585
  (258 shorter events, 105.5 us)
Async XLA Ops:
  7.2 76.4 %reduce-scatter.10.cloned.1.call-start = ((), (), s32[]{:S(2)}) async-start(), calls=%async_computation.7 | async-start | bytes 2949120 | tf_op jit(solution)/shard_map/qkv/reduce_scatter | solution.py:540
  7.2 8.9 %collective-permute-start = (bf16[96,1024]{1,0:T(8,128)(2,1)}, bf16[96,1024]{1,0:T(8,128)(2,1)S(1)}, u32[]{:S(2)}, u32[]{:S(2)}) collective-permute-start(bf16[96,1024]{1,0:T(8,128)(2,1)} %bitcast.132), channel_id=1, source_target_pairs={{0,2},{1,3},{2,0},{3,1},{4,6},{5,7},{6,4},{7,5},{8,10},{9,11},{10,... | collective-permute-start | bytes 589832 | tf_op jit(solution)/shard_map/inputs_gather/ppermute | solution.py:32
  10.2 10.8 %collective-permute-start.1 = (bf16[96,1024]{1,0:T(8,128)(2,1)}, bf16[96,1024]{1,0:T(8,128)(2,1)S(1)}, u32[]{:S(2)}, u32[]{:S(2)}) collective-permute-start(bf16[96,1024]{1,0:T(8,128)(2,1)} %bitcast.133), channel_id=1, source_target_pairs={{0,4},{1,5},{2,6},{3,7},{4,0},{5,1},{6,2},{7,3},{8,12},{9,13},{10,... | collective-permute-start | bytes 589832 | tf_op jit(solution)/shard_map/inputs_gather/ppermute | solution.py:32
  11.7 9.3 %collective-permute-start.2 = (bf16[96,1024]{1,0:T(8,128)(2,1)}, bf16[96,1024]{1,0:T(8,128)(2,1)S(1)}, u32[]{:S(2)}, u32[]{:S(2)}) collective-permute-start(bf16[96,1024]{1,0:T(8,128)(2,1)} %bitcast.134), channel_id=1, source_target_pairs={{0,6},{1,7},{2,4},{3,5},{4,2},{5,3},{6,0},{7,1},{8,14},{9,15},{10,... | collective-permute-start | bytes 589832 | tf_op jit(solution)/shard_map/inputs_gather/ppermute | solution.py:32
  11.8 10.7 %collective-permute-start.3 = (bf16[96,1024]{1,0:T(8,128)(2,1)}, bf16[96,1024]{1,0:T(8,128)(2,1)S(1)}, u32[]{:S(2)}, u32[]{:S(2)}) collective-permute-start(bf16[96,1024]{1,0:T(8,128)(2,1)} %bitcast.135), channel_id=1, source_target_pairs={{0,1},{1,0},{2,3},{3,2},{4,5},{5,4},{6,7},{7,6},{8,9},{9,8},{10,11... | collective-permute-start | bytes 589832 | tf_op jit(solution)/shard_map/inputs_gather/ppermute | solution.py:32
  33.9 104.7 %reduce-scatter.8.cloned.1.call-start = ((), (), s32[]{:S(2)}) async-start(), calls=%async_computation.6 | async-start | bytes 1966080 | tf_op jit(solution)/shard_map/up/reduce_scatter | solution.py:548
  48.4 9.4 %collective-permute-start.7 = (f32[16,128]{1,0:T(8,128)S(1)}, f32[16,128]{1,0:T(8,128)S(1)}, u32[]{:S(2)}, u32[]{:S(2)}) collective-permute-start(f32[16,128]{1,0:T(8,128)S(1)} %get-tuple-element.140), channel_id=1, source_target_pairs={{0,8},{8,16},{16,24},{24,0},{1,9},{9,17},{17,25},{25,1},{2,10},{10... | collective-permute-start | bytes 24584 | tf_op jit(solution)/shard_map/statistics/ppermute | solution.py:28
  48.5 9.3 %collective-permute-start.8 = (f32[16,128]{1,0:T(8,128)S(1)}, f32[16,128]{1,0:T(8,128)S(1)}, u32[]{:S(2)}, u32[]{:S(2)}) collective-permute-start(f32[16,128]{1,0:T(8,128)S(1)} %get-tuple-element.140), channel_id=1, source_target_pairs={{0,16},{8,24},{16,0},{24,8},{1,17},{9,25},{17,1},{25,9},{2,18},{10... | collective-permute-start | bytes 24584 | tf_op jit(solution)/shard_map/statistics/ppermute | solution.py:28
  58.0 140.1 %reduce-scatter.6.cloned.1.call-start = ((), (), s32[]{:S(2)}) async-start(), calls=%async_computation.5 | async-start | bytes 1966080 | tf_op jit(solution)/shard_map/up/reduce_scatter | solution.py:548
  63.2 258.2 %reduce-scatter.12.cloned.1.call-start = ((), (), s32[]{:S(2)}) async-start(), calls=%async_computation.8 | async-start | bytes 1474560 | tf_op jit(solution)/shard_map/next_0/reduce_scatter | solution.py:585
  86.8 10.4 %collective-permute-start.13 = (bf16[768,128]{1,0:T(8,128)(2,1)S(1)}, bf16[768,128]{1,0:T(8,128)(2,1)S(1)}, u32[]{:S(2)}, u32[]{:S(2)}) collective-permute-start(bf16[768,128]{1,0:T(8,128)(2,1)S(1)} %get-tuple-element.164.rest_0_.q_ref), channel_id=1, source_target_pairs={{0,8},{8,16},{16,24},{24,0},{1,9},{9,17},{17,25},{25,1},{2,10},{10... | collective-permute-start | bytes 589832 | tf_op jit(solution)/shard_map/attention/ppermute | solution.py:28
  88.4 25.1 %collective-permute-start.14 = (bf16[768,128]{1,0:T(8,128)(2,1)S(1)}, bf16[768,128]{1,0:T(8,128)(2,1)S(1)}, u32[]{:S(2)}, u32[]{:S(2)}) collective-permute-start(bf16[768,128]{1,0:T(8,128)(2,1)S(1)} %get-tuple-element.164.rest_0_.q_ref), channel_id=1, source_target_pairs={{0,16},{8,24},{16,0},{24,8},{1,17},{9,25},{17,1},{25,9},{2,18},{10... | collective-permute-start | bytes 589832 | tf_op jit(solution)/shard_map/attention/ppermute | solution.py:28
  89.7 23.8 %collective-permute-start.15 = (bf16[768,128]{1,0:T(8,128)(2,1)S(1)}, bf16[768,128]{1,0:T(8,128)(2,1)S(1)}, u32[]{:S(2)}, u32[]{:S(2)}) collective-permute-start(bf16[768,128]{1,0:T(8,128)(2,1)S(1)} %get-tuple-element.164.rest_0_.q_ref), channel_id=1, source_target_pairs={{0,24},{8,0},{16,8},{24,16},{1,25},{9,1},{17,9},{25,17},{2,26},{10... | collective-permute-start | bytes 589832 | tf_op jit(solution)/shard_map/attention/ppermute | solution.py:28
  141.8 56.3 %collective-permute-start.16 = (bf16[96,2048]{1,0:T(8,128)(2,1)S(1)}, bf16[96,2048]{1,0:T(8,128)(2,1)}, u32[]{:S(2)}, u32[]{:S(2)}) collective-permute-start(bf16[96,2048]{1,0:T(8,128)(2,1)S(1)} %fusion.2.refs_4_), channel_id=1, source_target_pairs={{0,8},{8,16},{16,24},{1,9},{9,17},{17,25},{2,10},{10,18},{18,26},{... | collective-permute-start | bytes 1179656 | tf_op jit(solution)/shard_map/activated_gather/ppermute | solution.py:84
  160.7 38.8 %collective-permute-start.31 = (bf16[96,2048]{1,0:T(8,128)(2,1)S(1)}, bf16[96,2048]{1,0:T(8,128)(2,1)}, u32[]{:S(2)}, u32[]{:S(2)}) collective-permute-start(bf16[96,2048]{1,0:T(8,128)(2,1)S(1)} %fusion.2.refs_4_), channel_id=1, source_target_pairs={{8,0},{16,8},{24,16},{9,1},{17,9},{25,17},{10,2},{18,10},{26,18},{... | collective-permute-start | bytes 1179656 | tf_op jit(solution)/shard_map/activated_gather/ppermute | solution.py:85
  162.0 21.1 %collective-permute-start.23 = (bf16[816,128]{1,0:T(8,128)(2,1)}, bf16[816,128]{1,0:T(8,128)(2,1)S(1)}, u32[]{:S(2)}, u32[]{:S(2)}) collective-permute-start(bf16[816,128]{1,0:T(8,128)(2,1)} %get-tuple-element.178), channel_id=1, source_target_pairs={{0,8},{8,16},{16,24},{24,0},{1,9},{9,17},{17,25},{25,1},{2,10},{10... | collective-permute-start | bytes 626696 | tf_op jit(solution)/shard_map/attention/ppermute | solution.py:28
  164.7 25.9 %collective-permute-start.24 = (bf16[816,128]{1,0:T(8,128)(2,1)}, bf16[816,128]{1,0:T(8,128)(2,1)S(1)}, u32[]{:S(2)}, u32[]{:S(2)}) collective-permute-start(bf16[816,128]{1,0:T(8,128)(2,1)} %get-tuple-element.179), channel_id=1, source_target_pairs={{0,16},{8,24},{16,0},{24,8},{1,17},{9,25},{17,1},{25,9},{2,18},{10... | collective-permute-start | bytes 626696 | tf_op jit(solution)/shard_map/attention/ppermute | solution.py:28
  164.7 25.9 %collective-permute-start.25 = (bf16[816,128]{1,0:T(8,128)(2,1)S(1)}, bf16[816,128]{1,0:T(8,128)(2,1)S(1)}, u32[]{:S(2)}, u32[]{:S(2)}) collective-permute-start(bf16[816,128]{1,0:T(8,128)(2,1)S(1)} %get-tuple-element.180), channel_id=1, source_target_pairs={{0,24},{8,0},{16,8},{24,16},{1,25},{9,1},{17,9},{25,17},{2,26},{10... | collective-permute-start | bytes 626696 | tf_op jit(solution)/shard_map/attention/ppermute | solution.py:28
  191.8 18.1 %collective-permute-start.26 = (bf16[192,512]{1,0:T(8,128)(2,1)S(1)}, bf16[192,512]{1,0:T(8,128)(2,1)S(1)}, u32[]{:S(2)}, u32[]{:S(2)}) collective-permute-start(bf16[192,512]{1,0:T(8,128)(2,1)S(1)} %attention.5.refs_0_), channel_id=1, source_target_pairs={{0,8},{8,16},{16,24},{24,0},{1,9},{9,17},{17,25},{25,1},{2,10},{10... | collective-permute-start | bytes 589832 | tf_op jit(solution)/shard_map/attention/ppermute | solution.py:28
  196.7 23.8 %collective-permute-start.27 = (bf16[192,512]{1,0:T(8,128)(2,1)S(1)}, bf16[192,512]{1,0:T(8,128)(2,1)S(1)}, u32[]{:S(2)}, u32[]{:S(2)}) collective-permute-start(bf16[192,512]{1,0:T(8,128)(2,1)S(1)} %attention.5.refs_0_), channel_id=1, source_target_pairs={{0,16},{8,24},{16,0},{24,8},{1,17},{9,25},{17,1},{25,9},{2,18},{10... | collective-permute-start | bytes 589832 | tf_op jit(solution)/shard_map/attention/ppermute | solution.py:28
  198.1 13.1 %collective-permute-start.29 = (bf16[96,2048]{1,0:T(8,128)(2,1)}, bf16[96,2048]{1,0:T(8,128)(2,1)}, u32[]{:S(2)}, u32[]{:S(2)}) collective-permute-start(bf16[96,2048]{1,0:T(8,128)(2,1)} %collective-permute-done.16.refs_5_), channel_id=1, source_target_pairs={{8,16},{16,24},{9,17},{17,25},{10,18},{18,26},{11,19},{19,27},{12,... | collective-permute-start | bytes 1179656 | tf_op jit(solution)/shard_map/activated_gather/ppermute | solution.py:84
  199.5 19.7 %collective-permute-start.32 = (bf16[96,2048]{1,0:T(8,128)(2,1)}, bf16[96,2048]{1,0:T(8,128)(2,1)}, u32[]{:S(2)}, u32[]{:S(2)}) collective-permute-start(bf16[96,2048]{1,0:T(8,128)(2,1)} %collective-permute-done.31.refs_8_), channel_id=1, source_target_pairs={{8,0},{16,8},{9,1},{17,9},{10,2},{18,10},{11,3},{19,11},{12,4},{20... | collective-permute-start | bytes 1179656 | tf_op jit(solution)/shard_map/activated_gather/ppermute | solution.py:85
  203.9 16.9 %collective-permute-start.17 = (bf16[96,2048]{1,0:T(8,128)(2,1)S(1)}, bf16[96,2048]{1,0:T(8,128)(2,1)S(1)}, u32[]{:S(2)}, u32[]{:S(2)}) collective-permute-start(bf16[96,2048]{1,0:T(8,128)(2,1)S(1)} %fusion.5.refs_4_), channel_id=1, source_target_pairs={{0,8},{8,16},{16,24},{1,9},{9,17},{17,25},{2,10},{10,18},{18,26},{... | collective-permute-start | bytes 1179656 | tf_op jit(solution)/shard_map/activated_gather/ppermute | solution.py:84
  209.8 17.7 %collective-permute-start.20 = (bf16[96,2048]{1,0:T(8,128)(2,1)S(1)}, bf16[96,2048]{1,0:T(8,128)(2,1)S(1)}, u32[]{:S(2)}, u32[]{:S(2)}) collective-permute-start(bf16[96,2048]{1,0:T(8,128)(2,1)S(1)} %fusion.5.refs_4_), channel_id=1, source_target_pairs={{8,0},{16,8},{24,16},{9,1},{17,9},{25,17},{10,2},{18,10},{26,18},{... | collective-permute-start | bytes 1179656 | tf_op jit(solution)/shard_map/activated_gather/ppermute | solution.py:85
  211.1 28.0 %collective-permute-start.30 = (bf16[96,2048]{1,0:T(8,128)(2,1)}, bf16[96,2048]{1,0:T(8,128)(2,1)}, u32[]{:S(2)}, u32[]{:S(2)}) collective-permute-start(bf16[96,2048]{1,0:T(8,128)(2,1)} %collective-permute-done.29.refs_6_), channel_id=1, source_target_pairs={{16,24},{17,25},{18,26},{19,27},{20,28},{21,29},{22,30},{23,31}} | collective-permute-start | bytes 1179656 | tf_op jit(solution)/shard_map/activated_gather/ppermute | solution.py:84
  219.2 20.0 %collective-permute-start.33 = (bf16[96,2048]{1,0:T(8,128)(2,1)}, bf16[96,2048]{1,0:T(8,128)(2,1)}, u32[]{:S(2)}, u32[]{:S(2)}) collective-permute-start(bf16[96,2048]{1,0:T(8,128)(2,1)} %collective-permute-done.32.refs_9_), channel_id=1, source_target_pairs={{8,0},{9,1},{10,2},{11,3},{12,4},{13,5},{14,6},{15,7}} | collective-permute-start | bytes 1179656 | tf_op jit(solution)/shard_map/activated_gather/ppermute | solution.py:85
  220.5 18.7 %collective-permute-start.28 = (bf16[192,512]{1,0:T(8,128)(2,1)S(1)}, bf16[192,512]{1,0:T(8,128)(2,1)S(1)}, u32[]{:S(2)}, u32[]{:S(2)}) collective-permute-start(bf16[192,512]{1,0:T(8,128)(2,1)S(1)} %attention.5.refs_0_), channel_id=1, source_target_pairs={{0,24},{8,0},{16,8},{24,16},{1,25},{9,1},{17,9},{25,17},{2,26},{10... | collective-permute-start | bytes 589832 | tf_op jit(solution)/shard_map/attention/ppermute | solution.py:28
  220.8 27.1 %collective-permute-start.18 = (bf16[96,2048]{1,0:T(8,128)(2,1)S(1)}, bf16[96,2048]{1,0:T(8,128)(2,1)}, u32[]{:S(2)}, u32[]{:S(2)}) collective-permute-start(bf16[96,2048]{1,0:T(8,128)(2,1)S(1)} %collective-permute-done.17.refs_5_), channel_id=1, source_target_pairs={{8,16},{16,24},{9,17},{17,25},{10,18},{18,26},{11,19},{19,27},{12,... | collective-permute-start | bytes 1179656 | tf_op jit(solution)/shard_map/activated_gather/ppermute | solution.py:84
  227.5 21.1 %collective-permute-start.21 = (bf16[96,2048]{1,0:T(8,128)(2,1)S(1)}, bf16[96,2048]{1,0:T(8,128)(2,1)}, u32[]{:S(2)}, u32[]{:S(2)}) collective-permute-start(bf16[96,2048]{1,0:T(8,128)(2,1)S(1)} %collective-permute-done.20.refs_8_), channel_id=1, source_target_pairs={{8,0},{16,8},{9,1},{17,9},{10,2},{18,10},{11,3},{19,11},{12,4},{20... | collective-permute-start | bytes 1179656 | tf_op jit(solution)/shard_map/activated_gather/ppermute | solution.py:85
  247.9 14.9 %collective-permute-start.19 = (bf16[96,2048]{1,0:T(8,128)(2,1)}, bf16[96,2048]{1,0:T(8,128)(2,1)S(1)}, u32[]{:S(2)}, u32[]{:S(2)}) collective-permute-start(bf16[96,2048]{1,0:T(8,128)(2,1)} %collective-permute-done.18.refs_6_), channel_id=1, source_target_pairs={{16,24},{17,25},{18,26},{19,27},{20,28},{21,29},{22,30},{23,31}} | collective-permute-start | bytes 1179656 | tf_op jit(solution)/shard_map/activated_gather/ppermute | solution.py:84
  248.6 14.2 %collective-permute-start.22 = (bf16[96,2048]{1,0:T(8,128)(2,1)}, bf16[96,2048]{1,0:T(8,128)(2,1)}, u32[]{:S(2)}, u32[]{:S(2)}) collective-permute-start(bf16[96,2048]{1,0:T(8,128)(2,1)} %collective-permute-done.21.refs_9_), channel_id=1, source_target_pairs={{8,0},{9,1},{10,2},{11,3},{12,4},{13,5},{14,6},{15,7}} | collective-permute-start | bytes 1179656 | tf_op jit(solution)/shard_map/activated_gather/ppermute | solution.py:85
  278.4 59.6 %reduce-scatter.14.cloned.1.call-start = ((), (), s32[]{:S(2)}) async-start(), calls=%async_computation.9 | async-start | bytes 1474560 | tf_op jit(solution)/shard_map/next_1/reduce_scatter | solution.py:585
  (59 other events, 485.8 us)
Sparse Core Ops, SparseCore 0:
  34.0 49.5 reduce-scatter.9
  85.9 47.1 reduce-scatter.7
  135.4 40.4 reduce-scatter.5
  278.5 28.5 reduce-scatter.11
  309.3 28.6 reduce-scatter.13

commit v3 on v2

--- a/solution.py
+++ b/solution.py
@@ -42,11 +42,10 @@
 def scatter_sum(mine, other):
     size = lax.axis_size("req")
     pair = lax.axis_index("mlp") // 2
-    rank = lax.axis_index("req")
     summed = (mine.astype(F32) + flipped(other, "mlp", 1).astype(F32)).astype(BF16)
 
     def block(owner):
-        return lax.dynamic_index_in_dim(summed, (rank - owner) % size, 0, keepdims=False)
+        return lax.dynamic_index_in_dim(summed, owner, 0, keepdims=False)
 
     total = block(pair).astype(F32)
     for d in range(1, size):
@@ -54,38 +53,8 @@
     return total
 
 
-def line_scatter(partial):
-    size = lax.axis_size("req")
-    rank = lax.axis_index("req")
-
-    def block(owner):
-        return lax.dynamic_index_in_dim(
-            partial, jnp.clip(owner, 0, size - 1), 0, keepdims=False
-        ).astype(F32)
-
-    right = left = None
-    for t in range(1, size):
-        to_right, to_left = block(rank + size - t), block(rank - size + t)
-        if right is not None:
-            to_right, to_left = to_right + right, to_left + left
-        right = lax.ppermute(to_right.astype(BF16), "req", [(k, k + 1) for k in range(t)])
-        left = lax.ppermute(
-            to_left.astype(BF16), "req", [(size - 1 - k, size - 2 - k) for k in range(t)]
-        )
-        right, left = right.astype(F32), left.astype(F32)
-    return block(rank) + right + left
-
-
-def line_gather(block):
-    size = lax.axis_size("req")
-    rights, lefts = [], []
-    right = left = block
-    for t in range(1, size):
-        right = lax.ppermute(right, "req", [(k, k + 1) for k in range(t - 1, size - 1)])
-        left = lax.ppermute(left, "req", [(k + 1, k) for k in range(size - t)])
-        rights.append(right)
-        lefts.append(left)
-    return rights, lefts
+def after(value, *others):
+    return lax.optimization_barrier((value,) + others)[0]
 
 
 def eye_mask(rows):
@@ -93,10 +62,10 @@
     return lax.broadcasted_iota(jnp.int32, shape, 0) == lax.broadcasted_iota(jnp.int32, shape, 1)
 
 
-def project_kernel(count, steps, place_ref, gain_ref, weight_ref, *refs):
-    pieces, (out, stats, *extra, held) = refs[:count], refs[count:]
+def project_kernel(count, widths, place_ref, gain_ref, weight_ref, *refs):
+    pieces, refs = refs[:count], refs[count:]
+    outs, (stats, *extra, held) = refs[: len(widths)], refs[len(widths) :]
     rows = pieces[0].shape[0]
-    beams = rows // steps
 
     @pl.when(pl.program_id(0) == 0)
     def _():
@@ -116,34 +85,37 @@
             at = pl.ds(pl.multiple_of(owner * rows, rows), rows)
             held[at, :] = (centred * gain_ref[0:1, :]).astype(BF16)
             if extra:
-                scaled = (centred * gain_ref[1:2, :]).astype(BF16)
-                at = pl.ds(pl.multiple_of(owner * beams, beams), beams)
-                for s in range(steps):
-                    extra[s][at, :] = scaled[s * beams : (s + 1) * beams]
-
-    out[...] = jnp.dot(held[...], weight_ref[...], preferred_element_type=F32).astype(BF16)
-
-
-def project(pieces, gains, weight, steps):
+                extra[0][at, :] = (centred * gain_ref[1:2, :]).astype(BF16)
+
+    result = jnp.dot(held[...], weight_ref[...], preferred_element_type=F32).astype(BF16)
+    for k, out in enumerate(outs):
+        out[...] = result[:, sum(widths[:k]) : sum(widths[: k + 1])]
+
+
+def project(pieces, gains, weight, widths):
     count = len(pieces)
     rows, width = pieces[0].shape
     columns = weight.shape[1]
-    tile = math.gcd(columns, 256)
+    tile = sum(widths)
+    steps = columns // tile
     place = lax.axis_index("mlp").astype(jnp.int32).reshape(1)
-    extra = jax.ShapeDtypeStruct((count * rows // steps, width), BF16)
-    extras = (extra,) * (steps if gains.shape[0] > 1 else 0)
+    extra = jax.ShapeDtypeStruct((count * rows, width), BF16)
+    extras = (extra,) * (gains.shape[0] - 1)
     stats = jax.ShapeDtypeStruct((2 * count, LANES), F32)
     return pl.pallas_call(
-        functools.partial(project_kernel, count, steps),
-        out_shape=(jax.ShapeDtypeStruct((count * rows, columns), BF16), stats) + extras,
-        grid=(columns // tile,),
+        functools.partial(project_kernel, count, widths),
+        out_shape=tuple(jax.ShapeDtypeStruct((count * rows, steps * w), BF16) for w in widths)
+        + (stats,)
+        + extras,
+        grid=(steps,),
         in_specs=[
             pl.BlockSpec(memory_space=pltpu.SMEM),
             full_block(gains.shape),
             pl.BlockSpec((width, tile), lambda n: (0, n)),
         ]
         + [full_block((rows, width))] * count,
-        out_specs=[pl.BlockSpec((count * rows, tile), lambda n: (0, n)), full_block(stats.shape)]
+        out_specs=[pl.BlockSpec((count * rows, w), lambda n: (0, n)) for w in widths]
+        + [full_block(stats.shape)]
         + [full_block(extra.shape)] * len(extras),
         scratch_shapes=[pltpu.VMEM((count * rows, width), BF16)],
         compiler_params=pltpu.CompilerParams(vmem_limit_bytes=32 << 20),
@@ -152,7 +124,68 @@
             bytes_accessed=2 * (width * columns + count * rows * (2 * width + columns)),
             transcendentals=0,
         ),
-    )(place, gains, weight, *pieces)
+    )(place, gains, in_hbm(weight), *pieces)
+
+
+def next_kernel(count, ranks, place_ref, gain_ref, weight_ref, *refs):
+    pieces, (out, held) = refs[:count], refs[count:]
+    rows = pieces[0].shape[0]
+    tile = weight_ref.shape[1]
+    step = pl.program_id(0)
+
+    @pl.when(step == 0)
+    def _():
+        lane = lax.broadcasted_iota(jnp.int32, (rows, LANES), 1)
+        pair, core, rank = place_ref[0] // 2, place_ref[0] % 2, place_ref[1]
+        for k in range(count):
+            d, away = k % (count // 2), k // (count // 2)
+            owner = (pair ^ d) * 2 + (core ^ away)
+            value = pieces[k][...].astype(F32)
+            mean = jnp.mean(value, axis=1, keepdims=True)
+            centred = value - mean
+            square = jnp.sum(centred * centred, axis=1, keepdims=True)
+            columns = jnp.zeros((rows, LANES), F32)
+            for j, rest in enumerate((mean, square)):
+                for part in range(3):
+                    rounded = rest.astype(BF16).astype(F32)
+                    rest = rest - rounded
+                    at = (j * 3 + part) * ranks + rank
+                    columns = jnp.where(lane == at, rounded, columns)
+            at = pl.ds(pl.multiple_of(owner * rows, rows), rows)
+            held[at, :] = (centred * gain_ref[...]).astype(BF16)
+            out[at, out.shape[1] - LANES :] = columns.astype(BF16)
+
+    result = jnp.dot(held[...], weight_ref[...], preferred_element_type=F32)
+    out[:, pl.ds(pl.multiple_of(step * tile, tile), tile)] = result.astype(BF16)
+
+
+def project_next(pieces, gain, weight):
+    count = len(pieces)
+    rows, width = pieces[0].shape
+    columns = weight.shape[1]
+    ranks = lax.axis_size("req")
+    tile = math.gcd(columns, 256)
+    place = jnp.stack([lax.axis_index("mlp"), lax.axis_index("req")]).astype(jnp.int32)
+    out = jax.ShapeDtypeStruct((count * rows, columns + LANES), BF16)
+    return pl.pallas_call(
+        functools.partial(next_kernel, count, ranks),
+        out_shape=out,
+        grid=(columns // tile,),
+        in_specs=[
+            pl.BlockSpec(memory_space=pltpu.SMEM),
+            full_block(gain.shape),
+            pl.BlockSpec((width, tile), lambda n: (0, n)),
+        ]
+        + [full_block((rows, width))] * count,
+        out_specs=full_block(out.shape),
+        scratch_shapes=[pltpu.VMEM((count * rows, width), BF16)],
+        compiler_params=pltpu.CompilerParams(vmem_limit_bytes=32 << 20),
+        cost_estimate=pl.CostEstimate(
+            flops=2 * count * rows * width * columns,
+            bytes_accessed=2 * (width * columns + count * rows * (width + columns)),
+            transcendentals=0,
+        ),
+    )(place, gain, in_hbm(weight), *pieces)
 
 
 def exchange(part):
@@ -173,83 +206,145 @@
 def weight_sums(gain, weight):
     high = gain.astype(BF16)
     low = (gain - high.astype(F32)).astype(BF16)
-    rows = jnp.zeros((16, gain.shape[0]), BF16).at[0].set(high).at[1].set(low)
+    rows = jnp.concatenate([high[None], low[None], jnp.zeros((14, gain.shape[0]), BF16)])
     both = jnp.dot(rows, weight, preferred_element_type=F32)
-    return both[0] + both[1]
-
-
-def corrected(total, away, scale, sums):
-    for part, columns in zip(away, sums):
-        total = total + part.reshape(-1, 1) * columns[None, :]
-    return total * scale.reshape(-1, 1)
-
-
-def update_kernel(ranks, steps, step, place_ref, down_ref, dense_ref, *refs):
-    attended, refs = refs[:ranks], refs[ranks:]
-    own, rights, lefts = refs[0], refs[1:ranks], refs[ranks : 2 * ranks - 1]
-    mine, other, hidden, heads = refs[2 * ranks - 1 :]
-    rows = own.shape[0]
+    return both[0:1] + both[1:2]
+
+
+def stat_columns(away, scale):
+    ranks = away.shape[0]
+    stats = jnp.concatenate([away.reshape(ranks, -1), scale.reshape(1, -1)]).T
+    return jnp.pad(stats, ((0, 0), (0, LANES - ranks - 1)))
+
+
+def corrected(total, stat_ref, sums):
+    ranks = sums.shape[0]
+    for d in range(ranks):
+        total = total + stat_ref[:, d : d + 1] * sums[d : d + 1, :]
+    return total * stat_ref[:, ranks : ranks + 1]
+
+
+def activate_kernel(beams, total_ref, stat_ref, sum_ref, *outs):
+    total = corrected(total_ref[...].astype(F32), stat_ref, sum_ref[...])
+    total = (0.5 * total * (1.0 + lax.erf(total * math.sqrt(0.5)))).astype(BF16)
+    for part in range(total.shape[0] // (STEPS * beams)):
+        for s in range(STEPS):
+            first = (part * STEPS + s) * beams
+            outs[s][part * beams : (part + 1) * beams, :] = total[first : first + beams]
+
+
+def activate(total, stats, sums, first, beams):
+    rows, columns = total.shape
+    tile = math.gcd(math.gcd(columns, 512), first)
+    out = pl.BlockSpec((rows // STEPS, tile), lambda n: (0, n))
+    return pl.pallas_call(
+        functools.partial(activate_kernel, beams),
+        out_shape=(jax.ShapeDtypeStruct((rows // STEPS, columns), BF16),) * STEPS,
+        grid=(columns // tile,),
+        in_specs=[
+            pl.BlockSpec((rows, tile), lambda n: (0, n)),
+            full_block(stats.shape),
+            pl.BlockSpec((sums.shape[0], tile), lambda n: (0, first // tile + n)),
+        ],
+        out_specs=(out,) * STEPS,
+        compiler_params=pltpu.CompilerParams(vmem_limit_bytes=24 << 20),
+    )(total, stats, sums)
+
+
+def finish_kernel(ranks, width, rank_ref, *refs):
+    totals, columns, (sum_ref, out) = refs[:STEPS], refs[STEPS : 2 * STEPS], refs[2 * STEPS :]
+    for s in range(STEPS):
+        held = columns[s][...].astype(F32)
+        lane = lax.broadcasted_iota(jnp.int32, held.shape, 1)
+
+        def column(j, d):
+            at = j * 3 * ranks + lax.rem(rank_ref[0] + ranks - d, ranks)
+            chosen = (lane == at) | (lane == at + ranks) | (lane == at + 2 * ranks)
+            return jnp.sum(jnp.where(chosen, held, 0.0), axis=1, keepdims=True)
+
+        means = [column(0, d) for d in range(ranks)]
+        mean = sum(means[1:], means[0]) * (1.0 / ranks)
+        square = jnp.zeros_like(mean)
+        total = totals[s][...].astype(F32)
+        for d in range(ranks):
+            away = means[d] - mean
+            square = square + column(1, d) + width * away * away
+            total = total + away * sum_ref[d : d + 1, :]
+        out[s] = (total * lax.rsqrt(square * (1.0 / (width * ranks)) + EPSILON)).astype(BF16)
+
+
+def finish(totals, sums, first, width):
+    rows = totals[0].shape[0]
+    columns = totals[0].shape[1] - LANES
+    tile = math.gcd(math.gcd(columns, 512), first)
+    ranks = lax.axis_size("req")
+    rank = lax.axis_index("req").astype(jnp.int32).reshape(1)
+    totals = [in_hbm(total) for total in totals]
+    return pl.pallas_call(
+        functools.partial(finish_kernel, ranks, width),
+        out_shape=jax.ShapeDtypeStruct((STEPS, rows, columns), BF16),
+        grid=(columns // tile,),
+        in_specs=[pl.BlockSpec(memory_space=pltpu.SMEM)]
+        + [pl.BlockSpec((rows, tile), lambda n: (0, n))] * STEPS
+        + [pl.BlockSpec((rows, LANES), lambda n: (0, columns // LANES))] * STEPS
+        + [pl.BlockSpec((sums.shape[0], tile), lambda n: (0, first // tile + n))],
+        out_specs=pl.BlockSpec((STEPS, rows, tile), lambda n: (0, 0, n)),
+        compiler_params=pltpu.CompilerParams(vmem_limit_bytes=24 << 20),
+    )(rank, *totals, *totals, sums)
+
+
+def update_kernel(ranks, step, place_ref, hidden_ref, down_ref, dense_ref, *refs):
+    attended, (mine, other, heads) = refs[:ranks], refs[ranks:]
+    rows = hidden_ref.shape[0] // ranks
     rank, core = place_ref[0], place_ref[1]
 
     @pl.when(pl.program_id(0) == 0)
     def _():
-        hidden[0:rows, :] = own[...]
-        for d in range(1, ranks):
-            at = slice(d * rows, (d + 1) * rows)
-
-            @pl.when(rank >= d)
-            def _():
-                hidden[at, :] = rights[d - 1][...]
-
-            @pl.when(rank < d)
-            def _():
-                hidden[at, :] = lefts[ranks - d - 1][...]
-
         for d in range(ranks):
-            heads[d * rows : (d + 1) * rows, :] = attended[d][step * rows : (step + 1) * rows, :]
-
-    result = jnp.dot(hidden[...], down_ref[...], preferred_element_type=F32) + jnp.dot(
+            owner = lax.rem(rank + ranks - d, ranks)
+            heads[pl.ds(pl.multiple_of(owner * rows, rows), rows), :] = attended[d][
+                step * rows : (step + 1) * rows, :
+            ]
+
+    result = jnp.dot(hidden_ref[...], down_ref[...], preferred_element_type=F32) + jnp.dot(
         heads[...], dense_ref[...], preferred_element_type=F32
     )
     half = rows // 2
-    for d in range(ranks):
-        first = result[d * rows : d * rows + half]
-        second = result[d * rows + half : (d + 1) * rows]
-        mine[d] = jnp.where(core == 0, first, second).astype(BF16)
-        other[d] = jnp.where(core == 0, second, first).astype(BF16)
-
-
-def layer_update(step, attended, own, rights, lefts, dense_weight, down_weight):
+    for k in range(ranks):
+        first = result[k * rows : k * rows + half]
+        second = result[k * rows + half : (k + 1) * rows]
+        mine[k] = jnp.where(core == 0, first, second).astype(BF16)
+        other[k] = jnp.where(core == 0, second, first).astype(BF16)
+
+
+def layer_update(step, hidden, attended, dense_weight, down_weight):
     ranks = lax.axis_size("req")
-    rows, hidden = own.shape
+    rows, columns = hidden.shape
     head_width, width = dense_weight.shape
     tile = min(256, width)
     place = jnp.stack([lax.axis_index("req"), lax.axis_index("mlp") % 2]).astype(jnp.int32)
-    shape = jax.ShapeDtypeStruct((ranks, rows // 2, width), BF16)
-    out_block = pl.BlockSpec((ranks, rows // 2, tile), lambda n: (0, 0, n))
-    return pl.pallas_call(
-        functools.partial(update_kernel, ranks, STEPS, step),
+    shape = jax.ShapeDtypeStruct((ranks, rows // ranks // 2, width), BF16)
+    out_block = pl.BlockSpec((ranks, rows // ranks // 2, tile), lambda n: (0, 0, n))
+    return pl.pallas_call(
+        functools.partial(update_kernel, ranks, step),
         out_shape=(shape, shape),
         grid=(width // tile,),
         in_specs=[
             pl.BlockSpec(memory_space=pltpu.SMEM),
-            pl.BlockSpec((hidden, tile), lambda n: (0, n)),
+            full_block(hidden.shape),
+            pl.BlockSpec((columns, tile), lambda n: (0, n)),
             pl.BlockSpec((head_width, tile), lambda n: (0, n)),
         ]
-        + [full_block(attended[0].shape)] * ranks
-        + [full_block((rows, hidden))] * (2 * ranks - 1),
+        + [full_block(attended[0].shape)] * ranks,
         out_specs=(out_block, out_block),
-        scratch_shapes=[
-            pltpu.VMEM((ranks * rows, hidden), BF16),
-            pltpu.VMEM((ranks * rows, head_width), BF16),
-        ],
+        scratch_shapes=[pltpu.VMEM((rows, head_width), BF16)],
         compiler_params=pltpu.CompilerParams(vmem_limit_bytes=40 << 20),
         cost_estimate=pl.CostEstimate(
-            flops=2 * ranks * rows * (hidden + head_width) * width,
-            bytes_accessed=2 * (hidden + head_width) * width + 4 * ranks * rows * hidden,
+            flops=2 * rows * (columns + head_width) * width,
+            bytes_accessed=2 * (columns + head_width) * (width + rows),
             transcendentals=0,
         ),
-    )(place, down_weight, dense_weight, *attended, own, *rights, *lefts)
+    )(place, in_hbm(hidden), in_hbm(down_weight), in_hbm(dense_weight), *attended)
 
 
 def rotary_tables(positions):
@@ -264,45 +359,82 @@
     return cosine, upper, lower
 
 
+def in_hbm(array):
+    return pltpu.with_memory_space_constraint(array, pltpu.HBM)
+
+
 def full_block(shape):
     return pl.BlockSpec(shape, lambda *_: (0,) * len(shape))
 
 
-def head_split_kernel(heads, parts, requests, ranks, x_ref, stat_ref, sum_ref, *refs):
+def turn(value, tables):
+    return (
+        value * tables[0][...]
+        + pltpu.roll(value, HD - ROT // 2, 1) * tables[1][...]
+        + pltpu.roll(value, ROT // 2, 1) * tables[2][...]
+    )
+
+
+def store_head(out, value, head, heads, parts, requests):
+    rows = requests * BEAM
+    for part in range(parts):
+        for request in range(requests):
+            first = part * STEPS * rows + request * BEAM
+            pair = [value[first + s * rows : first + s * rows + BEAM] for s in range(STEPS)]
+            at = ((part * requests + request) * heads + head) * STEPS * BEAM
+            out[at : at + STEPS * BEAM, :] = jnp.concatenate(pair, axis=0).astype(BF16)
+
+
+def query_kernel(heads, parts, requests, rank_ref, own_ref, *refs):
+    received, (stat_ref, sum_ref, *tables, out) = refs[:-6], refs[-6:]
+    for head in range(heads):
+        at = slice(head * HD, (head + 1) * HD)
+        value = own_ref[0, :, at].astype(F32)
+        for piece in received:
+            value = value + piece[:, at].astype(F32)
+        first = head * 3 * HD
+        value = corrected(value, stat_ref, sum_ref[:, first : first + HD])
+        store_head(out, turn(value, tables), head, heads, parts, requests)
+
+
+def split_queries(partial, received, stats, sums, tables, heads, parts, requests):
+    rank = lax.axis_index("req").astype(jnp.int32).reshape(1)
+    operands = (*received, stats, sums, *tables)
+    rows = parts * requests * heads * STEPS * BEAM
+    return pl.pallas_call(
+        functools.partial(query_kernel, heads, parts, requests),
+        out_shape=jax.ShapeDtypeStruct((rows, HD), BF16),
+        grid_spec=pltpu.PrefetchScalarGridSpec(
+            num_scalar_prefetch=1,
+            grid=(1,),
+            in_specs=[pl.BlockSpec((1,) + partial.shape[1:], lambda n, r: (r[0], 0, 0))]
+            + [full_block(operand.shape) for operand in operands],
+            out_specs=full_block((rows, HD)),
+        ),
+        compiler_params=pltpu.CompilerParams(vmem_limit_bytes=24 << 20),
+    )(rank, partial, *operands)
+
+
+def key_value_kernel(heads, parts, requests, x_ref, stat_ref, sum_ref, *refs):
     tables, outs = refs[:3], refs[3:]
-    rows = requests * BEAM
-    scale = stat_ref[:, ranks : ranks + 1]
     for head in range(heads):
         for kind, out in enumerate(outs):
-            column = (head * 3 + kind) * HD
+            column = (head * 2 + kind) * HD
             value = x_ref[:, column : column + HD].astype(F32)
-            for d in range(ranks):
-                value = value + stat_ref[:, d : d + 1] * sum_ref[d : d + 1, column : column + HD]
-            value = value * scale
-            if kind < 2:
-                value = (
-                    value * tables[0][...]
-                    + pltpu.roll(value, HD - ROT // 2, 1) * tables[1][...]
-                    + pltpu.roll(value, ROT // 2, 1) * tables[2][...]
-                )
-            for part in range(parts):
-                for request in range(requests):
-                    first = part * STEPS * rows + request * BEAM
-                    pair = [value[first + s * rows : first + s * rows + BEAM] for s in range(STEPS)]
-                    at = ((part * requests + request) * heads + head) * STEPS * BEAM
-                    out[at : at + STEPS * BEAM, :] = jnp.concatenate(pair, axis=0).astype(BF16)
-
-
-def head_split(shared, away, scale, sums, tables, heads, parts, requests):
-    ranks = len(sums)
-    stats = jnp.concatenate([away.reshape(ranks, -1), scale.reshape(1, -1)]).T
-    stats = jnp.pad(stats, ((0, 0), (0, LANES - ranks - 1)))
+            column = (head * 3 + kind + 1) * HD
+            value = corrected(value, stat_ref, sum_ref[:, column : column + HD])
+            if kind == 0:
+                value = turn(value, tables)
+            store_head(out, value, head, heads, parts, requests)
+
+
+def split_keys_values(total, stats, sums, tables, heads, parts, requests):
     shape = jax.ShapeDtypeStruct((parts * requests * heads * STEPS * BEAM, HD), BF16)
     return pl.pallas_call(
-        functools.partial(head_split_kernel, heads, parts, requests, ranks),
-        out_shape=(shape, shape, shape),
-        compiler_params=pltpu.CompilerParams(vmem_limit_bytes=32 << 20),
-    )(shared, stats, jnp.stack(sums), *tables)
+        functools.partial(key_value_kernel, heads, parts, requests),
+        out_shape=(shape, shape),
+        compiler_params=pltpu.CompilerParams(vmem_limit_bytes=24 << 20),
+    )(total, stats, sums, *tables)
 
 
 def page_kernel(heads, ranks, own_rows, slot_ref, length_ref, me_ref, k_ref, v_ref, *rest):
@@ -410,13 +542,13 @@
         compiler_params=pltpu.CompilerParams(vmem_limit_bytes=40 << 20),
         cost_estimate=pl.CostEstimate(
             flops=4 * slots * PAGE * heads * HD * STEPS * BEAM,
-            bytes_accessed=2 * slots * PAGE * heads * HD * 2,
+            bytes_accessed=8 * slots * PAGE * heads * HD * 2,
             transcendentals=slots * PAGE * heads * STEPS * BEAM,
         ),
-    )(slot_table, lengths, me, keys, values, *queries)
-
-
-def merge_kernel(heads, ranks, requests, q_ref, k_ref, v_ref, parent_ref, *rest):
+    )(slot_table, lengths, me, in_hbm(keys), in_hbm(values), *queries)
+
+
+def merge_kernel(heads, ranks, parts, requests, q_ref, k_ref, v_ref, parent_ref, *rest):
     pieces, out, work = rest[:ranks], rest[ranks], rest[ranks + 1]
     chunk = STEPS * BEAM
     height = heads * chunk
@@ -469,24 +601,25 @@
             result = result + factor * piece[at, :].astype(F32)
         work[at, :] = result / total
     rows = requests * BEAM
-    for request in range(0, requests, 2):
-        for head in range(heads):
-            for s in range(STEPS):
-                tiles = []
-                for r in (request, request + 1):
-                    first = r * height + head * chunk + s * BEAM
-                    tiles.append(work[first : first + BEAM, :])
-                first = s * rows + request * BEAM
-                out[first : first + 2 * BEAM, head * HD : (head + 1) * HD] = jnp.concatenate(
-                    tiles, axis=0
-                ).astype(BF16)
-
-
-def merge(queries, keys, values, parents, pieces, heads, requests):
+    for part in range(parts):
+        for request in range(0, requests, 2):
+            for head in range(heads):
+                for s in range(STEPS):
+                    tiles = []
+                    for r in (request, request + 1):
+                        first = (part * requests + r) * height + head * chunk + s * BEAM
+                        tiles.append(work[first : first + BEAM, :])
+                    first = (s * parts + part) * rows + request * BEAM
+                    out[first : first + 2 * BEAM, head * HD : (head + 1) * HD] = jnp.concatenate(
+                        tiles, axis=0
+                    ).astype(BF16)
+
+
+def merge(queries, keys, values, parents, pieces, heads, parts, requests):
     ranks = len(pieces)
-    rows = requests * STEPS * BEAM
-    return pl.pallas_call(
-        functools.partial(merge_kernel, heads, ranks, requests),
+    rows = STEPS * parts * requests * BEAM
+    return pl.pallas_call(
+        functools.partial(merge_kernel, heads, ranks, parts, requests),
         out_shape=jax.ShapeDtypeStruct((rows, heads * HD), BF16),
         scratch_shapes=[pltpu.VMEM(queries.shape, F32)],
         compiler_params=pltpu.CompilerParams(vmem_limit_bytes=32 << 20),
@@ -529,63 +662,59 @@
 
     with jax.named_scope("inputs_gather"):
         pieces = gather_pieces(inputs.reshape(STEPS * beams, width))
+    with jax.named_scope("qkv"):
+        query, key_value, stats, mlp_in = project(
+            pieces, norm_gains[:2], attn_weight, (HD, 2 * HD)
+        )
+        key_value = lax.psum_scatter(key_value, "req", scatter_dimension=0, tiled=True)
+        query = query.reshape(ranks, -1, query.shape[1])
+        received = [
+            rotated(
+                lax.dynamic_index_in_dim(query, (rank + d) % ranks, 0, keepdims=False), "req", d
+            )
+            for d in range(1, ranks)
+        ]
     with jax.named_scope("weight_sums"):
         weights = (attn_weight, up_weight, next_weight)
-        sums = jnp.concatenate([weight_sums(norm_gains[k], w) for k, w in enumerate(weights)])
-        sums = [part.reshape(-1) for part in exchange(sums.reshape(-1, LANES))]
-        cuts = (0, weights[0].shape[1], weights[0].shape[1] + weights[1].shape[1], sums[0].shape[0])
-        sums = [[part[a:b] for part in sums] for a, b in zip(cuts, cuts[1:])]
-    with jax.named_scope("qkv"):
-        partial, stats, *mlp_in = project(pieces, norm_gains[:2], attn_weight, STEPS)
-        mixed = lax.psum_scatter(partial, "req", scatter_dimension=0, tiled=True)
+        sums = [weight_sums(norm_gains[k], w) for k, w in enumerate(weights)]
+        sums = jnp.concatenate(exchange(jnp.concatenate(sums, axis=1)))
+        up_first = attn_weight.shape[1]
+        next_first = up_first + up_weight.shape[1]
     with jax.named_scope("statistics"):
-        away, scale = own_statistics(stats, width, STEPS * beams)
+        stats = stat_columns(*own_statistics(stats, width, STEPS * beams))
+    with jax.named_scope("queries"):
+        queries = split_queries(query, received, stats, sums, tables, heads, parts, requests)
+        queries_all = exchange(queries)
     with jax.named_scope("up"):
-        hiddens = []
-        for s in range(STEPS):
-            partial = jnp.dot(mlp_in[s], up_weight, preferred_element_type=F32).astype(BF16)
-            partial, away, scale, sums = lax.optimization_barrier((partial, away, scale, sums))
-            hiddens.append(lax.psum_scatter(partial, "req", scatter_dimension=0, tiled=True))
-
-    def activate(s, hidden):
-        at = slice(s * beams, (s + 1) * beams)
-        with jax.named_scope("gelu"):
-            hidden = corrected(hidden.astype(F32), away[..., at], scale[:, at], sums[1])
-            own = jax.nn.gelu(hidden, approximate=False).astype(BF16)
-        with jax.named_scope("activated_gather"):
-            return (own,) + line_gather(own)
-
-    with jax.named_scope("attention"):
-        queries, keys, values = head_split(
-            mixed, away, scale, sums[0], tables, heads, parts, requests
-        )
-        queries_all = exchange(queries)
+        up = jnp.dot(after(mlp_in, queries), up_weight, preferred_element_type=F32).astype(BF16)
+        up = lax.psum_scatter(up, "req", scatter_dimension=0, tiled=True)
+    with jax.named_scope("pages"):
         pieces = page_attention(
             queries_all, cache_keys, cache_values, slot_table, lengths, heads, ranks
         )
-    hiddens[0], pieces = lax.optimization_barrier((hiddens[0], pieces))
-    activated = [activate(0, hiddens[0])]
-    with jax.named_scope("attention"):
         pieces = [pieces[0]] + [rotated(pieces[d], "req", d) for d in range(1, ranks)]
-        attended = merge(queries, keys, values, parent_wide, pieces, heads, own_requests)
-        attended = exchange(attended)
-    hiddens[1], first = lax.optimization_barrier((hiddens[1], activated[0][1][0]))
-    activated[0][1][0] = first
-    activated.append(activate(1, hiddens[1]))
-    layers, followings = [], []
+    with jax.named_scope("merge"):
+        key_value = after(key_value, pieces[0])
+        keys, values = split_keys_values(
+            key_value, stats, sums, tables, heads, parts, requests
+        )
+        attended = merge(queries, keys, values, parent_wide, pieces, heads, parts, requests)
+        attended_all = exchange(attended)
+    with jax.named_scope("activated"):
+        activated = activate(after(up, attended), stats, sums, up_first, beams)
+        activated = [lax.all_gather(own, "req", axis=0, tiled=True) for own in activated]
+    layers, totals = [], []
     for s in range(STEPS):
         with jax.named_scope(f"down_{s}"):
-            mine, other = layer_update(s, attended, *activated[s], dense_weight, down_weight)
+            mine, other = layer_update(s, activated[s], attended_all, dense_weight, down_weight)
             layer = (inputs[s].astype(F32) + scatter_sum(mine, other)).astype(BF16)
-            if s + 1 < STEPS:
-                activated[s + 1], layer = lax.optimization_barrier((activated[s + 1], layer))
             layers.append(layer)
         with jax.named_scope(f"next_{s}"):
-            partial, stats = project(gather_pieces(layer), norm_gains[2:], next_weight, 1)
-            total = lax.psum_scatter(partial, "req", scatter_dimension=0, tiled=True).astype(F32)
-            away, scale = own_statistics(stats, width, beams)
-            followings.append(corrected(total, away, scale, sums[2]).astype(BF16))
-    return jnp.stack(layers), jnp.stack(followings)
+            partial = project_next(gather_pieces(layer), norm_gains[2:], next_weight)
+            if s + 1 < STEPS:
+                activated[s + 1] = after(activated[s + 1], partial)
+            totals.append(lax.psum_scatter(partial, "req", scatter_dimension=0, tiled=True))
+    return jnp.stack(layers), finish(totals, sums, next_first, width)
 
 
 def solution(mesh):

time: 348 us -> 337 us (0.968)
  local copies, waits for them, and re-layouts: 23.9 us -> 5.14 us
  waiting for transfers between devices: 140 us -> 158 us
  Pallas kernels: 49.5 us -> 62 us
  other arithmetic: 12.9 us -> 2.76 us
  starting transfers between devices: 91.7 us -> 82.2 us
    ppermute x12 -> x0, starting transfers between devices: 37.7 us -> none  [the longest x6 29.8 us: line_gather(): lax.ppermute(right, 'req', [(k, k + 1) for k in range(t - 1, size - 1)])]
    all_gather x0 -> x2, waiting for transfers between devices: none -> 27.6 us  [shards(): lax.all_gather(own, 'req', axis=0, tiled=True)]
    ppermute x21 -> x18, starting transfers between devices: 34.3 us -> 61.7 us  [rotated(): lax.ppermute(array, axis, [(k, (k + distance) % size) for k in range(size)])]
    reduce_scatter x1 -> x2, waiting for transfers between devices: 18.6 us -> 0.02 us  [the longest x1 0.02 us: shards(): up = lax.psum_scatter(up, 'req', scatter_dimension=0, tiled=True)]
    unnamed x48 -> x21, local copies, waits for them, and re-layouts: 18.9 us -> 3.34 us
    reduce_scatter x4 -> x2, waiting for transfers between devices: 16.6 us -> 31.8 us  [shards(): lax.psum_scatter(partial, 'req', scatter_dimension=0, tiled=True)]
    pallas_call x7 -> x10, Pallas kernels: 27.9 us -> 40.8 us  [the longest x2 12.9 us: project_next(): pl.pallas_call(functools.partial(next_kernel, count, ranks), out_shape=ou...]
    ppermute x21 -> x18, waiting for transfers between devices: 61.8 us -> 74.2 us  [rotated(): lax.ppermute(array, axis, [(k, (k + distance) % size) for k in range(size)])]
  transfers between devices with their start and end apart: 67 -> 53, of which waited for: 33 -> 28; matrix products, arithmetic and copies ran while one was open for 9% -> 5% of each run, Pallas kernels for 12% -> 17%
where the time goes in v3:
time: 337 us; the launch traced here: 336 us
  waiting for transfers between devices  158 us (47%)
  starting transfers between devices  82.2 us (24%)
  Pallas kernels  62 us (18%)
  between operations  14.5 us (4%)
  matrix products  11.9 us (4%)
  local copies, waits for them, and re-layouts  5.14 us (2%)
    ppermute x18, waiting for transfers between devices, rotated(): lax.ppermute(array, axis, [(k, (k + distance) % size) for k in range(size)])  74.2 us
    ppermute x18, starting transfers between devices, rotated(): lax.ppermute(array, axis, [(k, (k + distance) % size) for k in range(size)])  61.7 us
    reduce_scatter x2, waiting for transfers between devices, shards(): lax.psum_scatter(partial, 'req', scatter_dimension=0, tiled=True)  31.8 us
    all_gather x2, waiting for transfers between devices, shards(): lax.all_gather(own, 'req', axis=0, tiled=True)  27.6 us
    ppermute x29, waiting for transfers between devices, flipped(): lax.ppermute(array, axis, [(k, k ^ bits) for k in range(lax.axis_size(axi...  23.3 us
    pallas_call x1, Pallas kernels, page_attention(): pl.pallas_call(functools.partial(page_kernel, heads, ranks, own_rows), ou...  21.2 us
    ppermute x29, starting transfers between devices, flipped(): lax.ppermute(array, axis, [(k, k ^ bits) for k in range(lax.axis_size(axi...  20.3 us
    pallas_call x2, Pallas kernels, project_next(): pl.pallas_call(functools.partial(next_kernel, count, ranks), out_shape=ou...  12.9 us
  transfers between devices with their start and end apart: 53, of which 28 were waited for; matrix products, arithmetic and copies ran while one was open for 5% of the time, Pallas kernels for 17%

profile of v3, /device:TPU:0, one launch (start us, length us, event | category | flops | bytes accessed | tf_op | source)
XLA Modules:
  0.0 336.1 jit_solution(16681967050324505069)
XLA Ops:
  7.2 3.0 collective-permute-start
  13.6 3.0 fusion.17
  17.8 2.1 collective-permute-start.13
  21.5 2.7 collective-permute-start.14
  25.6 7.6 %qkv.1 = (bf16[768,512]{1,0:T(8,128)(2,1)S(1)}, bf16[768,1024]{1,0:T(8,128)(2,1)}, f32[16,128]{1,0:T(8,128)S(1)}, bf16[768,1024]{1,0:T(8,128)(2,1)S(1)}) custom-call(s32[1]{0:T(128)} %bitcast.3.place_ref, f32[2,1024]{1,0:T(2,128)S(1)} %slice.49.gain_ref, bf16[1024,1536]{1,0:T(8,128)(2,1)} %weight_ref.3, bf16[96,1024]{1,0:T(8,128)(2,1)S(1)} %bitcast.77, ...), custom_call_target="tpu_custom_call" | custom-call | flops 2415919104 | bytes 8650752 | tf_op jit(solution)/shard_map/qkv/pallas_call | solution.py:105
  36.9 2.8 collective-permute-start.12
  41.2 2.8 collective-permute-start.9
  44.5 9.1 %collective-permute-done.7.refs_0_ = bf16[192,512]{1,0:T(8,128)(2,1)S(1)} collective-permute-done((bf16[192,512]{1,0:T(8,128)(2,1)S(1)}, bf16[192,512]{1,0:T(8,128)(2,1)S(1)}, u32[]{:S(2)}, u32[]{:S(2)}) %collective-permute-start.7) | collective-permute-done | bytes 196640 | tf_op jit(solution)/shard_map/qkv/ppermute | solution.py:28
  53.6 12.4 %collective-permute-done.8.refs_1_ = bf16[192,512]{1,0:T(8,128)(2,1)S(1)} collective-permute-done((bf16[192,512]{1,0:T(8,128)(2,1)S(1)}, bf16[192,512]{1,0:T(8,128)(2,1)S(1)}, u32[]{:S(2)}, u32[]{:S(2)}) %collective-permute-start.8) | collective-permute-done | bytes 196640 | tf_op jit(solution)/shard_map/qkv/ppermute | solution.py:28
  67.0 7.7 %convolution_convert_fusion = bf16[768,2048]{1,0:T(8,128)(2,1)} fusion(bf16[768,1024]{1,0:T(8,128)(2,1)} %copy-done.5, bf16[1024,2048]{1,0:T(8,128)(2,1)} %param.15), kind=kOutput, calls=%fused_computation | convolution fusion | flops 3222798336 | bytes 8912896 | tf_op jit(solution)/shard_map/up/dot_general | solution.py:689
  74.8 15.1 %collective-permute-start.16 = (bf16[768,128]{1,0:T(8,128)(2,1)S(1)}, bf16[768,128]{1,0:T(8,128)(2,1)S(1)}, u32[]{:S(2)}, u32[]{:S(2)}) collective-permute-start(bf16[768,128]{1,0:T(8,128)(2,1)S(1)} %queries.1.rest_0_.q_ref), channel_id=1, source_target_pairs={{0,8},{8,16},{16,24},{24,0},{1,9},{9,17},{17,25},{25,1},{2,10},{10... | collective-permute-start | bytes 589832 | tf_op jit(solution)/shard_map/queries/ppermute | solution.py:28
  92.4 4.7 %collective-permute-done.16.rest_1_ = bf16[768,128]{1,0:T(8,128)(2,1)S(1)} collective-permute-done((bf16[768,128]{1,0:T(8,128)(2,1)S(1)}, bf16[768,128]{1,0:T(8,128)(2,1)S(1)}, u32[]{:S(2)}, u32[]{:S(2)}) %collective-permute-start.16) | collective-permute-done | bytes 196640 | tf_op jit(solution)/shard_map/queries/ppermute | solution.py:28
  97.1 11.7 %collective-permute-done.17.rest_2_ = bf16[768,128]{1,0:T(8,128)(2,1)S(1)} collective-permute-done((bf16[768,128]{1,0:T(8,128)(2,1)S(1)}, bf16[768,128]{1,0:T(8,128)(2,1)S(1)}, u32[]{:S(2)}, u32[]{:S(2)}) %collective-permute-start.17) | collective-permute-done | bytes 196640 | tf_op jit(solution)/shard_map/queries/ppermute | solution.py:28
  110.2 21.2 %pages.1 = (bf16[816,128]{1,0:T(8,128)(2,1)S(1)}, bf16[816,128]{1,0:T(8,128)(2,1)S(1)}, bf16[816,128]{1,0:T(8,128)(2,1)S(1)}, bf16[816,128]{1,0:T(8,128)(2,1)S(1)}) custom-call(s32[2,64]{1,0:T(2,128)S(1)} %copy-done.3, s32[48]{0:T(128)S(1)} %copy-done.4, s32[1]{0:T(128)} %bitcast.1.rank_ref.me_ref, bf16[64,128,512]{2,1,0:T(8,128)(2,1)} %k_ref.1, ...), custom_call_target="tpu_custom_call" | custom-call | flops 268435456 | bytes 67108864 | tf_op jit(solution)/shard_map/pages/pallas_call | solution.py:532
  131.4 15.9 %collective-permute-start.19 = (bf16[816,128]{1,0:T(8,128)(2,1)S(1)}, bf16[816,128]{1,0:T(8,128)(2,1)S(1)}, u32[]{:S(2)}, u32[]{:S(2)}) collective-permute-start(bf16[816,128]{1,0:T(8,128)(2,1)S(1)} %get-tuple-element.31), channel_id=1, source_target_pairs={{0,8},{8,16},{16,24},{24,0},{1,9},{9,17},{17,25},{25,1},{2,10},{10... | collective-permute-start | bytes 626696 | tf_op jit(solution)/shard_map/pages/ppermute | solution.py:28
  147.3 2.4 collective-permute-start.21
  152.3 5.0 %collective-permute-done.19.rest_1_ = bf16[816,128]{1,0:T(8,128)(2,1)S(1)} collective-permute-done((bf16[816,128]{1,0:T(8,128)(2,1)S(1)}, bf16[816,128]{1,0:T(8,128)(2,1)S(1)}, u32[]{:S(2)}, u32[]{:S(2)}) %collective-permute-start.19) | collective-permute-done | bytes 208928 | tf_op jit(solution)/shard_map/pages/ppermute | solution.py:28
  157.4 9.5 %collective-permute-done.20.rest_2_ = bf16[816,128]{1,0:T(8,128)(2,1)S(1)} collective-permute-done((bf16[816,128]{1,0:T(8,128)(2,1)S(1)}, bf16[816,128]{1,0:T(8,128)(2,1)S(1)}, u32[]{:S(2)}, u32[]{:S(2)}) %collective-permute-start.20) | collective-permute-done | bytes 208928 | tf_op jit(solution)/shard_map/pages/ppermute | solution.py:28
  169.2 2.3 activated.1
  172.2 8.4 %collective-permute-start.22 = (bf16[192,512]{1,0:T(8,128)(2,1)S(1)}, bf16[192,512]{1,0:T(8,128)(2,1)S(1)}, u32[]{:S(2)}, u32[]{:S(2)}) collective-permute-start(bf16[192,512]{1,0:T(8,128)(2,1)S(1)} %merge.3.refs_0_), channel_id=1, source_target_pairs={{0,8},{8,16},{16,24},{24,0},{1,9},{9,17},{17,25},{25,1},{2,10},{10... | collective-permute-start | bytes 589832 | tf_op jit(solution)/shard_map/merge/ppermute | solution.py:28
  183.1 4.9 %collective-permute-done.22.refs_1_ = bf16[192,512]{1,0:T(8,128)(2,1)S(1)} collective-permute-done((bf16[192,512]{1,0:T(8,128)(2,1)S(1)}, bf16[192,512]{1,0:T(8,128)(2,1)S(1)}, u32[]{:S(2)}, u32[]{:S(2)}) %collective-permute-start.22) | collective-permute-done | bytes 196640 | tf_op jit(solution)/shard_map/merge/ppermute | solution.py:28
  187.9 15.5 %collective-permute-done.23.refs_2_ = bf16[192,512]{1,0:T(8,128)(2,1)S(1)} collective-permute-done((bf16[192,512]{1,0:T(8,128)(2,1)S(1)}, bf16[192,512]{1,0:T(8,128)(2,1)S(1)}, u32[]{:S(2)}, u32[]{:S(2)}) %collective-permute-start.23) | collective-permute-done | bytes 196640 | tf_op jit(solution)/shard_map/merge/ppermute | solution.py:28
  203.5 21.4 %all-gather.3.cloned.1.call-done.hidden_ref = bf16[384,2048]{1,0:T(8,128)(2,1)} async-done(((bf16[96,2048]{1,0:T(8,128)(2,1)}), bf16[384,2048]{1,0:T(8,128)(2,1)}) %all-gather.3.cloned.1.call-update) | async-done | bytes 1572880 | tf_op jit(solution)/shard_map/activated/all_gather | solution.py:705
  224.9 5.4 %down_0.1 = (bf16[4,48,1024]{2,1,0:T(8,128)(2,1)S(1)}, bf16[4,48,1024]{2,1,0:T(8,128)(2,1)S(1)}) custom-call(s32[2]{0:T(128)S(1)} %pad_add_fusion.place_ref, bf16[384,2048]{1,0:T(8,128)(2,1)} %all-gather.3.cloned.1.call-done.hidden_ref, bf16[2048,1024]{1,0:T(8,128)(2,1)} %down_ref.3, bf16[512,1024]{1,0:T(8,128)(2,1)} %dense_ref.3, ...), custom_call_target="tpu_custom_call" | custom-call | flops 2013265920 | bytes 7208960 | tf_op jit(solution)/shard_map/down_0/pallas_call | solution.py:328
  244.3 2.2 collective-permute-done.29.refs_1_
  249.6 6.4 %next_0.1 = bf16[384,1664]{1,0:T(8,128)(2,1)} custom-call(s32[2]{0:T(128)S(1)} %pad_add_fusion.1.place_ref, f32[1,1024]{1,0:T(1,128)S(1)} %get-tuple-element.51.gain_ref, bf16[1024,1536]{1,0:T(8,128)(2,1)} %weight_ref.5, bf16[48,1024]{1,0:T(8,128)(2,1)S(1)} %fusion.7.refs_0_, bf16[48,1024]{1,0:T(8,128)(2,1)S(1)} %collective-permute-done.29.refs_1_, ...), custom_call_target="tpu_custom_call" | custom-call | flops 1207959552 | bytes 5111808 | tf_op jit(solution)/shard_map/next_0/pallas_call | solution.py:170
  256.1 6.2 %all-gather.5.cloned.1.call-done.hidden_ref = bf16[384,2048]{1,0:T(8,128)(2,1)} async-done(((bf16[96,2048]{1,0:T(8,128)(2,1)}), bf16[384,2048]{1,0:T(8,128)(2,1)}) %all-gather.5.cloned.1.call-update) | async-done | bytes 1572880 | tf_op jit(solution)/shard_map/activated/all_gather | solution.py:705
  262.2 5.4 %down_1.1 = (bf16[4,48,1024]{2,1,0:T(8,128)(2,1)S(1)}, bf16[4,48,1024]{2,1,0:T(8,128)(2,1)S(1)}) custom-call(s32[2]{0:T(128)S(1)} %pad_add_fusion.place_ref, bf16[384,2048]{1,0:T(8,128)(2,1)} %all-gather.5.cloned.1.call-done.hidden_ref, bf16[2048,1024]{1,0:T(8,128)(2,1)} %down_ref.3, bf16[512,1024]{1,0:T(8,128)(2,1)} %dense_ref.3, ...), custom_call_target="tpu_custom_call" | custom-call | flops 2013265920 | bytes 7208960 | tf_op jit(solution)/shard_map/down_1/pallas_call | solution.py:328
  274.6 2.4 collective-permute-done.38
  286.9 6.4 %next_1.1 = bf16[384,1664]{1,0:T(8,128)(2,1)} custom-call(s32[2]{0:T(128)S(1)} %pad_add_fusion.1.place_ref, f32[1,1024]{1,0:T(1,128)S(1)} %get-tuple-element.51.gain_ref, bf16[1024,1536]{1,0:T(8,128)(2,1)} %weight_ref.5, bf16[48,1024]{1,0:T(8,128)(2,1)S(1)} %fusion.3.refs_0_, bf16[48,1024]{1,0:T(8,128)(2,1)S(1)} %collective-permute-done.40.refs_1_, ...), custom_call_target="tpu_custom_call" | custom-call | flops 1207959552 | bytes 5111808 | tf_op jit(solution)/shard_map/next_1/pallas_call | solution.py:170
  294.1 31.8 %reduce-scatter.11.cloned.1.call-done.refs_1_.refs_3_ = bf16[96,1664]{1,0:T(8,128)(2,1)} async-done(((bf16[384,1664]{1,0:T(8,128)(2,1)}), bf16[96,1664]{1,0:T(8,128)(2,1)}) %reduce-scatter.11.cloned.1.call-update) | async-done | bytes 319504 | tf_op jit(solution)/shard_map/next_1/reduce_scatter | solution.py:716
  325.8 3.4 %shard_map.131 = bf16[2,96,1536]{2,1,0:T(8,128)(2,1)} custom-call(s32[1]{0:T(128)} %bitcast.1.rank_ref.me_ref, bf16[96,1664]{1,0:T(8,128)(2,1)} %reduce-scatter.9.cloned.1.call-done.refs_0_.refs_2_, bf16[96,1664]{1,0:T(8,128)(2,1)} %reduce-scatter.11.cloned.1.call-done.refs_1_.refs_3_, bf16[96,1664]{1,0:T(8,128)(2,1)} %reduce-scatter.9.cloned.1.call-done.refs_0_.refs_2_, ...), custom_call_target="tpu_custom_call" | custom-call | tf_op jit(solution)/shard_map/pallas_call | solution.py:283
  (158 shorter events, 60.5 us)
Async XLA Ops:
  7.2 142.6 %reduce-scatter.7.cloned.1.call-start = ((), (), s32[]{:S(2)}) async-start(), calls=%async_computation.5 | async-start | bytes 1966080 | tf_op jit(solution)/shard_map/qkv/reduce_scatter | solution.py:669
  7.2 13.1 %collective-permute-start = (bf16[96,1024]{1,0:T(8,128)(2,1)}, bf16[96,1024]{1,0:T(8,128)(2,1)S(1)}, u32[]{:S(2)}, u32[]{:S(2)}) collective-permute-start(bf16[96,1024]{1,0:T(8,128)(2,1)} %bitcast.73), channel_id=1, source_target_pairs={{0,2},{1,3},{2,0},{3,1},{4,6},{5,7},{6,4},{7,5},{8,10},{9,11},{10,... | collective-permute-start | bytes 589832 | tf_op jit(solution)/shard_map/inputs_gather/ppermute | solution.py:32
  10.2 10.8 %collective-permute-start.1 = (bf16[96,1024]{1,0:T(8,128)(2,1)}, bf16[96,1024]{1,0:T(8,128)(2,1)S(1)}, u32[]{:S(2)}, u32[]{:S(2)}) collective-permute-start(bf16[96,1024]{1,0:T(8,128)(2,1)} %bitcast.74), channel_id=1, source_target_pairs={{0,4},{1,5},{2,6},{3,7},{4,0},{5,1},{6,2},{7,3},{8,12},{9,13},{10,... | collective-permute-start | bytes 589832 | tf_op jit(solution)/shard_map/inputs_gather/ppermute | solution.py:32
  11.7 9.3 %collective-permute-start.2 = (bf16[96,1024]{1,0:T(8,128)(2,1)}, bf16[96,1024]{1,0:T(8,128)(2,1)S(1)}, u32[]{:S(2)}, u32[]{:S(2)}) collective-permute-start(bf16[96,1024]{1,0:T(8,128)(2,1)} %bitcast.75), channel_id=1, source_target_pairs={{0,6},{1,7},{2,4},{3,5},{4,2},{5,3},{6,0},{7,1},{8,14},{9,15},{10,... | collective-permute-start | bytes 589832 | tf_op jit(solution)/shard_map/inputs_gather/ppermute | solution.py:32
  11.8 9.8 %collective-permute-start.3 = (bf16[96,1024]{1,0:T(8,128)(2,1)}, bf16[96,1024]{1,0:T(8,128)(2,1)S(1)}, u32[]{:S(2)}, u32[]{:S(2)}) collective-permute-start(bf16[96,1024]{1,0:T(8,128)(2,1)} %bitcast.76), channel_id=1, source_target_pairs={{0,1},{1,0},{2,3},{3,2},{4,5},{5,4},{6,7},{7,6},{8,9},{9,8},{10,11... | collective-permute-start | bytes 589832 | tf_op jit(solution)/shard_map/inputs_gather/ppermute | solution.py:32
  17.8 17.1 %collective-permute-start.13 = (f32[1,5120]{1,0:T(1,128)S(1)}, f32[1,5120]{1,0:T(1,128)S(1)}, u32[]{:S(2)}, u32[]{:S(2)}) collective-permute-start(f32[1,5120]{1,0:T(1,128)S(1)} %pad_maximum_fusion.2), channel_id=1, source_target_pairs={{0,8},{8,16},{16,24},{24,0},{1,9},{9,17},{17,25},{25,1},{2,10},{10... | collective-permute-start | bytes 61448 | tf_op jit(solution)/shard_map/weight_sums/ppermute | solution.py:28
  21.5 13.4 %collective-permute-start.14 = (f32[1,5120]{1,0:T(1,128)S(1)}, f32[1,5120]{1,0:T(1,128)S(1)}, u32[]{:S(2)}, u32[]{:S(2)}) collective-permute-start(f32[1,5120]{1,0:T(1,128)S(1)} %pad_maximum_fusion.2), channel_id=1, source_target_pairs={{0,16},{8,24},{16,0},{24,8},{1,17},{9,25},{17,1},{25,9},{2,18},{10... | collective-permute-start | bytes 61448 | tf_op jit(solution)/shard_map/weight_sums/ppermute | solution.py:28
  24.2 10.8 %collective-permute-start.15 = (f32[1,5120]{1,0:T(1,128)S(1)}, f32[1,5120]{1,0:T(1,128)S(1)}, u32[]{:S(2)}, u32[]{:S(2)}) collective-permute-start(f32[1,5120]{1,0:T(1,128)S(1)} %pad_maximum_fusion.2), channel_id=1, source_target_pairs={{0,24},{8,0},{16,8},{24,16},{1,25},{9,1},{17,9},{25,17},{2,26},{10... | collective-permute-start | bytes 61448 | tf_op jit(solution)/shard_map/weight_sums/ppermute | solution.py:28
  34.4 133.7 %reduce-scatter.5.cloned.1.call-start = ((), (), s32[]{:S(2)}) async-start(), calls=%async_computation.4 | async-start | bytes 3932160 | tf_op jit(solution)/shard_map/up/reduce_scatter | solution.py:690
  35.1 6.1 %collective-permute-start.10 = (f32[16,128]{1,0:T(8,128)S(1)}, f32[16,128]{1,0:T(8,128)S(1)}, u32[]{:S(2)}, u32[]{:S(2)}) collective-permute-start(f32[16,128]{1,0:T(8,128)S(1)} %get-tuple-element.24), channel_id=1, source_target_pairs={{0,8},{8,16},{16,24},{24,0},{1,9},{9,17},{17,25},{25,1},{2,10},{10... | collective-permute-start | bytes 24584 | tf_op jit(solution)/shard_map/statistics/ppermute | solution.py:28
  35.8 8.2 %collective-permute-start.11 = (f32[16,128]{1,0:T(8,128)S(1)}, f32[16,128]{1,0:T(8,128)S(1)}, u32[]{:S(2)}, u32[]{:S(2)}) collective-permute-start(f32[16,128]{1,0:T(8,128)S(1)} %get-tuple-element.24), channel_id=1, source_target_pairs={{0,16},{8,24},{16,0},{24,8},{1,17},{9,25},{17,1},{25,9},{2,18},{10... | collective-permute-start | bytes 24584 | tf_op jit(solution)/shard_map/statistics/ppermute | solution.py:28
  36.9 7.1 %collective-permute-start.12 = (f32[16,128]{1,0:T(8,128)S(1)}, f32[16,128]{1,0:T(8,128)S(1)}, u32[]{:S(2)}, u32[]{:S(2)}) collective-permute-start(f32[16,128]{1,0:T(8,128)S(1)} %get-tuple-element.24), channel_id=1, source_target_pairs={{0,24},{8,0},{16,8},{24,16},{1,25},{9,1},{17,9},{25,17},{2,26},{10... | collective-permute-start | bytes 24584 | tf_op jit(solution)/shard_map/statistics/ppermute | solution.py:28
  39.8 13.8 %collective-permute-start.7 = (bf16[192,512]{1,0:T(8,128)(2,1)S(1)}, bf16[192,512]{1,0:T(8,128)(2,1)S(1)}, u32[]{:S(2)}, u32[]{:S(2)}) collective-permute-start(bf16[192,512]{1,0:T(8,128)(2,1)S(1)} %get-tuple-element.44), channel_id=1, source_target_pairs={{0,8},{8,16},{16,24},{24,0},{1,9},{9,17},{17,25},{25,1},{2,10},{10... | collective-permute-start | bytes 589832 | tf_op jit(solution)/shard_map/qkv/ppermute | solution.py:28
  39.9 26.2 %collective-permute-start.8 = (bf16[192,512]{1,0:T(8,128)(2,1)S(1)}, bf16[192,512]{1,0:T(8,128)(2,1)S(1)}, u32[]{:S(2)}, u32[]{:S(2)}) collective-permute-start(bf16[192,512]{1,0:T(8,128)(2,1)S(1)} %get-tuple-element.43), channel_id=1, source_target_pairs={{0,16},{8,24},{16,0},{24,8},{1,17},{9,25},{17,1},{25,9},{2,18},{10... | collective-permute-start | bytes 589832 | tf_op jit(solution)/shard_map/qkv/ppermute | solution.py:28
  41.2 24.9 %collective-permute-start.9 = (bf16[192,512]{1,0:T(8,128)(2,1)S(1)}, bf16[192,512]{1,0:T(8,128)(2,1)S(1)}, u32[]{:S(2)}, u32[]{:S(2)}) collective-permute-start(bf16[192,512]{1,0:T(8,128)(2,1)S(1)} %get-tuple-element.42), channel_id=1, source_target_pairs={{0,24},{8,0},{16,8},{24,16},{1,25},{9,1},{17,9},{25,17},{2,26},{10... | collective-permute-start | bytes 589832 | tf_op jit(solution)/shard_map/qkv/ppermute | solution.py:28
  74.8 150.1 %all-gather.3.cloned.1.call-start = ((), (), s32[]{:S(2)}) async-start(), calls=%async_computation.6 | async-start | bytes 1966080 | tf_op jit(solution)/shard_map/activated/all_gather | solution.py:705
  74.8 22.3 %collective-permute-start.16 = (bf16[768,128]{1,0:T(8,128)(2,1)S(1)}, bf16[768,128]{1,0:T(8,128)(2,1)S(1)}, u32[]{:S(2)}, u32[]{:S(2)}) collective-permute-start(bf16[768,128]{1,0:T(8,128)(2,1)S(1)} %queries.1.rest_0_.q_ref), channel_id=1, source_target_pairs={{0,8},{8,16},{16,24},{24,0},{1,9},{9,17},{17,25},{25,1},{2,10},{10... | collective-permute-start | bytes 589832 | tf_op jit(solution)/shard_map/queries/ppermute | solution.py:28
  89.9 18.8 %collective-permute-start.17 = (bf16[768,128]{1,0:T(8,128)(2,1)S(1)}, bf16[768,128]{1,0:T(8,128)(2,1)S(1)}, u32[]{:S(2)}, u32[]{:S(2)}) collective-permute-start(bf16[768,128]{1,0:T(8,128)(2,1)S(1)} %queries.1.rest_0_.q_ref), channel_id=1, source_target_pairs={{0,16},{8,24},{16,0},{24,8},{1,17},{9,25},{17,1},{25,9},{2,18},{10... | collective-permute-start | bytes 589832 | tf_op jit(solution)/shard_map/queries/ppermute | solution.py:28
  91.7 18.4 %collective-permute-start.18 = (bf16[768,128]{1,0:T(8,128)(2,1)S(1)}, bf16[768,128]{1,0:T(8,128)(2,1)S(1)}, u32[]{:S(2)}, u32[]{:S(2)}) collective-permute-start(bf16[768,128]{1,0:T(8,128)(2,1)S(1)} %queries.1.rest_0_.q_ref), channel_id=1, source_target_pairs={{0,24},{8,0},{16,8},{24,16},{1,25},{9,1},{17,9},{25,17},{2,26},{10... | collective-permute-start | bytes 589832 | tf_op jit(solution)/shard_map/queries/ppermute | solution.py:28
  131.4 25.9 %collective-permute-start.19 = (bf16[816,128]{1,0:T(8,128)(2,1)S(1)}, bf16[816,128]{1,0:T(8,128)(2,1)S(1)}, u32[]{:S(2)}, u32[]{:S(2)}) collective-permute-start(bf16[816,128]{1,0:T(8,128)(2,1)S(1)} %get-tuple-element.31), channel_id=1, source_target_pairs={{0,8},{8,16},{16,24},{24,0},{1,9},{9,17},{17,25},{25,1},{2,10},{10... | collective-permute-start | bytes 626696 | tf_op jit(solution)/shard_map/pages/ppermute | solution.py:28
  147.3 19.5 %collective-permute-start.20 = (bf16[816,128]{1,0:T(8,128)(2,1)S(1)}, bf16[816,128]{1,0:T(8,128)(2,1)S(1)}, u32[]{:S(2)}, u32[]{:S(2)}) collective-permute-start(bf16[816,128]{1,0:T(8,128)(2,1)S(1)} %get-tuple-element.32), channel_id=1, source_target_pairs={{0,16},{8,24},{16,0},{24,8},{1,17},{9,25},{17,1},{25,9},{2,18},{10... | collective-permute-start | bytes 626696 | tf_op jit(solution)/shard_map/pages/ppermute | solution.py:28
  147.3 19.5 %collective-permute-start.21 = (bf16[816,128]{1,0:T(8,128)(2,1)S(1)}, bf16[816,128]{1,0:T(8,128)(2,1)S(1)}, u32[]{:S(2)}, u32[]{:S(2)}) collective-permute-start(bf16[816,128]{1,0:T(8,128)(2,1)S(1)} %get-tuple-element.33), channel_id=1, source_target_pairs={{0,24},{8,0},{16,8},{24,16},{1,25},{9,1},{17,9},{25,17},{2,26},{10... | collective-permute-start | bytes 626696 | tf_op jit(solution)/shard_map/pages/ppermute | solution.py:28
  171.6 90.7 %all-gather.5.cloned.1.call-start = ((), (), s32[]{:S(2)}) async-start(), calls=%async_computation.7 | async-start | bytes 1966080 | tf_op jit(solution)/shard_map/activated/all_gather | solution.py:705
  172.1 121.9 %reduce-scatter.9.cloned.1.call-start = ((), (), s32[]{:S(2)}) async-start(), calls=%async_computation.8 | async-start | bytes 1597440 | tf_op jit(solution)/shard_map/next_0/reduce_scatter | solution.py:716
  172.2 15.8 %collective-permute-start.22 = (bf16[192,512]{1,0:T(8,128)(2,1)S(1)}, bf16[192,512]{1,0:T(8,128)(2,1)S(1)}, u32[]{:S(2)}, u32[]{:S(2)}) collective-permute-start(bf16[192,512]{1,0:T(8,128)(2,1)S(1)} %merge.3.refs_0_), channel_id=1, source_target_pairs={{0,8},{8,16},{16,24},{24,0},{1,9},{9,17},{17,25},{25,1},{2,10},{10... | collective-permute-start | bytes 589832 | tf_op jit(solution)/shard_map/merge/ppermute | solution.py:28
  180.6 22.9 %collective-permute-start.23 = (bf16[192,512]{1,0:T(8,128)(2,1)S(1)}, bf16[192,512]{1,0:T(8,128)(2,1)S(1)}, u32[]{:S(2)}, u32[]{:S(2)}) collective-permute-start(bf16[192,512]{1,0:T(8,128)(2,1)S(1)} %merge.3.refs_0_), channel_id=1, source_target_pairs={{0,16},{8,24},{16,0},{24,8},{1,17},{9,25},{17,1},{25,9},{2,18},{10... | collective-permute-start | bytes 589832 | tf_op jit(solution)/shard_map/merge/ppermute | solution.py:28
  182.6 20.9 %collective-permute-start.24 = (bf16[192,512]{1,0:T(8,128)(2,1)S(1)}, bf16[192,512]{1,0:T(8,128)(2,1)S(1)}, u32[]{:S(2)}, u32[]{:S(2)}) collective-permute-start(bf16[192,512]{1,0:T(8,128)(2,1)S(1)} %merge.3.refs_0_), channel_id=1, source_target_pairs={{0,24},{8,0},{16,8},{24,16},{1,25},{9,1},{17,9},{25,17},{2,26},{10... | collective-permute-start | bytes 589832 | tf_op jit(solution)/shard_map/merge/ppermute | solution.py:28
  233.2 6.1 %collective-permute-start.27 = (bf16[48,1024]{1,0:T(8,128)(2,1)S(1)}, bf16[48,1024]{1,0:T(8,128)(2,1)S(1)}, u32[]{:S(2)}, u32[]{:S(2)}) collective-permute-start(bf16[48,1024]{1,0:T(8,128)(2,1)S(1)} %get-tuple-element.50), channel_id=1, source_target_pairs={{0,4},{1,5},{2,6},{3,7},{4,0},{5,1},{6,2},{7,3},{8,12},{9,13},{10,... | collective-permute-start | bytes 294920 | tf_op jit(solution)/shard_map/down_0/ppermute | solution.py:32
  240.7 5.7 %collective-permute-start.29 = (bf16[48,1024]{1,0:T(8,128)(2,1)S(1)}, bf16[48,1024]{1,0:T(8,128)(2,1)S(1)}, u32[]{:S(2)}, u32[]{:S(2)}) collective-permute-start(bf16[48,1024]{1,0:T(8,128)(2,1)S(1)} %fusion.7.refs_0_), channel_id=1, source_target_pairs={{0,2},{1,3},{2,0},{3,1},{4,6},{5,7},{6,4},{7,5},{8,10},{9,11},{10,... | collective-permute-start | bytes 294920 | tf_op jit(solution)/shard_map/next_0/ppermute | solution.py:32
  256.0 69.8 %reduce-scatter.11.cloned.1.call-start = ((), (), s32[]{:S(2)}) async-start(), calls=%async_computation.9 | async-start | bytes 1597440 | tf_op jit(solution)/shard_map/next_1/reduce_scatter | solution.py:716
  271.2 5.8 %collective-permute-start.38 = (bf16[48,1024]{1,0:T(8,128)(2,1)S(1)}, bf16[48,1024]{1,0:T(8,128)(2,1)S(1)}, u32[]{:S(2)}, u32[]{:S(2)}) collective-permute-start(bf16[48,1024]{1,0:T(8,128)(2,1)S(1)} %get-tuple-element.47), channel_id=1, source_target_pairs={{0,4},{1,5},{2,6},{3,7},{4,0},{5,1},{6,2},{7,3},{8,12},{9,13},{10,... | collective-permute-start | bytes 294920 | tf_op jit(solution)/shard_map/down_1/ppermute | solution.py:32
  278.3 5.6 %collective-permute-start.40 = (bf16[48,1024]{1,0:T(8,128)(2,1)S(1)}, bf16[48,1024]{1,0:T(8,128)(2,1)S(1)}, u32[]{:S(2)}, u32[]{:S(2)}) collective-permute-start(bf16[48,1024]{1,0:T(8,128)(2,1)S(1)} %fusion.3.refs_0_), channel_id=1, source_target_pairs={{0,2},{1,3},{2,0},{3,1},{4,6},{5,7},{6,4},{7,5},{8,10},{9,11},{10,... | collective-permute-start | bytes 294920 | tf_op jit(solution)/shard_map/next_1/ppermute | solution.py:32
  (31 other events, 235.4 us)
Sparse Core Ops, SparseCore 0:
  34.5 47.8 reduce-scatter.6
  84.7 79.3 reduce-scatter.4
  171.7 53.1 all-gather.2
  226.3 35.8 all-gather.4
  264.4 29.5 reduce-scatter.8
  296.3 29.4 reduce-scatter.10

commit v4 on v3

--- a/solution.py
+++ b/solution.py
@@ -55,6 +55,18 @@
 
 def after(value, *others):
     return lax.optimization_barrier((value,) + others)[0]
+
+
+def line_gather(block):
+    size = lax.axis_size("req")
+    rights, lefts = [], []
+    right = left = block
+    for t in range(1, size):
+        right = lax.ppermute(right, "req", [(k, k + 1) for k in range(t - 1, size - 1)])
+        left = lax.ppermute(left, "req", [(k + 1, k) for k in range(size - t)])
+        rights.append(right)
+        lefts.append(left)
+    return rights, lefts
 
 
 def eye_mask(rows):
@@ -164,7 +176,7 @@
     rows, width = pieces[0].shape
     columns = weight.shape[1]
     ranks = lax.axis_size("req")
-    tile = math.gcd(columns, 256)
+    tile = math.gcd(columns, 512)
     place = jnp.stack([lax.axis_index("mlp"), lax.axis_index("req")]).astype(jnp.int32)
     out = jax.ShapeDtypeStruct((count * rows, columns + LANES), BF16)
     return pl.pallas_call(
@@ -273,38 +285,42 @@
         out[s] = (total * lax.rsqrt(square * (1.0 / (width * ranks)) + EPSILON)).astype(BF16)
 
 
-def finish(totals, sums, first, width):
+def finish(totals, sums, width):
     rows = totals[0].shape[0]
     columns = totals[0].shape[1] - LANES
-    tile = math.gcd(math.gcd(columns, 512), first)
     ranks = lax.axis_size("req")
     rank = lax.axis_index("req").astype(jnp.int32).reshape(1)
     totals = [in_hbm(total) for total in totals]
     return pl.pallas_call(
         functools.partial(finish_kernel, ranks, width),
         out_shape=jax.ShapeDtypeStruct((STEPS, rows, columns), BF16),
-        grid=(columns // tile,),
+        grid=(1,),
         in_specs=[pl.BlockSpec(memory_space=pltpu.SMEM)]
-        + [pl.BlockSpec((rows, tile), lambda n: (0, n))] * STEPS
+        + [pl.BlockSpec((rows, columns), lambda n: (0, 0))] * STEPS
         + [pl.BlockSpec((rows, LANES), lambda n: (0, columns // LANES))] * STEPS
-        + [pl.BlockSpec((sums.shape[0], tile), lambda n: (0, first // tile + n))],
-        out_specs=pl.BlockSpec((STEPS, rows, tile), lambda n: (0, 0, n)),
+        + [full_block(sums.shape)],
+        out_specs=full_block((STEPS, rows, columns)),
         compiler_params=pltpu.CompilerParams(vmem_limit_bytes=24 << 20),
     )(rank, *totals, *totals, sums)
 
 
 def update_kernel(ranks, step, place_ref, hidden_ref, down_ref, dense_ref, *refs):
-    attended, (mine, other, heads) = refs[:ranks], refs[ranks:]
+    attended, (mine, other, heads) = refs[: 2 * ranks - 1], refs[2 * ranks - 1 :]
     rows = hidden_ref.shape[0] // ranks
     rank, core = place_ref[0], place_ref[1]
 
     @pl.when(pl.program_id(0) == 0)
     def _():
-        for d in range(ranks):
-            owner = lax.rem(rank + ranks - d, ranks)
-            heads[pl.ds(pl.multiple_of(owner * rows, rows), rows), :] = attended[d][
-                step * rows : (step + 1) * rows, :
-            ]
+        def place(owner, piece):
+            at = pl.ds(pl.multiple_of(owner * rows, rows), rows)
+            heads[at, :] = piece[step * rows : (step + 1) * rows, :]
+
+        place(rank, attended[0])
+        for d in range(1, ranks):
+            pl.when(rank >= d)(functools.partial(place, rank - d, attended[d]))
+            pl.when(rank + d < ranks)(
+                functools.partial(place, rank + d, attended[ranks + d - 1])
+            )
 
     result = jnp.dot(hidden_ref[...], down_ref[...], preferred_element_type=F32) + jnp.dot(
         heads[...], dense_ref[...], preferred_element_type=F32
@@ -321,7 +337,7 @@
     ranks = lax.axis_size("req")
     rows, columns = hidden.shape
     head_width, width = dense_weight.shape
-    tile = min(256, width)
+    tile = math.gcd(512, width)
     place = jnp.stack([lax.axis_index("req"), lax.axis_index("mlp") % 2]).astype(jnp.int32)
     shape = jax.ShapeDtypeStruct((ranks, rows // ranks // 2, width), BF16)
     out_block = pl.BlockSpec((ranks, rows // ranks // 2, tile), lambda n: (0, 0, n))
@@ -335,7 +351,7 @@
             pl.BlockSpec((columns, tile), lambda n: (0, n)),
             pl.BlockSpec((head_width, tile), lambda n: (0, n)),
         ]
-        + [full_block(attended[0].shape)] * ranks,
+        + [full_block(attended[0].shape)] * (2 * ranks - 1),
         out_specs=(out_block, out_block),
         scratch_shapes=[pltpu.VMEM((rows, head_width), BF16)],
         compiler_params=pltpu.CompilerParams(vmem_limit_bytes=40 << 20),
@@ -699,7 +715,8 @@
             key_value, stats, sums, tables, heads, parts, requests
         )
         attended = merge(queries, keys, values, parent_wide, pieces, heads, parts, requests)
-        attended_all = exchange(attended)
+        rights, lefts = line_gather(attended)
+        attended_all = [attended, *rights, *lefts]
     with jax.named_scope("activated"):
         activated = activate(after(up, attended), stats, sums, up_first, beams)
         activated = [lax.all_gather(own, "req", axis=0, tiled=True) for own in activated]
@@ -714,7 +731,7 @@
             if s + 1 < STEPS:
                 activated[s + 1] = after(activated[s + 1], partial)
             totals.append(lax.psum_scatter(partial, "req", scatter_dimension=0, tiled=True))
-    return jnp.stack(layers), finish(totals, sums, next_first, width)
+    return jnp.stack(layers), finish(totals, sums[:, next_first:], width)
 
 
 def solution(mesh):

time: 337 us -> 333 us (0.988)
  Pallas kernels: 62 us -> 57.4 us
  starting transfers between devices: 82.2 us -> 86.7 us
  waiting for transfers between devices: 158 us -> 154 us
    ppermute x0 -> x6, waiting for transfers between devices: none -> 36.9 us  [the longest x3 33.4 us: line_gather(): left = lax.ppermute(left, 'req', [(k + 1, k) for k in range(size - t)])]
    all_gather x2, waiting for transfers between devices: 27.6 us -> 5.51 us  [shards(): lax.all_gather(own, 'req', axis=0, tiled=True)]
    ppermute x18 -> x15, waiting for transfers between devices: 74.2 us -> 53.9 us  [rotated(): lax.ppermute(array, axis, [(k, (k + distance) % size) for k in range(size)])]
    ppermute x0 -> x6, starting transfers between devices: none -> 15.4 us  [the longest x3 11.6 us: line_gather(): lax.ppermute(right, 'req', [(k, k + 1) for k in range(t - 1, size - 1)])]
    ppermute x18 -> x15, starting transfers between devices: 61.7 us -> 50.8 us  [rotated(): lax.ppermute(array, axis, [(k, (k + distance) % size) for k in range(size)])]
  transfers between devices with their start and end apart: 53 -> 56, of which waited for: 28 -> 31; matrix products, arithmetic and copies ran while one was open for 5% -> 5% of each run, Pallas kernels for 17% -> 16%
where the time goes in v4:
time: 333 us
  waiting for transfers between devices  154 us (46%)
  starting transfers between devices  86.7 us (26%)
  Pallas kernels  57.4 us (17%)
  between operations  14.7 us (4%)
  matrix products  11.9 us (4%)
  local copies, waits for them, and re-layouts  5.14 us (2%)
    ppermute x15, waiting for transfers between devices, rotated(): lax.ppermute(array, axis, [(k, (k + distance) % size) for k in range(size)])  53.9 us
    ppermute x15, starting transfers between devices, rotated(): lax.ppermute(array, axis, [(k, (k + distance) % size) for k in range(size)])  50.8 us
    reduce_scatter x2, waiting for transfers between devices, shards(): lax.psum_scatter(partial, 'req', scatter_dimension=0, tiled=True)  33.6 us
    ppermute x3, waiting for transfers between devices, line_gather(): left = lax.ppermute(left, 'req', [(k + 1, k) for k in range(size - t)])  33.4 us
    ppermute x29, waiting for transfers between devices, flipped(): lax.ppermute(array, axis, [(k, k ^ bits) for k in range(lax.axis_size(axi...  23.5 us
    pallas_call x1, Pallas kernels, page_attention(): pl.pallas_call(functools.partial(page_kernel, heads, ranks, own_rows), ou...  21.2 us
    ppermute x29, starting transfers between devices, flipped(): lax.ppermute(array, axis, [(k, k ^ bits) for k in range(lax.axis_size(axi...  20.2 us
    ppermute x3, starting transfers between devices, line_gather(): lax.ppermute(right, 'req', [(k, k + 1) for k in range(t - 1, size - 1)])  11.6 us
  transfers between devices with their start and end apart: 56, of which 31 were waited for; matrix products, arithmetic and copies ran while one was open for 5% of the time, Pallas kernels for 16%

profile of v4, /device:TPU:0, one launch (start us, length us, event | category | flops | bytes accessed | tf_op | source)
XLA Modules:
  0.0 332.6 jit_solution(6348906964890166225)
XLA Ops:
  7.2 3.0 collective-permute-start
  13.6 3.0 fusion.17
  21.5 2.7 collective-permute-start.14
  25.6 7.6 %qkv.1 = (bf16[768,512]{1,0:T(8,128)(2,1)S(1)}, bf16[768,1024]{1,0:T(8,128)(2,1)}, f32[16,128]{1,0:T(8,128)S(1)}, bf16[768,1024]{1,0:T(8,128)(2,1)S(1)}) custom-call(s32[1]{0:T(128)} %bitcast.3.place_ref, f32[2,1024]{1,0:T(2,128)S(1)} %slice.52.gain_ref, bf16[1024,1536]{1,0:T(8,128)(2,1)} %weight_ref.3, bf16[96,1024]{1,0:T(8,128)(2,1)S(1)} %bitcast.77, ...), custom_call_target="tpu_custom_call" | custom-call | flops 2415919104 | bytes 8650752 | tf_op jit(solution)/shard_map/qkv/pallas_call | solution.py:117
  36.9 2.8 collective-permute-start.12
  41.2 2.8 collective-permute-start.9
  44.5 9.1 %collective-permute-done.7.refs_0_ = bf16[192,512]{1,0:T(8,128)(2,1)S(1)} collective-permute-done((bf16[192,512]{1,0:T(8,128)(2,1)S(1)}, bf16[192,512]{1,0:T(8,128)(2,1)S(1)}, u32[]{:S(2)}, u32[]{:S(2)}) %collective-permute-start.7) | collective-permute-done | bytes 196640 | tf_op jit(solution)/shard_map/qkv/ppermute | solution.py:28
  53.6 12.4 %collective-permute-done.8.refs_1_ = bf16[192,512]{1,0:T(8,128)(2,1)S(1)} collective-permute-done((bf16[192,512]{1,0:T(8,128)(2,1)S(1)}, bf16[192,512]{1,0:T(8,128)(2,1)S(1)}, u32[]{:S(2)}, u32[]{:S(2)}) %collective-permute-start.8) | collective-permute-done | bytes 196640 | tf_op jit(solution)/shard_map/qkv/ppermute | solution.py:28
  67.0 7.7 %convolution_convert_fusion = bf16[768,2048]{1,0:T(8,128)(2,1)} fusion(bf16[768,1024]{1,0:T(8,128)(2,1)} %copy-done.5, bf16[1024,2048]{1,0:T(8,128)(2,1)} %param.15), kind=kOutput, calls=%fused_computation | convolution fusion | flops 3222798336 | bytes 8912896 | tf_op jit(solution)/shard_map/up/dot_general | solution.py:705
  74.8 15.1 %collective-permute-start.16 = (bf16[768,128]{1,0:T(8,128)(2,1)S(1)}, bf16[768,128]{1,0:T(8,128)(2,1)S(1)}, u32[]{:S(2)}, u32[]{:S(2)}) collective-permute-start(bf16[768,128]{1,0:T(8,128)(2,1)S(1)} %queries.1.rest_0_.q_ref), channel_id=1, source_target_pairs={{0,8},{8,16},{16,24},{24,0},{1,9},{9,17},{17,25},{25,1},{2,10},{10... | collective-permute-start | bytes 589832 | tf_op jit(solution)/shard_map/queries/ppermute | solution.py:28
  92.4 4.7 %collective-permute-done.16.rest_1_ = bf16[768,128]{1,0:T(8,128)(2,1)S(1)} collective-permute-done((bf16[768,128]{1,0:T(8,128)(2,1)S(1)}, bf16[768,128]{1,0:T(8,128)(2,1)S(1)}, u32[]{:S(2)}, u32[]{:S(2)}) %collective-permute-start.16) | collective-permute-done | bytes 196640 | tf_op jit(solution)/shard_map/queries/ppermute | solution.py:28
  97.1 11.6 %collective-permute-done.17.rest_2_ = bf16[768,128]{1,0:T(8,128)(2,1)S(1)} collective-permute-done((bf16[768,128]{1,0:T(8,128)(2,1)S(1)}, bf16[768,128]{1,0:T(8,128)(2,1)S(1)}, u32[]{:S(2)}, u32[]{:S(2)}) %collective-permute-start.17) | collective-permute-done | bytes 196640 | tf_op jit(solution)/shard_map/queries/ppermute | solution.py:28
  110.2 21.2 %pages.1 = (bf16[816,128]{1,0:T(8,128)(2,1)S(1)}, bf16[816,128]{1,0:T(8,128)(2,1)S(1)}, bf16[816,128]{1,0:T(8,128)(2,1)S(1)}, bf16[816,128]{1,0:T(8,128)(2,1)S(1)}) custom-call(s32[2,64]{1,0:T(2,128)S(1)} %copy-done.3, s32[48]{0:T(128)S(1)} %copy-done.4, s32[1]{0:T(128)} %bitcast.1.rank_ref.me_ref, bf16[64,128,512]{2,1,0:T(8,128)(2,1)} %k_ref.1, ...), custom_call_target="tpu_custom_call" | custom-call | flops 268435456 | bytes 67108864 | tf_op jit(solution)/shard_map/pages/pallas_call | solution.py:548
  131.4 15.9 %collective-permute-start.19 = (bf16[816,128]{1,0:T(8,128)(2,1)S(1)}, bf16[816,128]{1,0:T(8,128)(2,1)S(1)}, u32[]{:S(2)}, u32[]{:S(2)}) collective-permute-start(bf16[816,128]{1,0:T(8,128)(2,1)S(1)} %get-tuple-element.31), channel_id=1, source_target_pairs={{0,8},{8,16},{16,24},{24,0},{1,9},{9,17},{17,25},{25,1},{2,10},{10... | collective-permute-start | bytes 626696 | tf_op jit(solution)/shard_map/pages/ppermute | solution.py:28
  147.3 2.4 collective-permute-start.21
  152.3 5.0 %collective-permute-done.19.rest_1_ = bf16[816,128]{1,0:T(8,128)(2,1)S(1)} collective-permute-done((bf16[816,128]{1,0:T(8,128)(2,1)S(1)}, bf16[816,128]{1,0:T(8,128)(2,1)S(1)}, u32[]{:S(2)}, u32[]{:S(2)}) %collective-permute-start.19) | collective-permute-done | bytes 208928 | tf_op jit(solution)/shard_map/pages/ppermute | solution.py:28
  157.4 9.5 %collective-permute-done.20.rest_2_ = bf16[816,128]{1,0:T(8,128)(2,1)S(1)} collective-permute-done((bf16[816,128]{1,0:T(8,128)(2,1)S(1)}, bf16[816,128]{1,0:T(8,128)(2,1)S(1)}, u32[]{:S(2)}, u32[]{:S(2)}) %collective-permute-start.20) | collective-permute-done | bytes 208928 | tf_op jit(solution)/shard_map/pages/ppermute | solution.py:28
  169.2 2.3 activated.1
  172.2 10.2 %collective-permute-start.22 = (bf16[192,512]{1,0:T(8,128)(2,1)S(1)}, bf16[192,512]{1,0:T(8,128)(2,1)S(1)}, u32[]{:S(2)}, u32[]{:S(2)}) collective-permute-start(bf16[192,512]{1,0:T(8,128)(2,1)S(1)} %merge.3.refs_0_), channel_id=1, source_target_pairs={{0,8},{8,16},{16,24},{1,9},{9,17},{17,25},{2,10},{10,18},{18,26},{... | collective-permute-start | bytes 589832 | tf_op jit(solution)/shard_map/merge/ppermute | solution.py:65
  183.7 3.5 %collective-permute-done.22.refs_1_ = bf16[192,512]{1,0:T(8,128)(2,1)S(1)} collective-permute-done((bf16[192,512]{1,0:T(8,128)(2,1)S(1)}, bf16[192,512]{1,0:T(8,128)(2,1)S(1)}, u32[]{:S(2)}, u32[]{:S(2)}) %collective-permute-start.22) | collective-permute-done | bytes 196640 | tf_op jit(solution)/shard_map/merge/ppermute | solution.py:65
  187.9 10.6 %collective-permute-done.25.refs_4_ = bf16[192,512]{1,0:T(8,128)(2,1)S(1)} collective-permute-done((bf16[192,512]{1,0:T(8,128)(2,1)S(1)}, bf16[192,512]{1,0:T(8,128)(2,1)S(1)}, u32[]{:S(2)}, u32[]{:S(2)}) %collective-permute-start.25) | collective-permute-done | bytes 196640 | tf_op jit(solution)/shard_map/merge/ppermute | solution.py:66
  200.5 14.6 %collective-permute-done.26.refs_5_ = bf16[192,512]{1,0:T(8,128)(2,1)S(1)} collective-permute-done((bf16[192,512]{1,0:T(8,128)(2,1)S(1)}, bf16[192,512]{1,0:T(8,128)(2,1)S(1)}, u32[]{:S(2)}, u32[]{:S(2)}) %collective-permute-start.26) | collective-permute-done | bytes 196640 | tf_op jit(solution)/shard_map/merge/ppermute | solution.py:66
  216.5 8.1 %collective-permute-done.27.refs_6_ = bf16[192,512]{1,0:T(8,128)(2,1)S(1)} collective-permute-done((bf16[192,512]{1,0:T(8,128)(2,1)S(1)}, bf16[192,512]{1,0:T(8,128)(2,1)S(1)}, u32[]{:S(2)}, u32[]{:S(2)}) %collective-permute-start.27) | collective-permute-done | bytes 196640 | tf_op jit(solution)/shard_map/merge/ppermute | solution.py:66
  224.7 4.8 %down_0.1 = (bf16[4,48,1024]{2,1,0:T(8,128)(2,1)S(1)}, bf16[4,48,1024]{2,1,0:T(8,128)(2,1)S(1)}) custom-call(s32[2]{0:T(128)S(1)} %pad_add_fusion.place_ref, bf16[384,2048]{1,0:T(8,128)(2,1)} %all-gather.3.cloned.1.call-done.hidden_ref, bf16[2048,1024]{1,0:T(8,128)(2,1)} %down_ref.3, bf16[512,1024]{1,0:T(8,128)(2,1)} %dense_ref.3, ...), custom_call_target="tpu_custom_call" | custom-call | flops 2013265920 | bytes 7208960 | tf_op jit(solution)/shard_map/down_0/pallas_call | solution.py:344
  243.1 2.1 collective-permute-done.32.refs_1_
  248.7 5.3 %next_0.1 = bf16[384,1664]{1,0:T(8,128)(2,1)} custom-call(s32[2]{0:T(128)S(1)} %pad_add_fusion.1.place_ref, f32[1,1024]{1,0:T(1,128)S(1)} %get-tuple-element.51.gain_ref, bf16[1024,1536]{1,0:T(8,128)(2,1)} %weight_ref.5, bf16[48,1024]{1,0:T(8,128)(2,1)S(1)} %fusion.7.refs_0_, bf16[48,1024]{1,0:T(8,128)(2,1)S(1)} %collective-permute-done.32.refs_1_, ...), custom_call_target="tpu_custom_call" | custom-call | flops 1207959552 | bytes 5111808 | tf_op jit(solution)/shard_map/next_0/pallas_call | solution.py:182
  254.0 5.5 %all-gather.5.cloned.1.call-done.hidden_ref = bf16[384,2048]{1,0:T(8,128)(2,1)} async-done(((bf16[96,2048]{1,0:T(8,128)(2,1)}), bf16[384,2048]{1,0:T(8,128)(2,1)}) %all-gather.5.cloned.1.call-update) | async-done | bytes 1572880 | tf_op jit(solution)/shard_map/activated/all_gather | solution.py:722
  259.6 4.8 %down_1.1 = (bf16[4,48,1024]{2,1,0:T(8,128)(2,1)S(1)}, bf16[4,48,1024]{2,1,0:T(8,128)(2,1)S(1)}) custom-call(s32[2]{0:T(128)S(1)} %pad_add_fusion.place_ref, bf16[384,2048]{1,0:T(8,128)(2,1)} %all-gather.5.cloned.1.call-done.hidden_ref, bf16[2048,1024]{1,0:T(8,128)(2,1)} %down_ref.3, bf16[512,1024]{1,0:T(8,128)(2,1)} %dense_ref.3, ...), custom_call_target="tpu_custom_call" | custom-call | flops 2013265920 | bytes 7208960 | tf_op jit(solution)/shard_map/down_1/pallas_call | solution.py:344
  271.2 2.4 collective-permute-done.41
  283.5 5.3 %next_1.1 = bf16[384,1664]{1,0:T(8,128)(2,1)} custom-call(s32[2]{0:T(128)S(1)} %pad_add_fusion.1.place_ref, f32[1,1024]{1,0:T(1,128)S(1)} %get-tuple-element.51.gain_ref, bf16[1024,1536]{1,0:T(8,128)(2,1)} %weight_ref.5, bf16[48,1024]{1,0:T(8,128)(2,1)S(1)} %fusion.3.refs_0_, bf16[48,1024]{1,0:T(8,128)(2,1)S(1)} %collective-permute-done.43.refs_1_, ...), custom_call_target="tpu_custom_call" | custom-call | flops 1207959552 | bytes 5111808 | tf_op jit(solution)/shard_map/next_1/pallas_call | solution.py:182
  291.4 31.8 %reduce-scatter.11.cloned.1.call-done.refs_1_.refs_3_ = bf16[96,1664]{1,0:T(8,128)(2,1)} async-done(((bf16[384,1664]{1,0:T(8,128)(2,1)}), bf16[96,1664]{1,0:T(8,128)(2,1)}) %reduce-scatter.11.cloned.1.call-update) | async-done | bytes 319504 | tf_op jit(solution)/shard_map/next_1/reduce_scatter | solution.py:733
  323.2 2.5 shard_map.131
  (165 shorter events, 67.2 us)
Async XLA Ops:
  7.2 142.6 %reduce-scatter.7.cloned.1.call-start = ((), (), s32[]{:S(2)}) async-start(), calls=%async_computation.5 | async-start | bytes 1966080 | tf_op jit(solution)/shard_map/qkv/reduce_scatter | solution.py:685
  7.2 13.1 %collective-permute-start = (bf16[96,1024]{1,0:T(8,128)(2,1)}, bf16[96,1024]{1,0:T(8,128)(2,1)S(1)}, u32[]{:S(2)}, u32[]{:S(2)}) collective-permute-start(bf16[96,1024]{1,0:T(8,128)(2,1)} %bitcast.73), channel_id=1, source_target_pairs={{0,2},{1,3},{2,0},{3,1},{4,6},{5,7},{6,4},{7,5},{8,10},{9,11},{10,... | collective-permute-start | bytes 589832 | tf_op jit(solution)/shard_map/inputs_gather/ppermute | solution.py:32
  10.2 10.8 %collective-permute-start.1 = (bf16[96,1024]{1,0:T(8,128)(2,1)}, bf16[96,1024]{1,0:T(8,128)(2,1)S(1)}, u32[]{:S(2)}, u32[]{:S(2)}) collective-permute-start(bf16[96,1024]{1,0:T(8,128)(2,1)} %bitcast.74), channel_id=1, source_target_pairs={{0,4},{1,5},{2,6},{3,7},{4,0},{5,1},{6,2},{7,3},{8,12},{9,13},{10,... | collective-permute-start | bytes 589832 | tf_op jit(solution)/shard_map/inputs_gather/ppermute | solution.py:32
  11.7 9.3 %collective-permute-start.2 = (bf16[96,1024]{1,0:T(8,128)(2,1)}, bf16[96,1024]{1,0:T(8,128)(2,1)S(1)}, u32[]{:S(2)}, u32[]{:S(2)}) collective-permute-start(bf16[96,1024]{1,0:T(8,128)(2,1)} %bitcast.75), channel_id=1, source_target_pairs={{0,6},{1,7},{2,4},{3,5},{4,2},{5,3},{6,0},{7,1},{8,14},{9,15},{10,... | collective-permute-start | bytes 589832 | tf_op jit(solution)/shard_map/inputs_gather/ppermute | solution.py:32
  11.8 9.8 %collective-permute-start.3 = (bf16[96,1024]{1,0:T(8,128)(2,1)}, bf16[96,1024]{1,0:T(8,128)(2,1)S(1)}, u32[]{:S(2)}, u32[]{:S(2)}) collective-permute-start(bf16[96,1024]{1,0:T(8,128)(2,1)} %bitcast.76), channel_id=1, source_target_pairs={{0,1},{1,0},{2,3},{3,2},{4,5},{5,4},{6,7},{7,6},{8,9},{9,8},{10,11... | collective-permute-start | bytes 589832 | tf_op jit(solution)/shard_map/inputs_gather/ppermute | solution.py:32
  17.8 17.1 %collective-permute-start.13 = (f32[1,5120]{1,0:T(1,128)S(1)}, f32[1,5120]{1,0:T(1,128)S(1)}, u32[]{:S(2)}, u32[]{:S(2)}) collective-permute-start(f32[1,5120]{1,0:T(1,128)S(1)} %pad_maximum_fusion.2), channel_id=1, source_target_pairs={{0,8},{8,16},{16,24},{24,0},{1,9},{9,17},{17,25},{25,1},{2,10},{10... | collective-permute-start | bytes 61448 | tf_op jit(solution)/shard_map/weight_sums/ppermute | solution.py:28
  21.5 13.4 %collective-permute-start.14 = (f32[1,5120]{1,0:T(1,128)S(1)}, f32[1,5120]{1,0:T(1,128)S(1)}, u32[]{:S(2)}, u32[]{:S(2)}) collective-permute-start(f32[1,5120]{1,0:T(1,128)S(1)} %pad_maximum_fusion.2), channel_id=1, source_target_pairs={{0,16},{8,24},{16,0},{24,8},{1,17},{9,25},{17,1},{25,9},{2,18},{10... | collective-permute-start | bytes 61448 | tf_op jit(solution)/shard_map/weight_sums/ppermute | solution.py:28
  24.2 10.8 %collective-permute-start.15 = (f32[1,5120]{1,0:T(1,128)S(1)}, f32[1,5120]{1,0:T(1,128)S(1)}, u32[]{:S(2)}, u32[]{:S(2)}) collective-permute-start(f32[1,5120]{1,0:T(1,128)S(1)} %pad_maximum_fusion.2), channel_id=1, source_target_pairs={{0,24},{8,0},{16,8},{24,16},{1,25},{9,1},{17,9},{25,17},{2,26},{10... | collective-permute-start | bytes 61448 | tf_op jit(solution)/shard_map/weight_sums/ppermute | solution.py:28
  34.4 133.7 %reduce-scatter.5.cloned.1.call-start = ((), (), s32[]{:S(2)}) async-start(), calls=%async_computation.4 | async-start | bytes 3932160 | tf_op jit(solution)/shard_map/up/reduce_scatter | solution.py:706
  35.1 6.1 %collective-permute-start.10 = (f32[16,128]{1,0:T(8,128)S(1)}, f32[16,128]{1,0:T(8,128)S(1)}, u32[]{:S(2)}, u32[]{:S(2)}) collective-permute-start(f32[16,128]{1,0:T(8,128)S(1)} %get-tuple-element.24), channel_id=1, source_target_pairs={{0,8},{8,16},{16,24},{24,0},{1,9},{9,17},{17,25},{25,1},{2,10},{10... | collective-permute-start | bytes 24584 | tf_op jit(solution)/shard_map/statistics/ppermute | solution.py:28
  35.8 8.2 %collective-permute-start.11 = (f32[16,128]{1,0:T(8,128)S(1)}, f32[16,128]{1,0:T(8,128)S(1)}, u32[]{:S(2)}, u32[]{:S(2)}) collective-permute-start(f32[16,128]{1,0:T(8,128)S(1)} %get-tuple-element.24), channel_id=1, source_target_pairs={{0,16},{8,24},{16,0},{24,8},{1,17},{9,25},{17,1},{25,9},{2,18},{10... | collective-permute-start | bytes 24584 | tf_op jit(solution)/shard_map/statistics/ppermute | solution.py:28
  36.9 7.1 %collective-permute-start.12 = (f32[16,128]{1,0:T(8,128)S(1)}, f32[16,128]{1,0:T(8,128)S(1)}, u32[]{:S(2)}, u32[]{:S(2)}) collective-permute-start(f32[16,128]{1,0:T(8,128)S(1)} %get-tuple-element.24), channel_id=1, source_target_pairs={{0,24},{8,0},{16,8},{24,16},{1,25},{9,1},{17,9},{25,17},{2,26},{10... | collective-permute-start | bytes 24584 | tf_op jit(solution)/shard_map/statistics/ppermute | solution.py:28
  39.8 13.8 %collective-permute-start.7 = (bf16[192,512]{1,0:T(8,128)(2,1)S(1)}, bf16[192,512]{1,0:T(8,128)(2,1)S(1)}, u32[]{:S(2)}, u32[]{:S(2)}) collective-permute-start(bf16[192,512]{1,0:T(8,128)(2,1)S(1)} %get-tuple-element.44), channel_id=1, source_target_pairs={{0,8},{8,16},{16,24},{24,0},{1,9},{9,17},{17,25},{25,1},{2,10},{10... | collective-permute-start | bytes 589832 | tf_op jit(solution)/shard_map/qkv/ppermute | solution.py:28
  39.9 26.2 %collective-permute-start.8 = (bf16[192,512]{1,0:T(8,128)(2,1)S(1)}, bf16[192,512]{1,0:T(8,128)(2,1)S(1)}, u32[]{:S(2)}, u32[]{:S(2)}) collective-permute-start(bf16[192,512]{1,0:T(8,128)(2,1)S(1)} %get-tuple-element.43), channel_id=1, source_target_pairs={{0,16},{8,24},{16,0},{24,8},{1,17},{9,25},{17,1},{25,9},{2,18},{10... | collective-permute-start | bytes 589832 | tf_op jit(solution)/shard_map/qkv/ppermute | solution.py:28
  41.2 24.9 %collective-permute-start.9 = (bf16[192,512]{1,0:T(8,128)(2,1)S(1)}, bf16[192,512]{1,0:T(8,128)(2,1)S(1)}, u32[]{:S(2)}, u32[]{:S(2)}) collective-permute-start(bf16[192,512]{1,0:T(8,128)(2,1)S(1)} %get-tuple-element.42), channel_id=1, source_target_pairs={{0,24},{8,0},{16,8},{24,16},{1,25},{9,1},{17,9},{25,17},{2,26},{10... | collective-permute-start | bytes 589832 | tf_op jit(solution)/shard_map/qkv/ppermute | solution.py:28
  74.8 149.9 %all-gather.3.cloned.1.call-start = ((), (), s32[]{:S(2)}) async-start(), calls=%async_computation.6 | async-start | bytes 1966080 | tf_op jit(solution)/shard_map/activated/all_gather | solution.py:722
  74.8 22.3 %collective-permute-start.16 = (bf16[768,128]{1,0:T(8,128)(2,1)S(1)}, bf16[768,128]{1,0:T(8,128)(2,1)S(1)}, u32[]{:S(2)}, u32[]{:S(2)}) collective-permute-start(bf16[768,128]{1,0:T(8,128)(2,1)S(1)} %queries.1.rest_0_.q_ref), channel_id=1, source_target_pairs={{0,8},{8,16},{16,24},{24,0},{1,9},{9,17},{17,25},{25,1},{2,10},{10... | collective-permute-start | bytes 589832 | tf_op jit(solution)/shard_map/queries/ppermute | solution.py:28
  89.9 18.8 %collective-permute-start.17 = (bf16[768,128]{1,0:T(8,128)(2,1)S(1)}, bf16[768,128]{1,0:T(8,128)(2,1)S(1)}, u32[]{:S(2)}, u32[]{:S(2)}) collective-permute-start(bf16[768,128]{1,0:T(8,128)(2,1)S(1)} %queries.1.rest_0_.q_ref), channel_id=1, source_target_pairs={{0,16},{8,24},{16,0},{24,8},{1,17},{9,25},{17,1},{25,9},{2,18},{10... | collective-permute-start | bytes 589832 | tf_op jit(solution)/shard_map/queries/ppermute | solution.py:28
  91.7 18.4 %collective-permute-start.18 = (bf16[768,128]{1,0:T(8,128)(2,1)S(1)}, bf16[768,128]{1,0:T(8,128)(2,1)S(1)}, u32[]{:S(2)}, u32[]{:S(2)}) collective-permute-start(bf16[768,128]{1,0:T(8,128)(2,1)S(1)} %queries.1.rest_0_.q_ref), channel_id=1, source_target_pairs={{0,24},{8,0},{16,8},{24,16},{1,25},{9,1},{17,9},{25,17},{2,26},{10... | collective-permute-start | bytes 589832 | tf_op jit(solution)/shard_map/queries/ppermute | solution.py:28
  131.4 25.9 %collective-permute-start.19 = (bf16[816,128]{1,0:T(8,128)(2,1)S(1)}, bf16[816,128]{1,0:T(8,128)(2,1)S(1)}, u32[]{:S(2)}, u32[]{:S(2)}) collective-permute-start(bf16[816,128]{1,0:T(8,128)(2,1)S(1)} %get-tuple-element.31), channel_id=1, source_target_pairs={{0,8},{8,16},{16,24},{24,0},{1,9},{9,17},{17,25},{25,1},{2,10},{10... | collective-permute-start | bytes 626696 | tf_op jit(solution)/shard_map/pages/ppermute | solution.py:28
  147.3 19.5 %collective-permute-start.20 = (bf16[816,128]{1,0:T(8,128)(2,1)S(1)}, bf16[816,128]{1,0:T(8,128)(2,1)S(1)}, u32[]{:S(2)}, u32[]{:S(2)}) collective-permute-start(bf16[816,128]{1,0:T(8,128)(2,1)S(1)} %get-tuple-element.32), channel_id=1, source_target_pairs={{0,16},{8,24},{16,0},{24,8},{1,17},{9,25},{17,1},{25,9},{2,18},{10... | collective-permute-start | bytes 626696 | tf_op jit(solution)/shard_map/pages/ppermute | solution.py:28
  147.3 19.5 %collective-permute-start.21 = (bf16[816,128]{1,0:T(8,128)(2,1)S(1)}, bf16[816,128]{1,0:T(8,128)(2,1)S(1)}, u32[]{:S(2)}, u32[]{:S(2)}) collective-permute-start(bf16[816,128]{1,0:T(8,128)(2,1)S(1)} %get-tuple-element.33), channel_id=1, source_target_pairs={{0,24},{8,0},{16,8},{24,16},{1,25},{9,1},{17,9},{25,17},{2,26},{10... | collective-permute-start | bytes 626696 | tf_op jit(solution)/shard_map/pages/ppermute | solution.py:28
  171.6 88.0 %all-gather.5.cloned.1.call-start = ((), (), s32[]{:S(2)}) async-start(), calls=%async_computation.7 | async-start | bytes 1966080 | tf_op jit(solution)/shard_map/activated/all_gather | solution.py:722
  172.1 119.3 %reduce-scatter.9.cloned.1.call-start = ((), (), s32[]{:S(2)}) async-start(), calls=%async_computation.8 | async-start | bytes 1597440 | tf_op jit(solution)/shard_map/next_0/reduce_scatter | solution.py:733
  172.2 15.1 %collective-permute-start.22 = (bf16[192,512]{1,0:T(8,128)(2,1)S(1)}, bf16[192,512]{1,0:T(8,128)(2,1)S(1)}, u32[]{:S(2)}, u32[]{:S(2)}) collective-permute-start(bf16[192,512]{1,0:T(8,128)(2,1)S(1)} %merge.3.refs_0_), channel_id=1, source_target_pairs={{0,8},{8,16},{16,24},{1,9},{9,17},{17,25},{2,10},{10,18},{18,26},{... | collective-permute-start | bytes 589832 | tf_op jit(solution)/shard_map/merge/ppermute | solution.py:65
  182.4 16.1 %collective-permute-start.25 = (bf16[192,512]{1,0:T(8,128)(2,1)S(1)}, bf16[192,512]{1,0:T(8,128)(2,1)S(1)}, u32[]{:S(2)}, u32[]{:S(2)}) collective-permute-start(bf16[192,512]{1,0:T(8,128)(2,1)S(1)} %merge.3.refs_0_), channel_id=1, source_target_pairs={{8,0},{16,8},{24,16},{9,1},{17,9},{25,17},{10,2},{18,10},{26,18},{... | collective-permute-start | bytes 589832 | tf_op jit(solution)/shard_map/merge/ppermute | solution.py:66
  187.2 12.6 %collective-permute-start.23 = (bf16[192,512]{1,0:T(8,128)(2,1)S(1)}, bf16[192,512]{1,0:T(8,128)(2,1)S(1)}, u32[]{:S(2)}, u32[]{:S(2)}) collective-permute-start(bf16[192,512]{1,0:T(8,128)(2,1)S(1)} %collective-permute-done.22.refs_1_), channel_id=1, source_target_pairs={{8,16},{16,24},{9,17},{17,25},{10,18},{18,26},{11,19},{19,27},{12,... | collective-permute-start | bytes 589832 | tf_op jit(solution)/shard_map/merge/ppermute | solution.py:65
  198.5 16.6 %collective-permute-start.26 = (bf16[192,512]{1,0:T(8,128)(2,1)S(1)}, bf16[192,512]{1,0:T(8,128)(2,1)S(1)}, u32[]{:S(2)}, u32[]{:S(2)}) collective-permute-start(bf16[192,512]{1,0:T(8,128)(2,1)S(1)} %collective-permute-done.25.refs_4_), channel_id=1, source_target_pairs={{8,0},{16,8},{9,1},{17,9},{10,2},{18,10},{11,3},{19,11},{12,4},{20... | collective-permute-start | bytes 589832 | tf_op jit(solution)/shard_map/merge/ppermute | solution.py:66
  199.8 16.7 %collective-permute-start.24 = (bf16[192,512]{1,0:T(8,128)(2,1)S(1)}, bf16[192,512]{1,0:T(8,128)(2,1)S(1)}, u32[]{:S(2)}, u32[]{:S(2)}) collective-permute-start(bf16[192,512]{1,0:T(8,128)(2,1)S(1)} %collective-permute-done.23.refs_2_), channel_id=1, source_target_pairs={{16,24},{17,25},{18,26},{19,27},{20,28},{21,29},{22,30},{23,31}} | collective-permute-start | bytes 589832 | tf_op jit(solution)/shard_map/merge/ppermute | solution.py:65
  215.1 9.5 %collective-permute-start.27 = (bf16[192,512]{1,0:T(8,128)(2,1)S(1)}, bf16[192,512]{1,0:T(8,128)(2,1)S(1)}, u32[]{:S(2)}, u32[]{:S(2)}) collective-permute-start(bf16[192,512]{1,0:T(8,128)(2,1)S(1)} %collective-permute-done.26.refs_5_), channel_id=1, source_target_pairs={{8,0},{9,1},{10,2},{11,3},{12,4},{13,5},{14,6},{15,7}} | collective-permute-start | bytes 589832 | tf_op jit(solution)/shard_map/merge/ppermute | solution.py:66
  232.4 5.8 %collective-permute-start.30 = (bf16[48,1024]{1,0:T(8,128)(2,1)S(1)}, bf16[48,1024]{1,0:T(8,128)(2,1)S(1)}, u32[]{:S(2)}, u32[]{:S(2)}) collective-permute-start(bf16[48,1024]{1,0:T(8,128)(2,1)S(1)} %get-tuple-element.50), channel_id=1, source_target_pairs={{0,4},{1,5},{2,6},{3,7},{4,0},{5,1},{6,2},{7,3},{8,12},{9,13},{10,... | collective-permute-start | bytes 294920 | tf_op jit(solution)/shard_map/down_0/ppermute | solution.py:32
  254.0 69.2 %reduce-scatter.11.cloned.1.call-start = ((), (), s32[]{:S(2)}) async-start(), calls=%async_computation.9 | async-start | bytes 1597440 | tf_op jit(solution)/shard_map/next_1/reduce_scatter | solution.py:733
  (34 other events, 253.2 us)
Sparse Core Ops, SparseCore 0:
  34.5 47.8 reduce-scatter.6
  84.7 79.3 reduce-scatter.4
  171.7 51.4 all-gather.2
  224.5 34.9 all-gather.4
  261.7 29.6 reduce-scatter.8
  293.7 29.4 reduce-scatter.10
